TPU v7x, 32 devices: a whole 2x2x4 slice. The times are simulated.
32 devices in a mesh: dp: 16 (over z, x, core), seq: 2 (over y).
Axes of the slice: x: 2, y: 2, z: 4, core: 2. Of those that a mesh axis runs over, the one named last changes fastest.
Arguments:
- tokens: float32 [32, 1024, 256], P('dp', 'seq'), may hold values from -6 to 6
- masked: int32 [32, 1024], P('dp', 'seq'), may hold values from 0 to 1
- lengths: int32 [32], P('dp'), may hold values from 256 to 1024, as said below
- cotangent: float32 [32, 1024, 256], P('dp', 'seq'), may hold values from -6 to 6
- mask_embed: float32 [256], replicated, may hold values from -4 to 4
- query_weight: float32 [256, 256], replicated, may hold values from -0.5 to 0.5
- query_bias: float32 [256], replicated, may hold values from -1.2 to 1.2
- key_weight: float32 [256, 256], replicated, may hold values from -0.5 to 0.5
- value_weight: float32 [256, 256], replicated, may hold values from -0.375 to 0.375
- value_bias: float32 [256], replicated, may hold values from -1.2 to 1.2
- out_weight: float32 [256, 256], replicated, may hold values from -1 to 1
- out_bias: float32 [256], replicated, may hold values from -3 to 3
- gain_one: float32 [256], replicated, may hold values from 0.1 to 1.9
- shift_one: float32 [256], replicated, may hold values from -3 to 3
- expand_weight: float32 [256, 512], replicated, may hold values from -0.375 to 0.375
- expand_bias: float32 [512], replicated, may hold values from -1.2 to 1.2
- reduce_weight: float32 [512, 256], replicated, may hold values from -0.25 to 0.25
- reduce_bias: float32 [256], replicated, may hold values from -3 to 3
- gain_two: float32 [256], replicated, may hold values from 0.1 to 1.9
- shift_two: float32 [256], replicated, may hold values from -3 to 3
Outputs:
- result: float32 [32, 1024, 256], P('dp', 'seq')
- tokens_grad: float32 [32, 1024, 256], P('dp', 'seq')
- mask_embed_grad: float32 [256], replicated
- query_weight_grad: float32 [256, 256], replicated
- query_bias_grad: float32 [256], replicated
- key_weight_grad: float32 [256, 256], replicated
- value_weight_grad: float32 [256, 256], replicated
- value_bias_grad: float32 [256], replicated
- out_weight_grad: float32 [256, 256], replicated
- out_bias_grad: float32 [256], replicated
- gain_one_grad: float32 [256], replicated
- shift_one_grad: float32 [256], replicated
- expand_weight_grad: float32 [256, 512], replicated
- expand_bias_grad: float32 [512], replicated
- reduce_weight_grad: float32 [512, 256], replicated
- reduce_bias_grad: float32 [256], replicated
- gain_two_grad: float32 [256], replicated
- shift_two_grad: float32 [256], replicated
- root_means: float32 [3], replicated
Inputs may be any that keep to these rules, and one draw needn't show every extreme that they name: `lengths`: in each group of 2 consecutive cells one cell is valid over all 1024 positions.
All inputs are finite; a program needn't handle non-finite values.
Results may differ from a plain program's by a relative error of at most 0.014.
The roundings to bfloat16 on the way count: a program that leaves them out, or rounds other values in their place, can miss the bound.
Values may be sent and summed in bfloat16 or wider, within the bound.
No kernel may reach another device: no remote copies, remote signals or barrier semaphores. Data moves between devices by JAX's collectives and lax.ppermute only.
A program may use at most 192 MiB of HBM per device.

v0:
```python
import jax
import jax.numpy as jnp
from jax import lax
from jax.sharding import PartitionSpec as P

HEADS = 4
HEAD_DIM = 64


EPSILON = 1e-05
NEGATIVE = -1e30
HIGH = lax.Precision.HIGHEST


def shifted(block, axis, distance):
    devices = range(lax.axis_size(axis))
    route = [((i - distance) % len(devices), i) for i in devices]
    return lax.ppermute(block, axis, route)


def layer_norm(matrix, gain_vec, offset_vec):
    row_mean = jnp.mean(matrix, axis=-1, keepdims=True)
    centred = matrix - row_mean
    row_var = jnp.mean(centred * centred, axis=-1, keepdims=True)
    return centred * lax.rsqrt(row_var + EPSILON) * gain_vec + offset_vec


def gelu_fn(matrix):
    return 0.5 * matrix * (1.0 + lax.erf(matrix * 0.7071067811865476))


def key_valid(lengths, offset, count):
    places = offset + jnp.arange(count, dtype=jnp.int32)
    return places[None, :] < lengths[:, None]


def split_heads(matrix):
    return matrix.reshape(matrix.shape[0], matrix.shape[1], HEADS, HEAD_DIM)


def scores_of(queries, key_heads, usable):
    raw_scores = jnp.einsum(
        "cqhe,ckhe->cqhk", queries, key_heads, preferred_element_type=jnp.float32
    )
    return jnp.where(usable[:, None, None, :], raw_scores * HEAD_DIM ** (-0.5), NEGATIVE)


def fold_keys(carried, shards, offset, queries, lengths):
    running_max, running_sum, partial_out = carried
    key_heads = split_heads(shards[0])
    value_heads = split_heads(shards[1])
    usable = key_valid(lengths, offset, key_heads.shape[1])
    scores = scores_of(queries, key_heads, usable)
    new_max = jnp.maximum(running_max, jnp.max(scores, axis=3))
    exp_scores = jnp.where(usable[:, None, None, :], jnp.exp(scores - new_max[..., None]), 0.0)
    running_sum = jnp.sum(exp_scores, axis=3)
    partial_out = jnp.einsum(
        "cqhk,ckhe->cqhe", exp_scores, value_heads.astype(jnp.float32), precision=HIGH
    )
    return (new_max, running_sum, partial_out)


def block_grads(queries, grad_heads, log_total, row_dot, key_block, value_block, usable):
    key_heads = split_heads(key_block)
    value_heads = split_heads(value_block)
    scores = scores_of(queries, key_heads, usable)
    soft_weights = jnp.where(usable[:, None, None, :], jnp.exp(scores - log_total[..., None]), 0.0)
    weight_grad = jnp.einsum(
        "cqhe,ckhe->cqhk", grad_heads, value_heads, preferred_element_type=jnp.float32
    )
    score_grad = (soft_weights * (weight_grad - row_dot[..., None])).astype(jnp.bfloat16)
    query_part = jnp.einsum(
        "cqhk,ckhe->cqhe", score_grad, key_heads, preferred_element_type=jnp.float32
    ) * HEAD_DIM ** (-0.5)
    key_part = jnp.einsum(
        "cqhk,cqhe->ckhe", score_grad, queries, preferred_element_type=jnp.float32
    ) * HEAD_DIM ** (-0.5)
    value_part = jnp.einsum(
        "cqhk,cqhe->ckhe", soft_weights, grad_heads.astype(jnp.float32), precision=HIGH
    )
    cell_count, key_rows = (key_block.shape[0], key_block.shape[1])
    return (
        query_part,
        key_part.reshape(cell_count, key_rows, -1),
        value_part.reshape(cell_count, key_rows, -1),
    )


def body(
    tokens,
    masked,
    lengths,
    cotangent,
    mask_embed,
    query_weight,
    query_bias,
    key_weight,
    value_weight,
    value_bias,
    out_weight,
    out_bias,
    gain_one,
    shift_one,
    expand_weight,
    expand_bias,
    reduce_weight,
    reduce_bias,
    gain_two,
    shift_two,
):
    cell_count, block_rows, model_width = tokens.shape
    cycle_size = lax.axis_size("seq")
    my_index = lax.axis_index("seq")
    usable_rows = key_valid(lengths, my_index * block_rows, block_rows)
    is_masked = masked[:, :, None] == 1
    stream = jnp.where(is_masked, mask_embed, tokens)
    residual_reduced = stream.astype(jnp.bfloat16)
    joined_weight = jnp.concatenate([query_weight, key_weight, value_weight], axis=1).astype(
        jnp.bfloat16
    )
    joined_bias = jnp.concatenate([query_bias, jnp.zeros_like(query_bias), value_bias])
    projected = (
        jnp.dot(residual_reduced, joined_weight, preferred_element_type=jnp.float32) + joined_bias
    ).astype(jnp.bfloat16)
    queries = split_heads(projected[:, :, :model_width])
    key_local = projected[:, :, model_width : 2 * model_width]
    value_local = projected[:, :, 2 * model_width :]
    start_state = (
        jnp.full((cell_count, block_rows, HEADS), NEGATIVE, jnp.float32),
        jnp.zeros((cell_count, block_rows, HEADS), jnp.float32),
        jnp.zeros((cell_count, block_rows, HEADS, HEAD_DIM), jnp.float32),
    )
    carried = fold_keys(
        start_state,
        (
            lax.all_gather(key_local, "seq", axis=1, tiled=True),
            lax.all_gather(value_local, "seq", axis=1, tiled=True),
        ),
        jnp.int32(0),
        queries,
        lengths,
    )
    running_max, running_sum, partial_out = carried
    attended = partial_out / running_sum[..., None]
    log_total = running_max + jnp.log(running_sum)
    attended_reduced = attended.reshape(cell_count, block_rows, model_width).astype(jnp.bfloat16)
    out_low = out_weight.astype(jnp.bfloat16)
    attn_out = jnp.dot(attended_reduced, out_low, preferred_element_type=jnp.float32) + out_bias
    normed_one, first_back = jax.vjp(layer_norm, stream + attn_out, gain_one, shift_one)
    normed_reduced = normed_one.astype(jnp.bfloat16)
    expand_low = expand_weight.astype(jnp.bfloat16)
    hidden_pre = (
        jnp.dot(normed_reduced, expand_low, preferred_element_type=jnp.float32) + expand_bias
    )
    activated, gelu_back = jax.vjp(gelu_fn, hidden_pre)
    activated_reduced = activated.astype(jnp.bfloat16)
    reduce_low = reduce_weight.astype(jnp.bfloat16)
    branch = (
        jnp.dot(activated_reduced, reduce_low, preferred_element_type=jnp.float32) + reduce_bias
    )
    result, second_back = jax.vjp(layer_norm, normed_one + branch, gain_two, shift_two)
    valid_float = usable_rows.astype(jnp.float32)
    valid_rows = valid_float[:, :, None]
    grad_result = cotangent * valid_rows
    grad_second, gain_two_grad, shift_two_grad = second_back(grad_result)
    branch_gradient = grad_second.astype(jnp.bfloat16)
    reduce_bias_grad = jnp.sum(branch_gradient.astype(jnp.float32), axis=(0, 1))
    reduce_weight_grad = jnp.einsum(
        "lwi,lwp->ip", activated_reduced, branch_gradient, preferred_element_type=jnp.float32
    )
    activated_grad = jnp.dot(branch_gradient, reduce_low.T, preferred_element_type=jnp.float32)
    hidden_gradient = gelu_back(activated_grad)[0].astype(jnp.bfloat16)
    expand_bias_grad = jnp.sum(hidden_gradient.astype(jnp.float32), axis=(0, 1))
    expand_weight_grad = jnp.einsum(
        "uhk,uhw->kw", normed_reduced, hidden_gradient, preferred_element_type=jnp.float32
    )
    grad_normed = grad_second + jnp.dot(
        hidden_gradient, expand_low.T, preferred_element_type=jnp.float32
    )
    grad_first, gain_one_grad, shift_one_grad = first_back(grad_normed)
    attention_gradient = grad_first.astype(jnp.bfloat16)
    out_bias_grad = jnp.sum(attention_gradient.astype(jnp.float32), axis=(0, 1))
    out_weight_grad = jnp.einsum(
        "uhk,uhw->kw", attended_reduced, attention_gradient, preferred_element_type=jnp.float32
    )
    grad_heads = split_heads(
        jnp.dot(attention_gradient, out_low.T, preferred_element_type=jnp.float32).astype(
            jnp.bfloat16
        )
    )
    row_dot = jnp.sum(grad_heads.astype(jnp.float32) * attended, axis=3)

    def grads_for(key_block, value_block, offset):
        usable = key_valid(lengths, offset, key_block.shape[1])
        return block_grads(queries, grad_heads, log_total, row_dot, key_block, value_block, usable)

    zero_query = jnp.zeros((cell_count, block_rows, HEADS, HEAD_DIM), jnp.float32)
    zero_keys = jnp.zeros((cell_count, block_rows, model_width), jnp.float32)

    def cycle_grads(cycle_step, query_acc, key_block, value_block, moving):
        anchor = (my_index - cycle_step) % cycle_size
        query_part, key_part, value_part = grads_for(key_block, value_block, anchor * block_rows)
        moving = (
            shifted((moving[0] + key_part).astype(jnp.bfloat16), "seq", 1).astype(jnp.float32),
            shifted((moving[1] + value_part).astype(jnp.bfloat16), "seq", 1).astype(jnp.float32),
        )
        return (query_acc + query_part, moving)

    def cycle_turn(cycle_step, carried):
        query_acc, key_block, value_block, moving = carried
        query_acc, moving = cycle_grads(cycle_step, query_acc, key_block, value_block, moving)
        key_block, value_block = shifted((key_block, value_block), "seq", 1)
        return (query_acc, key_block, value_block, moving)

    query_acc, key_block, value_block, moving = lax.fori_loop(
        0, cycle_size - 1, cycle_turn, (zero_query, key_local, value_local, (zero_keys, zero_keys))
    )
    query_acc, moving = cycle_grads(cycle_size - 1, query_acc, key_block, value_block, moving)
    key_grad, value_grad = moving
    joined_gradient = jnp.concatenate(
        [query_acc.reshape(cell_count, block_rows, model_width), key_grad, value_grad], axis=2
    ).astype(jnp.bfloat16)
    joined_weight_grad = jnp.einsum(
        "uhk,uhw->kw", residual_reduced, joined_gradient, preferred_element_type=jnp.float32
    )
    joined_bias_grad = jnp.sum(joined_gradient.astype(jnp.float32), axis=(0, 1))
    stream_grad = grad_first + jnp.dot(
        joined_gradient, joined_weight.T, preferred_element_type=jnp.float32
    )
    tokens_grad = jnp.where(is_masked, 0.0, stream_grad)
    mask_embed_grad = jnp.sum(jnp.where(is_masked, stream_grad, 0.0), axis=(0, 1))
    square_sums = jnp.stack(
        [
            jnp.sum(stream * stream * valid_rows),
            jnp.sum(attn_out * attn_out * valid_rows),
            jnp.sum(branch * branch * valid_rows),
        ]
    )
    valid_count = jnp.sum(valid_float)
    summed = lax.psum(
        (
            mask_embed_grad,
            joined_weight_grad,
            joined_bias_grad[:model_width],
            joined_bias_grad[2 * model_width :],
            out_weight_grad,
            out_bias_grad,
            gain_one_grad,
            shift_one_grad,
            expand_weight_grad,
            expand_bias_grad,
            reduce_weight_grad,
            reduce_bias_grad,
            gain_two_grad,
            shift_two_grad,
            square_sums,
            valid_count,
        ),
        ("dp", "seq"),
    )
    joined_total = summed[1]
    root_means = jnp.sqrt(summed[14] / (summed[15] * model_width))
    return (
        result,
        tokens_grad,
        summed[0],
        joined_total[:, :model_width],
        summed[2],
        joined_total[:, model_width : 2 * model_width],
        joined_total[:, 2 * model_width :],
        summed[3],
        summed[4],
        summed[5],
        summed[6],
        summed[7],
        summed[8],
        summed[9],
        summed[10],
        summed[11],
        summed[12],
        summed[13],
        root_means,
    )


def solution(mesh):
    placed = (
        P("dp", "seq", None),
        P("dp", "seq"),
        P("dp"),
        P("dp", "seq", None),
        P(),
        P(),
        P(),
        P(),
        P(),
        P(),
        P(),
        P(),
        P(),
        P(),
        P(),
        P(),
        P(),
        P(),
        P(),
        P(),
    )
    return jax.shard_map(
        body,
        mesh=mesh,
        in_specs=placed,
        out_specs=(
            P("dp", "seq", None),
            P("dp", "seq", None),
            P(),
            P(),
            P(),
            P(),
            P(),
            P(),
            P(),
            P(),
            P(),
            P(),
            P(),
            P(),
            P(),
            P(),
            P(),
            P(),
            P(),
        ),
        check_vma=False,
    )
```

profile of v0, /device:TPU:0, one launch (start us, length us, event | category | flops | bytes accessed | tf_op | source)
XLA Modules:
  0.0 332.3 jit_solution(14456772306723635265)
XLA Ops:
  7.2 1.6 copy.80
  13.2 1.4 add_convert_fusion
  15.5 3.0 collective-permute-start
  20.3 4.6 %fusion.87 = f32[2,4,512,512]{3,2,1,0:T(8,128)} fusion(bf16[2,512,4,64]{1,3,2,0:T(8,128)(2,1)S(1)} %bitcast.164, bf16[2,512,4,64]{1,3,2,0:T(8,128)(2,1)S(1)} %bitcast.153), kind=kOutput, calls=%fused_computation.148 | convolution fusion | flops 268435456 | bytes 9437184 | tf_op jit(solution)/shard_map/while/body/eval_jaxpr/cqhe,ckhe->cqhk/dot_general | solution.py:42
  26.6 1.6 copy.90
  28.2 8.0 %collective-permute-done = bf16[2,512,256]{2,1,0:T(8,128)(2,1)} collective-permute-done((bf16[2,512,256]{2,1,0:T(8,128)(2,1)}, bf16[2,512,256]{2,1,0:T(8,128)(2,1)}, u32[]{:S(2)}, u32[]{:S(2)}) %collective-permute-start) | collective-permute-done | bytes 524320 | tf_op jit(solution)/shard_map/while/body/eval_jaxpr/ppermute | solution.py:18
  37.5 4.5 %fusion.89 = f32[2,4,512,512]{3,2,1,0:T(8,128)} fusion(bf16[2,512,4,64]{1,3,2,0:T(8,128)(2,1)S(1)} %bitcast.162, bf16[2,512,4,64]{1,3,2,0:T(8,128)(2,1)S(1)} %bitcast.154), kind=kOutput, calls=%fused_computation.150 | convolution fusion | flops 268435456 | bytes 9437184 | tf_op jit(solution)/shard_map/cqhe,ckhe->cqhk/dot_general | solution.py:42
  42.0 11.3 %collective-permute-done.1 = bf16[2,512,256]{2,1,0:T(8,128)(2,1)} collective-permute-done((bf16[2,512,256]{2,1,0:T(8,128)(2,1)S(1)}, bf16[2,512,256]{2,1,0:T(8,128)(2,1)}, u32[]{:S(2)}, u32[]{:S(2)}) %collective-permute-start.1) | collective-permute-done | bytes 524320 | tf_op jit(solution)/shard_map/while/body/eval_jaxpr/ppermute | solution.py:18
  53.3 2.1 copy.98
  55.3 2.0 copy.83
  57.3 4.1 %bitcast_reduce_fusion = (f32[2,512,4]{1,2,0:T(4,128)S(1)}, f32[2,4,1024,512]{3,2,1,0:T(8,128)S(1)}) fusion(pred[2,1024]{1,0:T(4,128)(4,1)S(1)} %iota_compare_fusion, bf16[2,1024,4,64]{1,3,2,0:T(8,128)(2,1)S(1)} %bitcast.166, bf16[2,512,4,64]{1,3,2,0:T(8,128)(2,1)S(1)} %bitcast.155), kind=kOutput, calls=%fused_computation.1 | convolution fusion | flops 549449728 | bytes 18368512 | tf_op jit(solution)/shard_map/cqhe,ckhe->cqhk/dot_general | solution.py:42
  61.5 4.7 %fusion.2 = f32[2,512,4]{1,2,0:T(4,128)S(1)} fusion(f32[2,4,1024,512]{3,2,1,0:T(8,128)S(1)} %get-tuple-element.151, f32[2,512,4]{1,2,0:T(4,128)S(1)} %broadcast_maximum_fusion, pred[2,1024]{1,0:T(4,128)(4,1)S(1)} %iota_compare_fusion), kind=kLoop, calls=%fused_computation.5 | loop fusion | flops 20967424 | bytes 16812032 | tf_op jit(solution)/shard_map/reduce_sum | solution.py:56
  68.2 6.3 %all-gather.3.cloned.1.call-done = bf16[2,1024,256]{2,1,0:T(8,128)(2,1)} async-done(((bf16[2,512,256]{2,1,0:T(8,128)(2,1)}), bf16[2,1024,256]{2,1,0:T(8,128)(2,1)}) %all-gather.3.cloned.1.call-update) | async-done | bytes 1048592 | tf_op jit(solution)/shard_map/all_gather | solution.py:137
  74.5 1.5 copy.82
  76.0 13.9 %fusion.86 = (bf16[2,512,4,64]{1,3,2,0:T(8,128)(2,1)S(1)}, f32[2,512,4,64]{1,3,2,0:T(8,128)S(1)}) fusion(f32[2,512,4]{1,2,0:T(4,128)} %copy-done.35, bf16[2,1024,4,64]{1,3,2,0:T(8,128)(2,1)S(1)} %bitcast.173, f32[2,4,1024,512]{3,2,1,0:T(8,128)} %copy-done, f32[2,512,4]{1,2,0:T(4,128)} %copy-done.36, pred[2,1024]{1,0:T(4,128)(4,1)S(1)} %iota_compare_fusion), kind=kOutput, calls=%fused_computation.147 | convolution fusion | flops 3238526976 | bytes 19433472 | tf_op jit(solution)/shard_map/cqhk,ckhe->cqhe/dot_general | solution.py:57
  93.7 1.5 multiply_reduce_fusion.2
  95.2 1.5 fusion.79
  97.4 2.0 convert_reduce_fusion.1
  99.5 1.4 multiply_reduce_fusion.4
  103.9 6.9 %fusion.41 = bf16[2,4,64,512]{3,2,1,0:T(8,128)(2,1)S(1)} fusion(bf16[2,512,4,64]{1,3,2,0:T(8,128)(2,1)S(1)} %bitcast.177, f32[2,4,512,512]{3,2,1,0:T(8,128)S(1)} %bitcast.159, f32[2,512,4]{1,2,0:T(4,128)S(1)} %copy-done.40, pred[2,512]{1,0:T(4,128)(4,1)S(1)} %copy-done.54), kind=kOutput, calls=%fused_computation.60 | convolution fusion | flops 1619263488 | bytes 9454592 | tf_op jit(solution)/shard_map/while/body/eval_jaxpr/cqhk,cqhe->ckhe/dot_general | solution.py:78
  112.1 11.0 %fusion.21 = f32[2,4,64,512]{3,2,1,0:T(8,128)} fusion(bf16[2,512,4,64]{1,3,2,0:T(8,128)(2,1)S(1)} %bitcast.178, f32[2,4,512,512]{3,2,1,0:T(8,128)} %fusion.89, f32[2,512,4]{1,2,0:T(4,128)} %log_add_fusion, pred[2,512]{1,0:T(4,128)(4,1)} %get-tuple-element.148), kind=kOutput, calls=%fused_computation.26 | convolution fusion | flops 1619001344 | bytes 9978880 | tf_op jit(solution)/shard_map/cqhk,cqhe->ckhe/dot_general | solution.py:78
  123.1 5.7 %fusion.6 = bf16[2,512,4,512]{1,3,2,0:T(8,128)(2,1)S(1)} fusion(f32[2,4,512,512]{3,2,1,0:T(8,128)} %fusion.89, f32[2,512,4]{1,2,0:T(4,128)S(1)} %copy-done.39, f32[2,512,4]{1,2,0:T(4,128)S(1)} %copy-done.41, pred[2,512]{1,0:T(4,128)(4,1)S(1)} %copy-done.56, bf16[2,512,4,64]{1,3,2,0:T(8,128)(2,1)S(1)} %bitcast.175, bf16[2,512,4,64]{1,3,2,0:T(8,128)(2,1)S(1)} %bitcast.179), kind=kOutput, calls=%fused_computation.9 | convolution fusion | flops 283115520 | bytes 13665280 | tf_op jit(solution)/shard_map/cqhe,ckhe->cqhk/dot_general | solution.py:68
  128.9 1.4 convolution_multiply_fusion
  130.9 3.7 %fusion.10 = bf16[2,512,4,512]{1,3,2,0:T(8,128)(2,1)S(1)} fusion(f32[2,4,512,512]{3,2,1,0:T(8,128)S(1)} %bitcast.161, f32[2,512,4]{1,2,0:T(4,128)S(1)} %copy-done.39, f32[2,512,4]{1,2,0:T(4,128)S(1)} %copy-done.41, pred[2,512]{1,0:T(4,128)(4,1)S(1)} %copy-done.55, bf16[2,512,4,64]{1,3,2,0:T(8,128)(2,1)S(1)} %bitcast.174, ...), kind=kOutput, calls=%fused_computation.15 | convolution fusion | flops 283115520 | bytes 13665280 | tf_op jit(solution)/shard_map/while/body/eval_jaxpr/cqhe,ckhe->cqhk/dot_general | solution.py:68
  134.6 1.8 fusion.88
  136.5 2.2 fusion.40
  138.6 2.7 copy.107
  141.3 1.4 copy.103
  143.7 1.7 collective-permute-start.2
  145.5 4.1 %fusion.39 = bf16[2,4,64,512]{3,2,1,0:T(8,128)(2,1)} fusion(f32[2,4,64,512]{3,2,1,0:T(8,128)} %fusion.88, bf16[2,512,4,64]{1,3,2,0:T(8,128)(2,1)S(1)} %bitcast.163, bf16[2,512,4,512]{1,3,2,0:T(8,128)(2,1)} %copy-done.1), kind=kOutput, calls=%fused_computation.57 | convolution fusion | flops 269221888 | bytes 6291456 | tf_op jit(solution)/shard_map/cqhk,ckhe->cqhe/dot_general | solution.py:72
  149.6 2.2 copy.108
  151.8 1.6 add_convert_fusion.2
  153.8 5.1 %collective-permute-done.2 = bf16[2,512,256]{2,1,0:T(8,128)(2,1)} collective-permute-done((bf16[2,512,256]{2,1,0:T(8,128)(2,1)}, bf16[2,512,256]{2,1,0:T(8,128)(2,1)}, u32[]{:S(2)}, u32[]{:S(2)}) %collective-permute-start.2) | collective-permute-done | bytes 524320 | tf_op jit(solution)/shard_map/while/body/eval_jaxpr/ppermute | solution.py:18
  158.9 1.5 add_convert_fusion.3
  160.4 1.8 collective-permute-start.3
  165.8 4.2 %collective-permute-done.5 = bf16[2,512,256]{2,1,0:T(8,128)(2,1)S(1)} collective-permute-done((bf16[2,512,256]{2,1,0:T(8,128)(2,1)S(1)}, bf16[2,512,256]{2,1,0:T(8,128)(2,1)S(1)}, u32[]{:S(2)}, u32[]{:S(2)}) %collective-permute-start.5) | collective-permute-done | bytes 524320 | tf_op jit(solution)/shard_map/ppermute | solution.py:18
  170.0 9.9 %collective-permute-done.3 = bf16[2,512,256]{2,1,0:T(8,128)(2,1)S(1)} collective-permute-done((bf16[2,512,256]{2,1,0:T(8,128)(2,1)S(1)}, bf16[2,512,256]{2,1,0:T(8,128)(2,1)S(1)}, u32[]{:S(2)}, u32[]{:S(2)}) %collective-permute-start.3) | collective-permute-done | bytes 524320 | tf_op jit(solution)/shard_map/ppermute | solution.py:18
  180.8 1.6 convolution_bitcast_fusion
  183.0 1.3 copy.113
  184.4 2.5 pad_maximum_fusion.2
  186.9 2.3 select_reduce_fusion
  190.6 1.3 convert_reduce_fusion
  191.9 41.0 %all-reduce = (f32[256]{0:T(256)}, f32[256]{0:T(256)}, f32[256]{0:T(256)}, f32[256]{0:T(256)}, f32[256]{0:T(256)}, /*index=5*/f32[256]{0:T(256)}, f32[512]{0:T(5...) all-reduce(f32[256]{0:T(256)} %get-tuple-element.140, ...), channel_id=1, replica_groups=mesh['dp'=16,'seq'=2] {'dp','seq'}, use_global_device_ids=true, to_apply=%region_12.13 | all-reduce | flops 2820 | bytes 22560 | tf_op jit(solution)/shard_map/psum | solution.py:240
  234.1 84.0 %all-reduce.4.cloned.1.call-done = (f32[256,768]{1,0:T(8,128)}, f32[256,256]{1,0:T(8,128)}, f32[256,512]{1,0:T(8,128)}, f32[512,256]{1,0:T(8,128)}) async-done(((f32[256,768]{1,0:T(8,128)}, f32[256,256]{1,0:T(8,128)}, f32[256,512]{1,0:T(8,128)}, f32[512,256]{1,0:T(8,128)}), (f32[256,768]{1,0:T(8,128)}, f32[256,256]{1,0:T(8,128)}, f32[256,512]{1,0:T(8,128)}, ...) | async-done | bytes 2097168 | tf_op jit(solution)/shard_map/psum | solution.py:240
  318.1 2.0 fusion.84
  320.1 1.7 copy.139
  321.7 1.9 copy.140
  323.6 1.9 copy.141
  (184 shorter events, 29.8 us)
Async XLA Ops:
  7.2 48.1 %all-gather.5.cloned.1.call-start = ((), (), s32[]{:S(2)}) async-start(), calls=%async_computation.1 | async-start | bytes 1572864 | tf_op jit(solution)/shard_map/all_gather | solution.py:136
  8.8 6.7 %copy-start.2 = (f32[2,512,256]{1,2,0:T(8,128)}, f32[2,512,256]{1,2,0:T(8,128)S(1)}, u32[]{:S(2)}) copy-start(f32[2,512,256]{1,2,0:T(8,128)S(1)} %copy.80) | copy-start | bytes 3145732
  15.5 59.0 %all-gather.3.cloned.1.call-start = ((), (), s32[]{:S(2)}) async-start(), calls=%async_computation | async-start | bytes 1572864 | tf_op jit(solution)/shard_map/all_gather | solution.py:137
  15.5 20.7 %collective-permute-start = (bf16[2,512,256]{2,1,0:T(8,128)(2,1)}, bf16[2,512,256]{2,1,0:T(8,128)(2,1)}, u32[]{:S(2)}, u32[]{:S(2)}) collective-permute-start(bf16[2,512,256]{2,1,0:T(8,128)(2,1)} %get-tuple-element.137), channel_id=1, source_target_pairs={{1,0},{0,1},{3,2},{2,3},{5,4},{4,5},{7,6},{6,7},{9,8},{8,9},{11,10... | collective-permute-start | bytes 1572872 | tf_op jit(solution)/shard_map/while/body/eval_jaxpr/ppermute | solution.py:18
  18.6 34.7 %collective-permute-start.1 = (bf16[2,512,256]{2,1,0:T(8,128)(2,1)S(1)}, bf16[2,512,256]{2,1,0:T(8,128)(2,1)}, u32[]{:S(2)}, u32[]{:S(2)}) collective-permute-start(bf16[2,512,256]{2,1,0:T(8,128)(2,1)S(1)} %get-tuple-element.138), channel_id=1, source_target_pairs={{1,0},{0,1},{3,2},{2,3},{5,4},{4,5},{7,6},{6,7},{9,8},{8,9},{11,10... | collective-permute-start | bytes 1572872 | tf_op jit(solution)/shard_map/while/body/eval_jaxpr/ppermute | solution.py:18
  18.7 299.4 %all-reduce.4.cloned.1.call-start = ((), (), s32[]{:S(2)}) async-start(), calls=%async_computation.2 | async-start | bytes 4194304 | tf_op jit(solution)/shard_map/psum | solution.py:240
  20.0 4.8 %copy-start.9 = (bf16[2,512,256]{1,2,0:T(8,128)(2,1)}, bf16[2,512,256]{1,2,0:T(8,128)(2,1)S(1)}, u32[]{:S(2)}) copy-start(bf16[2,512,256]{1,2,0:T(8,128)(2,1)S(1)} %copy.93) | copy-start | bytes 1572868
  20.3 4.6 %copy-start.44 = (s32[2]{0:T(128)S(1)}, s32[2]{0:T(128)}, u32[]{:S(2)}) copy-start(s32[2]{0:T(128)} %param.22) | copy-start | bytes 28
  20.3 5.3 %copy-start.8 = (bf16[2,512,256]{2,1,0:T(8,128)(2,1)S(1)}, bf16[2,512,256]{2,1,0:T(8,128)(2,1)}, u32[]{:S(2)}) copy-start(bf16[2,512,256]{2,1,0:T(8,128)(2,1)} %copy-done.7) | copy-start | bytes 1572868
  24.9 17.1 %copy-start.37 = (s32[512]{0:T(512)}, s32[512]{0:T(512)S(1)}, u32[]{:S(2)}) copy-start(s32[512]{0:T(512)S(1)} %iota_add_fusion.2) | copy-start | bytes 6148
  61.4 5.7 %copy-start = (f32[2,4,1024,512]{3,2,1,0:T(8,128)}, f32[2,4,1024,512]{3,2,1,0:T(8,128)S(1)}, u32[]{:S(2)}) copy-start(f32[2,4,1024,512]{3,2,1,0:T(8,128)S(1)} %get-tuple-element.151) | copy-start | bytes 50331652
  61.4 6.1 %copy-start.36 = (f32[2,512,4]{1,2,0:T(4,128)}, f32[2,512,4]{1,2,0:T(4,128)S(1)}, u32[]{:S(2)}) copy-start(f32[2,512,4]{1,2,0:T(4,128)S(1)} %broadcast_maximum_fusion) | copy-start | bytes 49156
  75.9 14.0 %copy-start.3 = (f32[2,512,256]{1,2,0:T(8,128)S(1)}, f32[2,512,256]{1,2,0:T(8,128)}, u32[]{:S(2)}) copy-start(f32[2,512,256]{1,2,0:T(8,128)} %copy-done.2) | copy-start | bytes 3145732
  76.0 14.0 %copy-start.26 = (f32[256,256]{1,0:T(8,128)S(1)}, f32[256,256]{1,0:T(8,128)}, u32[]{:S(2)}) copy-start(f32[256,256]{1,0:T(8,128)} %param.30) | copy-start | bytes 786436
  76.0 14.0 %copy-start.49 = (f32[256]{0:T(256)S(1)}, f32[256]{0:T(256)}, u32[]{:S(2)}) copy-start(f32[256]{0:T(256)} %param.24) | copy-start | bytes 3076
  76.0 14.0 %copy-start.58 = (f32[256]{0:T(256)S(1)}, f32[256]{0:T(256)}, u32[]{:S(2)}) copy-start(f32[256]{0:T(256)} %param.31) | copy-start | bytes 3076
  97.4 6.4 %slice-start = ((s8[8388608]{0:T(1024)(128)(4,1)}), s8[4194304]{0:T(1024)(128)(4,1)S(1)}, s32[]{:S(2)}) async-start(s8[8388608]{0:T(1024)(128)(4,1)} %bitcast.158), calls=%async_computation.3 | async-start | bytes 8388608
  102.9 7.9 %copy-start.11 = (bf16[2,512,256]{1,2,0:T(8,128)(2,1)}, bf16[2,512,256]{1,2,0:T(8,128)(2,1)S(1)}, u32[]{:S(2)}) copy-start(bf16[2,512,256]{1,2,0:T(8,128)(2,1)S(1)} %get-tuple-element.127) | copy-start | bytes 1572868
  103.8 19.3 %copy-start.32 = (bf16[2,512,256]{1,2,0:T(8,128)(2,1)}, bf16[2,512,256]{1,2,0:T(8,128)(2,1)S(1)}, u32[]{:S(2)}) copy-start(bf16[2,512,256]{1,2,0:T(8,128)(2,1)S(1)} %get-tuple-element.160) | copy-start | bytes 1572868
  111.8 40.0 %collective-permute-start.4 = (bf16[2,512,256]{2,1,0:T(8,128)(2,1)}, bf16[2,512,256]{2,1,0:T(8,128)(2,1)}, u32[]{:S(2)}, u32[]{:S(2)}) collective-permute-start(bf16[2,512,256]{2,1,0:T(8,128)(2,1)} %copy.105), channel_id=1, source_target_pairs={{1,0},{0,1},{3,2},{2,3},{5,4},{4,5},{7,6},{6,7},{9,8},{8,9},{11,10... | collective-permute-start | bytes 1572872 | tf_op jit(solution)/shard_map/while/body/eval_jaxpr/ppermute | solution.py:18
  112.1 11.0 %copy-start.31 = (bf16[2,512,256]{1,2,0:T(8,128)(2,1)S(1)}, bf16[2,512,256]{1,2,0:T(8,128)(2,1)}, u32[]{:S(2)}) copy-start(bf16[2,512,256]{1,2,0:T(8,128)(2,1)} %copy.98) | copy-start | bytes 1572868
  112.1 11.0 %copy-start.39 = (f32[2,512,4]{1,2,0:T(4,128)S(1)}, f32[2,512,4]{1,2,0:T(4,128)}, u32[]{:S(2)}) copy-start(f32[2,512,4]{1,2,0:T(4,128)} %get-tuple-element.159) | copy-start | bytes 49156
  112.1 11.0 %copy-start.41 = (f32[2,512,4]{1,2,0:T(4,128)S(1)}, f32[2,512,4]{1,2,0:T(4,128)}, u32[]{:S(2)}) copy-start(f32[2,512,4]{1,2,0:T(4,128)} %log_add_fusion) | copy-start | bytes 49156
  112.1 11.0 %copy-start.56 = (pred[2,512]{1,0:T(4,128)(4,1)S(1)}, pred[2,512]{1,0:T(4,128)(4,1)}, u32[]{:S(2)}) copy-start(pred[2,512]{1,0:T(4,128)(4,1)} %get-tuple-element.148) | copy-start | bytes 3076
  112.1 18.8 %slice-start.2 = ((s8[8388608]{0:T(1024)(128)(4,1)}), s8[4194304]{0:T(1024)(128)(4,1)S(1)}, s32[]{:S(2)}) async-start(s8[8388608]{0:T(1024)(128)(4,1)} %bitcast.160), calls=%async_computation.5 | async-start | bytes 8388608
  123.1 7.7 %slice-start.3 = ((s8[8388608]{0:T(1024)(128)(4,1)}), s8[4194304]{0:T(1024)(128)(4,1)S(1)}, s32[]{:S(2)}) async-start(s8[8388608]{0:T(1024)(128)(4,1)} %bitcast.160), calls=%async_computation.6 | async-start | bytes 8388608
  143.7 15.1 %collective-permute-start.2 = (bf16[2,512,256]{2,1,0:T(8,128)(2,1)}, bf16[2,512,256]{2,1,0:T(8,128)(2,1)}, u32[]{:S(2)}, u32[]{:S(2)}) collective-permute-start(bf16[2,512,256]{2,1,0:T(8,128)(2,1)} %copy.101), channel_id=1, source_target_pairs={{1,0},{0,1},{3,2},{2,3},{5,4},{4,5},{7,6},{6,7},{9,8},{8,9},{11,10... | collective-permute-start | bytes 1572872 | tf_op jit(solution)/shard_map/while/body/eval_jaxpr/ppermute | solution.py:18
  149.6 12.6 %copy-start.12 = (bf16[2,512,256]{1,2,0:T(8,128)(2,1)S(1)}, bf16[2,512,256]{1,2,0:T(8,128)(2,1)}, u32[]{:S(2)}) copy-start(bf16[2,512,256]{1,2,0:T(8,128)(2,1)} %copy-done.11) | copy-start | bytes 1572868
  149.6 12.6 %copy-start.17 = (bf16[2,512,4,64]{1,3,2,0:T(8,128)(2,1)S(1)}, bf16[2,512,4,64]{1,3,2,0:T(8,128)(2,1)}, u32[]{:S(2)}) copy-start(bf16[2,512,4,64]{1,3,2,0:T(8,128)(2,1)} %copy-done.16) | copy-start | bytes 1572868
  149.6 13.6 %copy-start.6 = (bf16[2,512,512]{2,1,0:T(8,128)(2,1)S(1)}, bf16[2,512,512]{2,1,0:T(8,128)(2,1)}, u32[]{:S(2)}) copy-start(bf16[2,512,512]{2,1,0:T(8,128)(2,1)} %copy-done.5) | copy-start | bytes 3145732
  151.8 11.4 %copy-start.23 = (bf16[2,512,256]{1,2,0:T(8,128)(2,1)S(1)}, bf16[2,512,256]{1,2,0:T(8,128)(2,1)}, u32[]{:S(2)}) copy-start(bf16[2,512,256]{1,2,0:T(8,128)(2,1)} %copy-done.22) | copy-start | bytes 1572868
  151.8 12.7 %copy-start.25 = (bf16[2,512,512]{2,1,0:T(8,128)(2,1)S(1)}, bf16[2,512,512]{2,1,0:T(8,128)(2,1)}, u32[]{:S(2)}) copy-start(bf16[2,512,512]{2,1,0:T(8,128)(2,1)} %copy-done.24) | copy-start | bytes 3145732
  151.8 12.7 %copy-start.43 = (f32[256]{0:T(256)S(1)}, f32[256]{0:T(256)}, u32[]{:S(2)}) copy-start(f32[256]{0:T(256)} %param.32) | copy-start | bytes 3076
  151.8 12.7 %copy-start.52 = (f32[256]{0:T(256)S(1)}, f32[256]{0:T(256)}, u32[]{:S(2)}) copy-start(f32[256]{0:T(256)} %param.33) | copy-start | bytes 3076
  153.4 27.4 %copy-start.4 = (f32[2,512,256]{1,2,0:T(8,128)S(1)}, f32[2,512,256]{1,2,0:T(8,128)}, u32[]{:S(2)}) copy-start(f32[2,512,256]{1,2,0:T(8,128)} %copy-done.2) | copy-start | bytes 3145732
  153.4 27.4 %copy-start.18 = (bf16[2,512,256]{2,1,0:T(8,128)(2,1)S(1)}, bf16[2,512,256]{2,1,0:T(8,128)(2,1)}, u32[]{:S(2)}) copy-start(bf16[2,512,256]{2,1,0:T(8,128)(2,1)} %copy.108) | copy-start | bytes 1572868
  153.4 27.4 %copy-start.50 = (f32[256]{0:T(256)S(1)}, f32[256]{0:T(256)}, u32[]{:S(2)}) copy-start(f32[256]{0:T(256)} %param.24) | copy-start | bytes 3076
  153.4 16.6 %collective-permute-start.5 = (bf16[2,512,256]{2,1,0:T(8,128)(2,1)S(1)}, bf16[2,512,256]{2,1,0:T(8,128)(2,1)S(1)}, u32[]{:S(2)}, u32[]{:S(2)}) collective-permute-start(bf16[2,512,256]{2,1,0:T(8,128)(2,1)S(1)} %add_convert_fusion.2), channel_id=1, source_target_pairs={{1,0},{0,1},{3,2},{2,3},{5,4},{4,5},{7,6},{6,7},{9,8},{8,9},{11,10... | collective-permute-start | bytes 1572872 | tf_op jit(solution)/shard_map/ppermute | solution.py:18
  160.4 19.6 %collective-permute-start.3 = (bf16[2,512,256]{2,1,0:T(8,128)(2,1)S(1)}, bf16[2,512,256]{2,1,0:T(8,128)(2,1)S(1)}, u32[]{:S(2)}, u32[]{:S(2)}) collective-permute-start(bf16[2,512,256]{2,1,0:T(8,128)(2,1)S(1)} %add_convert_fusion.3), channel_id=1, source_target_pairs={{1,0},{0,1},{3,2},{2,3},{5,4},{4,5},{7,6},{6,7},{9,8},{8,9},{11,10... | collective-permute-start | bytes 1572872 | tf_op jit(solution)/shard_map/ppermute | solution.py:18
  165.8 16.6 %copy-start.38 = (s32[512]{0:T(512)S(1)}, s32[512]{0:T(512)}, u32[]{:S(2)}) copy-start(s32[512]{0:T(512)} %copy-done.37) | copy-start | bytes 6148
  165.8 16.6 %copy-start.45 = (s32[2]{0:T(128)S(1)}, s32[2]{0:T(128)}, u32[]{:S(2)}) copy-start(s32[2]{0:T(128)} %param.22) | copy-start | bytes 28
  165.8 17.3 %copy-start.13 = (f32[2,512,256]{1,2,0:T(8,128)S(1)}, f32[2,512,256]{1,2,0:T(8,128)}, u32[]{:S(2)}) copy-start(f32[2,512,256]{1,2,0:T(8,128)} %get-tuple-element.139) | copy-start | bytes 3145732
  165.8 21.1 %copy-start.15 = (f32[2,512,256]{1,2,0:T(8,128)S(1)}, f32[2,512,256]{1,2,0:T(8,128)}, u32[]{:S(2)}) copy-start(f32[2,512,256]{1,2,0:T(8,128)} %copy-done.14) | copy-start | bytes 3145732
  165.8 21.1 %copy-start.19 = (bf16[2,512,256]{2,1,0:T(8,128)(2,1)S(1)}, bf16[2,512,256]{2,1,0:T(8,128)(2,1)}, u32[]{:S(2)}) copy-start(bf16[2,512,256]{2,1,0:T(8,128)(2,1)} %copy.108) | copy-start | bytes 1572868
  170.0 10.0 %copy-start.27 = (bf16[2,512,256]{2,1,0:T(8,128)(2,1)}, bf16[2,512,256]{2,1,0:T(8,128)(2,1)S(1)}, u32[]{:S(2)}) copy-start(bf16[2,512,256]{2,1,0:T(8,128)(2,1)S(1)} %collective-permute-done.5) | copy-start | bytes 1572868
  182.3 4.6 %copy-start.28 = (bf16[2,512,256]{2,1,0:T(8,128)(2,1)S(1)}, bf16[2,512,256]{2,1,0:T(8,128)(2,1)}, u32[]{:S(2)}) copy-start(bf16[2,512,256]{2,1,0:T(8,128)(2,1)} %copy-done.27) | copy-start | bytes 1572868
  186.9 5.0 %copy-start.47 = (f32[256]{0:T(256)S(1)}, f32[256]{0:T(256)}, u32[]{:S(2)}) copy-start(f32[256]{0:T(256)} %get-tuple-element.105) | copy-start | bytes 3076
  186.9 5.0 %copy-start.48 = (f32[256]{0:T(256)S(1)}, f32[256]{0:T(256)}, u32[]{:S(2)}) copy-start(f32[256]{0:T(256)} %get-tuple-element.107) | copy-start | bytes 3076
  (25 other events, 55.3 us)
Sparse Core Ops, SparseCore 0:
  15.6 35.3 all-gather.4
  53.1 21.2 all-gather.2
  182.5 135.5 all-reduce.3
where the time goes:
time: 338 us; the launch traced here: 332 us
  waiting for transfers between devices  129 us (38%)
  matrix products  78.9 us (23%)
  blocking collectives  41 us (12%)
  local copies, waits for them, and re-layouts  37.1 us (11%)
  other arithmetic  23.5 us (7%)
  between operations  15.4 us (5%)
  starting transfers between devices  7.44 us (2%)
    psum x1, waiting for transfers between devices, body(): lax.psum((mask_embed_grad, joined_weight_grad, joined_bias_grad[:model_wi...  84 us
    psum x1, blocking collectives, body(): lax.psum((mask_embed_grad, joined_weight_grad, joined_bias_grad[:model_wi...  41 us
    ppermute x6, waiting for transfers between devices, shifted(): return lax.ppermute(block, axis, route)  38.5 us
    dot_general x2, matrix products, block_grads(): jnp.einsum('cqhk,cqhe->ckhe', soft_weights, grad_heads.astype(jnp.float32...  17.9 us
    unnamed x135, local copies, waits for them, and re-layouts  16.6 us
    dot_general x1, matrix products, fold_keys(): jnp.einsum('cqhk,ckhe->cqhe', exp_scores, value_heads.astype(jnp.float32)...  13.9 us
    dot_general x3, matrix products, scores_of(): jnp.einsum('cqhe,ckhe->cqhk', queries, key_heads, preferred_element_type=...  13.2 us
    dot_general x2, matrix products, block_grads(): jnp.einsum('cqhe,ckhe->cqhk', grad_heads, value_heads, preferred_element_...  9.46 us
  transfers between devices with their start and end apart: 9, of which 7 were waited for; matrix products, arithmetic and copies ran while one was open for 25% of the time, Pallas kernels for 0%

commit v1 on v0

v1 whole, which is shorter than its diff:
```python
import functools

import jax
import jax.numpy as jnp
from jax import lax
from jax.experimental import pallas as pl
from jax.experimental.pallas import tpu as pltpu
from jax.sharding import PartitionSpec as P

HEADS = 4
HEAD_DIM = 64
SLOT = 128
WIDE = HEADS * SLOT

EPSILON = 1e-05
NEGATIVE = -1e30
INV_ROOT_TWO_PI = 0.3989422804014327
BF = jnp.bfloat16
F32 = jnp.float32
VMEM_LIMIT = 16 * 1024 * 1024
MASK_ROWS = 16


def nn(left, right):
    return lax.dot_general(left, right, (((1,), (0,)), ((), ())), preferred_element_type=F32)


def nt(left, right):
    return lax.dot_general(left, right, (((1,), (1,)), ((), ())), preferred_element_type=F32)


def tn(left, right):
    return lax.dot_general(left, right, (((0,), (0,)), ((), ())), preferred_element_type=F32)


def lane_of(shape):
    return lax.broadcasted_iota(jnp.int32, shape, len(shape) - 1)


def row_of(shape):
    return lax.broadcasted_iota(jnp.int32, shape, len(shape) - 2)


def spread(matrix):
    pieces = []
    for pair in range(HEADS // 2):
        both = matrix[:, pair * SLOT : (pair + 1) * SLOT]
        first = lane_of(both.shape) < HEAD_DIM
        pieces.append(jnp.where(first, both, 0.0))
        pieces.append(jnp.where(first, pltpu.roll(both, HEAD_DIM, 1), 0.0))
    return jnp.concatenate(pieces, axis=1)


def joined(wide):
    pieces = []
    for pair in range(HEADS // 2):
        even = wide[:, 2 * pair * SLOT : (2 * pair + 1) * SLOT]
        odd = wide[:, (2 * pair + 1) * SLOT : (2 * pair + 2) * SLOT]
        pieces.append(jnp.where(lane_of(even.shape) < HEAD_DIM, even, pltpu.roll(odd, HEAD_DIM, 1)))
    return jnp.concatenate(pieces, axis=1)


def spread_rows(matrix):
    gap = jnp.zeros((SLOT - HEAD_DIM, matrix.shape[1]), matrix.dtype)
    pieces = []
    for head in range(HEADS):
        pieces += [matrix[head * HEAD_DIM : (head + 1) * HEAD_DIM], gap]
    return jnp.concatenate(pieces, axis=0)


def head_cols(head):
    return slice(head * SLOT, (head + 1) * SLOT)


def project_keys(x, w_all, bias_v, first_place, length, k_out, v_out):
    raw = nn(x, w_all[:, WIDE : 2 * WIDE])
    shut = lane_of(raw.shape) % SLOT == HEAD_DIM + 2
    shut &= row_of(raw.shape) + first_place >= length
    k_out[...] = jnp.where(shut, NEGATIVE, raw).astype(BF)
    one_row = lane_of((1, WIDE)) % SLOT
    ones_row = jnp.where((one_row == HEAD_DIM) | (one_row == HEAD_DIM + 1), 1.0, 0.0)
    v_out[...] = (nn(x, w_all[:, 2 * WIDE :]) + (spread(bias_v) + ones_row)).astype(BF)


def attend(queries, keys, values, kept):
    scores = nt(queries, keys)
    peak = jnp.max(scores, axis=1, keepdims=True)
    kept[...] = jnp.exp(scores - peak).astype(BF)
    return nn(kept[...], values), jnp.broadcast_to(peak, (peak.shape[0], SLOT))


def kept_rows(head, rows):
    return slice(head * rows, (head + 1) * rows)


def owner_of(distance, ring):
    return lax.rem(lax.axis_index("seq") - distance + ring, ring)


def mask_of(carrier, cell):
    rows = carrier.shape[0] - MASK_ROWS
    count = rows // carrier.shape[1]
    under = carrier[rows:, :].astype(F32)
    first = cell * count
    return jnp.concatenate([under[first + at : first + at + 1] for at in range(count)], axis=1)


def first_kernel(cells, lengths, *refs):
    xs, refs = refs[:cells], refs[cells:]
    wq, wk, wv, bias_q, bias_v, wo, w1, w2 = refs[:8]
    outs, (w_all, w_kv, wo_out, w1_out, w2_out) = refs[8:-5], refs[-5:]
    w_all[:, :WIDE] = spread(wq[...] * HEAD_DIM ** (-0.5)).astype(BF)
    w_all[:, WIDE : 2 * WIDE] = spread(wk[...]).astype(BF)
    w_all[:, 2 * WIDE :] = spread(wv[...]).astype(BF)
    rows = outs[0].shape[0]
    first_place = lax.axis_index("seq") * rows
    one_row = lane_of((1, WIDE)) % SLOT
    bias = spread(bias_q[...]) * HEAD_DIM ** (-0.5) + jnp.where(one_row == HEAD_DIM + 2, 1.0, 0.0)
    for cell in range(cells):
        x = xs[cell].at[:rows]
        q_out, k_out, v_out, kept_out, state_out, peak_out = outs[6 * cell : 6 * cell + 6]
        q_out[...] = (nn(x[...], w_all[:, :WIDE]) + bias).astype(BF)
        project_keys(x[...], w_all, bias_v[...], first_place, lengths[cell], k_out, v_out)
        for head in range(HEADS):
            cols = head_cols(head)
            state_out[:, cols], peak_out[:, cols] = attend(
                q_out[:, cols], k_out[:, cols], v_out[:, cols], kept_out.at[kept_rows(head, rows)]
            )
    width = wk.shape[1]
    w_kv[:, :width] = wk[...].astype(BF)
    w_kv[:, width:] = wv[...].astype(BF)
    wo_out[...] = spread_rows(wo[...].astype(BF))
    w1_out[...] = w1[...].astype(BF)
    w2_out[...] = w2[...].astype(BF)


def more_kernel(
    cell, distance, ring,
    lengths, x, q, state, peak, w_all, bias_v,
    k_out, v_out, kept_out, own_out, state_out, peak_out,
):
    rows = q.shape[0]
    first_place = owner_of(distance, ring) * rows
    project_keys(x[:rows, :], w_all, bias_v[...], first_place, lengths[cell], k_out, v_out)
    for head in range(HEADS):
        cols = head_cols(head)
        total, own = attend(
            q[:, cols], k_out[:, cols], v_out[:, cols], kept_out.at[kept_rows(head, rows)]
        )
        top = jnp.maximum(peak[:, cols], own)
        own_out[:, cols] = own
        peak_out[:, cols] = top
        state_out[:, cols] = state[:, cols] * jnp.exp(peak[:, cols] - top)
        state_out[:, cols] += total * jnp.exp(own - top)


def norm_parts(matrix):
    row_mean = jnp.mean(matrix, axis=1, keepdims=True)
    centred = matrix - row_mean
    row_var = jnp.mean(centred * centred, axis=1, keepdims=True)
    inverse = lax.rsqrt(row_var + EPSILON)
    return centred * inverse, inverse


def norm_back(grad, unit, inverse):
    shift = jnp.mean(grad, axis=1, keepdims=True)
    scale = jnp.mean(grad * unit, axis=1, keepdims=True)
    return (grad - shift - unit * scale) * inverse


def eight_sum(matrix):
    return jnp.sum(matrix.reshape(-1, 8, matrix.shape[1]), axis=0)


def inverse_of(value):
    guess = pl.reciprocal(value, approx=True)
    return guess * (2.0 - value * guess)


def gelu_parts(pre):
    bell = jnp.exp(pre * pre * (-0.5))
    t = inverse_of(1.0 + (0.3275911 * 0.7071067811865476) * jnp.abs(pre))
    poly = 0.5 * 1.061405429
    for factor in (-1.453152027, 1.421413741, -0.284496736, 0.254829592):
        poly = poly * t + 0.5 * factor
    tail = poly * t * bell
    half = jnp.where(pre >= 0.0, 1.0 - tail, tail)
    return pre * half, half + pre * bell * INV_ROOT_TWO_PI


def halve(pack, keep_out, give_out):
    half = keep_out.shape[0]
    core = lax.axis_index("core")
    keep_out[...] = pack[pl.ds(pl.multiple_of(core * half, half), half), :]
    give_out[...] = pack[pl.ds(pl.multiple_of((1 - core) * half, half), half), :]


def my_plane(ring):
    return lax.axis_index("x") * ring + lax.axis_index("seq")


def halve(pack, keep_out, give_out):
    half = keep_out.shape[0]
    core = lax.axis_index("core")
    keep_out[...] = pack[pl.ds(pl.multiple_of(core * half, half), half), :]
    give_out[...] = pack[pl.ds(pl.multiple_of((1 - core) * half, half), half), :]


def near_bits(ring, core):
    bits = [("seq", 1 << i) for i in range(ring.bit_length() - 1)]
    return bits + [("x", 1)] if core else [("x", 1)] + bits


def my_side(ring, step):
    sides = []
    for core in range(2):
        axis, bit = near_bits(ring, core)[step]
        sides.append(lax.rem(lax.axis_index(axis) // bit, 2))
    return jnp.where(lax.axis_index("core") == 0, sides[0], sides[1])


def halve_kernel(ring, step, keep, received, keep_out, give_out):
    half = keep_out.shape[0]
    side = my_side(ring, step)
    for out, place in ((keep_out, side), (give_out, 1 - side)):
        at = pl.ds(pl.multiple_of(place * half, half), half)
        out[...] = (keep[at, :].astype(F32) + received[at, :].astype(F32)).astype(BF)


def join_kernel(ring, step, mine, other, out):
    rows = mine.shape[0]
    side = my_side(ring, step)
    out[pl.ds(pl.multiple_of(side * rows, rows), rows), :] = mine[...]
    out[pl.ds(pl.multiple_of((1 - side) * rows, rows), rows), :] = other[...]


def divide_kernel(ring, keep, received, own_out, *give_outs):
    piece = own_out.shape[0]
    plane = my_plane(ring)
    for step, out in enumerate((own_out,) + give_outs):
        at = pl.ds(pl.multiple_of((plane ^ step) * piece, piece), piece)
        out[...] = (keep[at, :].astype(F32) + received[at, :].astype(F32)).astype(BF)


def place_pieces(ring, mine, other, pack_one, pack_two):
    plane, core = my_plane(ring), lax.axis_index("core")
    for step in range(2 * ring):
        start = 0
        for pack in (pack_one, pack_two):
            piece = pack.shape[0] // (4 * ring)
            for half, sources in ((core, mine), (1 - core, other)):
                at = pl.multiple_of((half * 2 * ring + (plane ^ step)) * piece, piece)
                pack[pl.ds(at, piece), :] = sources[step][start : start + piece, :]
            start += piece


def middle_kernel(
    cell, ring, carry, finish,
    lengths, x, q, state, peak, stream, cotangent, w_all, bias_v, wo, bias_o, gain_one, shift_one,
    w1, bias_1, w2, bias_2, gain_two, shift_two, *refs,
):
    count = ring - 1 if ring > 2 else 0
    before, refs = refs[:count], refs[count:]
    if carry:
        dwo_in, dw1_in, dw2_in, vec_in = refs[:4]
        refs = refs[4:]
    do_outs, refs = refs[:ring], refs[ring:]
    result_out, k_out, v_out, kept_out, first_out, vec_out = refs[:6]
    refs = refs[6:]
    if finish:
        keep_out, give_out = refs[:2]
        refs = refs[2:]
    else:
        dwo_out, dw1_out, dw2_out = refs[:3]
        refs = refs[3:]
    scales, refs = refs[:ring], refs[ring:]
    (
        attended_wide, attended_low, normed_low, active_low, hidden_low, branch_low, attn_low,
        unit_one, inverse_one, narrow_b, wide_b, acc, acc_wide, *pack_ref,
    ) = refs
    rows, width = stream.shape
    hidden = w1.shape[1]
    length = lengths[cell]
    first_place = owner_of(ring - 1, ring) * rows
    project_keys(x[:rows, :], w_all, bias_v[...], first_place, length, k_out, v_out)
    for head in range(HEADS):
        cols = head_cols(head)
        total, own = attend(
            q[:, cols], k_out[:, cols], v_out[:, cols], kept_out.at[kept_rows(head, rows)]
        )
        top = jnp.maximum(peak[:, cols], own)
        old_scale, own_scale = jnp.exp(peak[:, cols] - top), jnp.exp(own - top)
        both = state[:, cols] * old_scale + total * own_scale
        inverse = inverse_of(both[:, HEAD_DIM : HEAD_DIM + 1])
        attended = jnp.where(lane_of(both.shape) < HEAD_DIM, both * inverse, 0.0)
        attended_wide[:, cols] = attended
        attended_low[:, cols] = attended.astype(BF)
        scales[ring - 1][:, cols] = own_scale * inverse
        if ring == 2:
            scales[0][:, cols] = old_scale * inverse
        else:
            for block in range(ring - 1):
                scales[block][:, cols] = jnp.exp(before[block][:, cols] - top) * inverse

    my_place = lax.axis_index("seq") * rows

    valid = jnp.where(row_of((rows, width)) + my_place < length, 1.0, 0.0)

    def add(slot, matrix):
        acc[slot] = eight_sum(matrix)

    attn_out = nn(attended_low[...], wo[...]) + bias_o[...]
    unit, inverse = norm_parts(stream[...] + attn_out)
    unit_one[...] = unit
    inverse_one[...] = jnp.broadcast_to(inverse, (rows, SLOT))
    normed = unit * gain_one[...] + shift_one[...]
    narrow_b[...] = normed
    normed_low[...] = normed.astype(BF)
    add(8, stream[...] * stream[...] * valid)
    add(9, attn_out * attn_out * valid)

    active, slope = gelu_parts(nn(normed_low[...], w1[...]) + bias_1[...])
    active_low[...] = active.astype(BF)
    wide_b[...] = slope

    branch = nn(active_low[...], w2[...]) + bias_2[...]
    unit, inverse = norm_parts(narrow_b[...] + branch)
    result_out[...] = unit * gain_two[...] + shift_two[...]
    grad_result = cotangent[...] * valid
    grad_second = norm_back(grad_result * gain_two[...], unit, inverse)
    narrow_b[...] = grad_second
    branch_bf = grad_second.astype(BF)
    branch_low[...] = branch_bf
    add(0, grad_result * unit)
    add(1, grad_result)
    add(2, branch_bf.astype(F32))
    add(10, branch * branch * valid)
    add(11, valid)

    hidden_bf = (nt(branch_low[...], w2[...]) * wide_b[...]).astype(BF)
    hidden_low[...] = hidden_bf
    acc_wide[...] = eight_sum(hidden_bf.astype(F32))

    grad_normed = narrow_b[...] + nt(hidden_low[...], w1[...])
    unit = unit_one[...]
    grad_first = norm_back(grad_normed * gain_one[...], unit, inverse_one[:, :1])
    first_out[...] = grad_first
    attn_bf = grad_first.astype(BF)
    attn_low[...] = attn_bf
    add(5, grad_normed * unit)
    add(6, grad_normed)
    add(7, attn_bf.astype(F32))

    do_wide = nt(attn_low[...], wo[...]).astype(BF).astype(F32)
    for head in range(HEADS):
        cols = head_cols(head)
        do_head = do_wide[:, cols]
        row_dot = jnp.sum(do_head * attended_wide[:, cols], axis=1, keepdims=True)
        lane = lane_of(do_head.shape)
        for scale, do_out in zip(scales, do_outs):
            factor = scale[:, cols]
            dot = -row_dot * factor
            rest = dot - dot.astype(BF).astype(F32)
            scaled = jnp.where(lane == HEAD_DIM, dot, do_head * factor)
            do_out[:, cols] = jnp.where(lane == HEAD_DIM + 1, rest, scaled).astype(BF)

    hidden_sum = jnp.sum(acc_wide[...], axis=0, keepdims=True)
    sums = [
        hidden_sum[:, (slot - 3) * width : (slot - 2) * width]
        if slot in (3, 4)
        else jnp.sum(acc[slot], axis=0, keepdims=True)
        for slot in range(12)
    ]
    vec = jnp.concatenate(sums + [jnp.zeros((4, width), F32)], axis=0)
    vec_out[...] = vec + vec_in[...] if carry else vec

    dwo = tn(attn_low[...], attended_low[...])
    dw1 = tn(normed_low[...], hidden_low[...])
    dw2 = tn(branch_low[...], active_low[...])
    if carry:
        dwo += dwo_in[...]
        dw1 += dw1_in[...]
        dw2 += dw2_in[...]
    if not finish:
        dwo_out[...] = dwo
        dw1_out[...] = dw1
        dw2_out[...] = dw2
        return
    (pack,) = pack_ref
    pack[:width, :] = joined(dwo).astype(BF)
    pack[width : 2 * width, :] = dw1[:, :width].astype(BF)
    pack[2 * width : 3 * width, :] = dw1[:, width:].astype(BF)
    for at in range(0, hidden, width):
        pack[3 * width + at : 4 * width + at, :] = dw2[:, at : at + width].astype(BF)
    used = 3 * width + hidden
    if pack.shape[0] > used:
        pack[used:, :] = jnp.zeros((pack.shape[0] - used, width), BF)
    halve(pack, keep_out, give_out)


def head_grads(q, k, v, do, kept):
    score_grad = (kept.astype(F32) * nt(do, v)).astype(BF)
    return (
        nn(score_grad, k),
        tn(q[:, :HEAD_DIM], score_grad),
        tn(do[:, :HEAD_DIM], kept),
    )


def all_heads(q, k, v, do, kept, low, put_query):
    rows = q.shape[0]
    for head in range(HEADS):
        cols = head_cols(head)
        dq, dk, dv = head_grads(
            q[:, cols], k[:, cols], v[:, cols], do[:, cols], kept[kept_rows(head, rows), :]
        )
        put_query(cols, dq)
        low[head * HEAD_DIM : (head + 1) * HEAD_DIM, :] = dk.astype(BF)
        at = (HEADS + head) * HEAD_DIM
        low[at : at + HEAD_DIM, :] = dv.astype(BF)


def masked_sum(carrier, cell, grad_bf):
    mask = mask_of(carrier, cell)
    picked = jnp.broadcast_to(mask, (8, mask.shape[1])).astype(BF)
    return nn(picked, grad_bf)[0:1]


def value_sums(low):
    half = low.shape[0] // 2
    sums = jnp.sum(low[half:, :].astype(F32), axis=1, keepdims=True)
    return jnp.broadcast_to(sums, (half, SLOT))


def block_kernel(cell, carry_dq, carry, sent, carrier, q, do, k, v, kept, w_kv, *refs):
    if carry_dq:
        dq_in, refs = refs[0], refs[1:]
    if carry:
        (dw_in, sum_in, vec_in), refs = refs[:3], refs[3:]
    dq_out, dx_out, dw_out, sum_out, vec_out, low = refs

    def put_query(cols, dq):
        dq_out[:, cols] = dq + dq_in[:, cols] if carry_dq else dq

    all_heads(q, k, v, do, kept, low, put_query)
    x = sent[: q.shape[0], :]
    dx_bf = jnp.transpose(nn(w_kv[...], low[...])).astype(BF)
    dx_out[...] = dx_bf
    dw = nn(low[...], x)
    dw_out[...] = dw + dw_in[...] if carry else dw
    sums = value_sums(low)
    sum_out[...] = sums + sum_in[...] if carry else sums
    vec_out[...] = vec_in[...] if carry else jnp.zeros_like(vec_out)
    vec_out[0:1, : x.shape[1]] += masked_sum(carrier[...], cell, dx_bf)


def last_kernel(
    cell, carry, finish,
    sent, carrier, q, do, k, v, kept, w_all, w_kv, first, dq_in, dw_in, sum_in, vec_in, *refs
):
    if carry:
        dwq_in, refs = refs[0], refs[1:]
    if finish:
        vec_mid, dx_out, keep_out, give_out, low_q, low, pack = refs
    else:
        dx_out, dw_out, sum_out, vec_out, dwq_out, low_q, low = refs

    def put_query(cols, dq):
        low_q[:, cols] = ((dq + dq_in[:, cols]) * HEAD_DIM ** (-0.5)).astype(BF)

    all_heads(q, k, v, do, kept, low, put_query)
    grads = first[...] + nt(low_q[...], w_all[:, :WIDE]) * HEAD_DIM**0.5
    grads += jnp.transpose(nn(w_kv[...], low[...]))
    dx_out[...] = grads
    width = grads.shape[1]
    x = sent[: q.shape[0], :]
    dwq = tn(x, low_q[...])
    dw = nn(low[...], x) + dw_in[...]
    sum_q = jnp.sum(low_q[...].astype(F32), axis=0, keepdims=True) + vec_in[1:2, :]
    sum_v = value_sums(low) + sum_in[...]
    sum_mask = masked_sum(carrier[...], cell, grads.astype(BF)) + vec_in[0:1, :width]
    if carry:
        dwq += dwq_in[...]
    if not finish:
        dwq_out[...] = dwq
        dw_out[...] = dw
        sum_out[...] = sum_v
        vec_out[...] = jnp.zeros_like(vec_out)
        vec_out[0:1, :width] = sum_mask
        vec_out[1:2, :] = sum_q
        return
    pack[:width, :] = joined(dwq).astype(BF)
    pack[width : 3 * width, :] = dw.astype(BF)
    rows = jnp.concatenate(
        [
            vec_mid[:12, :],
            joined(sum_q),
            jnp.transpose(sum_v)[0:1, :],
            sum_mask,
            jnp.zeros((1, width), F32),
        ],
        axis=0,
    )
    high = rows.astype(BF)
    pack[3 * width : 3 * width + 16, :] = high
    pack[3 * width + 16 : 3 * width + 32, :] = (rows - high.astype(F32)).astype(BF)
    used = 3 * width + 32
    if pack.shape[0] > used:
        pack[used:, :] = jnp.zeros((pack.shape[0] - used, width), BF)
    halve(pack, keep_out, give_out)


def unpack_kernel(ring, *refs):
    mine, other, refs = refs[: 2 * ring], refs[2 * ring : 4 * ring], refs[4 * ring :]
    dwo_out, dw1_out, dw2_out, dwq_out, dwk_out, dwv_out = refs[:6]
    outs, pack_one, pack = refs[6:-2], refs[-2], refs[-1]
    place_pieces(ring, mine, other, pack_one, pack)
    width = pack.shape[1]
    dwo_out[...] = jnp.transpose(pack_one[:width, :].astype(F32))
    dw1_out[:, :width] = pack_one[width : 2 * width, :].astype(F32)
    dw1_out[:, width:] = pack_one[2 * width : 3 * width, :].astype(F32)
    for at in range(0, dw2_out.shape[0], width):
        dw2_out[at : at + width, :] = jnp.transpose(
            pack_one[3 * width + at : 4 * width + at, :].astype(F32)
        )
    dwq_out[...] = pack[:width, :].astype(F32)
    dwk_out[...] = jnp.transpose(pack[width : 2 * width, :].astype(F32))
    dwv_out[...] = jnp.transpose(pack[2 * width : 3 * width, :].astype(F32))
    vec = pack[3 * width : 3 * width + 16, :].astype(F32)
    vec += pack[3 * width + 16 : 3 * width + 32, :].astype(F32)
    for out, row in zip(outs, (0, 1, 2, (3, 4), 5, 6, 7, 12, 13, 14)):
        if isinstance(row, tuple):
            out[:, :width] = vec[row[0] : row[0] + 1]
            out[:, width:] = vec[row[1] : row[1] + 1]
        else:
            out[...] = vec[row : row + 1]
    squares = jnp.sum(vec[8:16], axis=1, keepdims=True)
    count = vec[11:12, 0:1]
    means = jnp.sqrt(squares / (count * width))
    lane = lane_of((1, 3))
    outs[10][...] = jnp.where(
        lane == 0, means[0:1], jnp.where(lane == 1, means[1:2], means[2:3])
    )


def finish_kernel(cells, carrier, *refs):
    local, received, out = refs[:cells], refs[cells:-1], refs[-1]
    rows, count = local[0].shape[0], len(received) // cells
    for cell in range(cells):
        grads = local[cell][...]
        for piece in received[cell * count : (cell + 1) * count]:
            grads += piece[...].astype(F32)
        mask = jnp.broadcast_to(mask_of(carrier[...], cell), (8, rows))
        out[cell] = jnp.where(jnp.transpose(mask)[:, :1] == 1.0, 0.0, grads)


def call(kernel, ins, outs, scratch=(), flops=0):
    moved = sum(a.size * a.dtype.itemsize for a in ins) + sum(
        s.size * s.dtype.itemsize for s in outs
    )
    vmem = pl.BlockSpec(memory_space=pltpu.VMEM)
    smem = pl.BlockSpec(memory_space=pltpu.SMEM)
    return pl.pallas_call(
        kernel,
        in_specs=[smem if a.ndim == 1 else vmem for a in ins],
        out_specs=[vmem] * len(outs),
        out_shape=outs,
        scratch_shapes=list(scratch),
        compiler_params=pltpu.CompilerParams(vmem_limit_bytes=VMEM_LIMIT),
        cost_estimate=pl.CostEstimate(
            flops=flops, bytes_accessed=moved if flops != 1 else 1, transcendentals=0
        ),
    )(*ins)


def send(block, distance, ring):
    route = [(i, (i + distance) % ring) for i in range(ring)]
    return lax.ppermute(block, "seq", route)


NEAR = ("x", "core", "seq")
PLANE = ("x", "seq")


def swap(block, axes, step):
    return lax.ppermute(block, axes, [(i, i ^ step) for i in range(lax.axis_size(axes))])


def tree_sum(blocks):
    blocks = [block.astype(F32) for block in blocks]
    while len(blocks) > 1:
        blocks = [a + b for a, b in zip(blocks[::2], blocks[1::2])]
    return blocks[0].astype(BF)


def swaps(blocks, axes):
    return {step: swap(blocks[step], axes, step) for step in sorted(blocks, reverse=True)}


def sum_steps(own, got):
    return tree_sum([own] + [got[step] for step in sorted(got)])


def divide(keep, received, ring):
    half, width = keep.shape
    piece = jax.ShapeDtypeStruct((half // (2 * ring), width), BF)
    own, *pieces = call(
        functools.partial(divide_kernel, ring), [keep, received], [piece] * (2 * ring)
    )
    return own, dict(enumerate(pieces, 1))


def to_all(block, axes):
    return swaps({step: block for step in range(1, lax.axis_size(axes))}, axes)


def padded(rows, pieces):
    piece = -(-rows // pieces)
    return -(-piece // 16) * 16 * pieces


def body(
    tokens, masked, lengths, cotangent, mask_embed, query_weight, query_bias, key_weight,
    value_weight, value_bias, out_weight, out_bias, gain_one, shift_one, expand_weight,
    expand_bias, reduce_weight, reduce_bias, gain_two, shift_two,
):
    cells, rows, width = tokens.shape
    hidden = expand_weight.shape[1]
    ring = lax.axis_size("seq")

    def row(vector):
        return vector.reshape(1, -1)

    shape = jax.ShapeDtypeStruct
    low_wide, full_wide = shape((rows, WIDE), BF), shape((rows, WIDE), F32)
    low_narrow, full_narrow = shape((rows, width), BF), shape((rows, width), F32)
    weights = shape((HEADS * rows, rows), BF)
    score_flops = 2 * rows * rows * HEADS * 256

    stream = [
        jnp.where(masked[cell][:, None] == 1, mask_embed, tokens[cell]) for cell in range(cells)
    ]
    x_low = [part.astype(BF) for part in stream]
    x_moved = [[part] for part in x_low]
    x_moved[0] += [send(x_low[0], t, ring) for t in range(1, ring)]
    under = masked.astype(BF).reshape(-1, width)
    under = jnp.pad(under, ((0, MASK_ROWS - under.shape[0]), (0, 0)))
    x_moved[-1] = [jnp.concatenate([x_low[-1], under], axis=0)]

    made = call(
        functools.partial(first_kernel, cells),
        [lengths]
        + x_low
        + [query_weight, key_weight, value_weight, row(query_bias), row(value_bias)]
        + [out_weight, expand_weight, reduce_weight],
        [low_wide, low_wide, low_wide, weights, full_wide, full_wide] * cells
        + [
            shape((width, 3 * WIDE), BF),
            shape((width, 2 * width), BF),
            shape((WIDE, width), BF),
            shape((width, hidden), BF),
            shape((hidden, width), BF),
        ],
        flops=2 * cells * score_flops,
    )
    w_all, w_kv, wo, w1, w2 = made[-5:]
    bias_v = row(value_bias)
    for cell in range(1, cells):
        sent, w_all = lax.optimization_barrier((x_moved[cell][0], w_all))
        x_moved[cell] += [send(sent, t, ring) for t in range(1, ring)]
    keys, values, kept, queries, states, peaks = [], [], [], [], [], []
    for cell in range(cells):
        q, k, v, p, state, peak = made[6 * cell : 6 * cell + 6]
        queries.append(q)
        keys.append([k])
        values.append([v])
        kept.append([p])
        own_peaks = [peak]
        for t in range(1, ring - 1):
            k, v, p, own, state, peak = call(
                functools.partial(more_kernel, cell, t, ring),
                [lengths, x_moved[cell][t], q, state, peak, w_all, bias_v],
                [low_wide, low_wide, weights, full_wide, full_wide, full_wide],
                flops=2 * score_flops,
            )
            keys[cell].append(k)
            values[cell].append(v)
            kept[cell].append(p)
            own_peaks.append(own)
        states.append([state, peak])
        peaks.append(own_peaks if ring > 2 else [])

    one_rows = padded(3 * width + hidden, lax.axis_size(NEAR))
    results, firsts, grads_out = [], [], []
    carried, carried_back, received = [], [], []
    dq = [None] * cells

    def backward_of_blocks(cell):
        nonlocal carried_back
        partial = []
        for t in range(1, ring):
            ins = [
                x_moved[cell][t], x_moved[-1][t], queries[cell], grads_out[cell][t],
                keys[cell][t], values[cell][t], kept[cell][t], w_kv,
            ]
            ins += ([dq[cell]] if t > 1 else []) + carried_back
            dq[cell], dx, *carried_back = call(
                functools.partial(block_kernel, cell, t > 1, bool(carried_back)),
                ins,
                [
                    full_wide,
                    low_narrow,
                    shape((2 * width, width), F32),
                    shape((width, SLOT), F32),
                    shape((8, WIDE), F32),
                ],
                [pltpu.VMEM((2 * width, rows), BF)],
                flops=5 * score_flops,
            )
            partial.append(dx)
        return partial

    def returned(partial):
        return [send(dx, -t, ring) for t, dx in enumerate(partial, 1)]

    for cell in range(cells):
        finish = cell == cells - 1
        if cell > 0:
            partial = backward_of_blocks(cell - 1)
            states[cell], partial = lax.optimization_barrier((states[cell], partial))
            received.append(returned(partial))
        outs = [low_wide] * ring
        outs += [full_narrow, low_wide, low_wide, weights, full_narrow]
        outs += [shape((16, width), F32)]
        if finish:
            outs += [shape((one_rows // 2, width), BF)] * 2
        else:
            outs += [shape((width, WIDE), F32)] + [shape((width, hidden), F32)] * 2
        scratch = [pltpu.VMEM((rows, WIDE), F32)] * ring + [
            pltpu.VMEM((rows, WIDE), F32),
            pltpu.VMEM((rows, WIDE), BF),
            pltpu.VMEM((rows, width), BF),
            pltpu.VMEM((rows, hidden), BF),
            pltpu.VMEM((rows, hidden), BF),
            pltpu.VMEM((rows, width), BF),
            pltpu.VMEM((rows, width), BF),
            pltpu.VMEM((rows, width), F32),
            pltpu.VMEM((rows, SLOT), F32),
            pltpu.VMEM((rows, width), F32),
            pltpu.VMEM((rows, hidden), F32),
            pltpu.VMEM((12, 8, width), F32),
            pltpu.VMEM((8, hidden), F32),
        ]
        if finish:
            scratch.append(pltpu.VMEM((one_rows, width), BF))
        made = call(
            functools.partial(middle_kernel, cell, ring, bool(carried), finish),
            [
                lengths, x_moved[cell][ring - 1], queries[cell], *states[cell], stream[cell],
                cotangent[cell], w_all, bias_v, wo, row(out_bias), row(gain_one), row(shift_one),
                w1, row(expand_bias), w2, row(reduce_bias), row(gain_two), row(shift_two),
            ]
            + peaks[cell]
            + carried,
            outs,
            scratch,
            flops=7 * score_flops,
        )
        grads_out.append(made[:ring])
        result, k, v, p, first, vec_mid = made[ring : ring + 6]
        results.append(result)
        keys[cell].append(k)
        values[cell].append(v)
        kept[cell].append(p)
        firsts.append(first)
        carried = list(made[ring + 6 :]) + [vec_mid]
    keep, give = made[ring + 6 :]
    received_one = swap(give, "core", 1)
    queries[-1], received = lax.optimization_barrier((queries[-1], received))
    partial = backward_of_blocks(cells - 1)
    own_one, pieces = divide(keep, received_one, ring)
    carried, partial, own_one, pieces = lax.optimization_barrier(
        (carried_back, partial, own_one, pieces)
    )
    got_one = swaps(pieces, PLANE)

    two_rows = padded(3 * width + 32, lax.axis_size(NEAR))
    local = []
    depth_steps = [1 << i for i in range(lax.axis_size("z").bit_length() - 1)]
    for cell in range(cells):
        finish = cell == cells - 1
        if finish:
            carried, got_one, partial = lax.optimization_barrier((carried, got_one, partial))
            own_one = sum_steps(own_one, got_one)
            got_one = swap(own_one, "z", depth_steps[0])
            received.append(returned(partial))
        ins = [
            x_moved[cell][0], x_moved[-1][0], queries[cell], grads_out[cell][0], keys[cell][0],
            values[cell][0], kept[cell][0], w_all, w_kv, firsts[cell], dq[cell],
        ]
        outs = [full_narrow]
        scratch = [pltpu.VMEM((rows, WIDE), BF), pltpu.VMEM((2 * width, rows), BF)]
        if finish:
            outs += [shape((two_rows // 2, width), BF)] * 2
            scratch += [pltpu.VMEM((two_rows, width), BF)]
        else:
            outs += [shape((2 * width, width), F32), shape((width, SLOT), F32)]
            outs += [shape((8, WIDE), F32), shape((width, WIDE), F32)]
        made = call(
            functools.partial(last_kernel, cell, cell > 0, finish),
            ins + carried + ([vec_mid] if finish else []),
            outs,
            scratch,
            flops=1,
        )
        local.append(made[0])
        carried = list(made[1:])
    keep, give = carried
    give, got_one = lax.optimization_barrier((give, got_one))
    other = swap(give, "core", 1)
    for step in depth_steps[1:]:
        own_one = tree_sum([own_one, got_one])
        got_one = swap(own_one, "z", step)
    other, received = lax.optimization_barrier((other, received))
    own, pieces = divide(keep, other, ring)
    got, got_one = lax.optimization_barrier((swaps(pieces, PLANE), got_one))
    own = sum_steps(own, got)
    own = sum_steps(own, to_all(own, "z"))
    own_one = tree_sum([own_one, got_one])
    own = jnp.concatenate([own_one, own], axis=0)
    tokens_grad = call(
        functools.partial(finish_kernel, cells),
        [x_moved[-1][0]] + local + sum(received, []),
        [shape((cells, rows, width), F32)],
    )[0]
    got = to_all(own, PLANE)
    result = jnp.stack(results)
    got[1], tokens_grad, result = lax.optimization_barrier((got[1], tokens_grad, result))
    mine = [own] + [got[step] for step in sorted(got)]
    other = [swap(piece, "core", 1) for piece in mine]

    vector = shape((1, width), F32)
    made = call(
        functools.partial(unpack_kernel, ring),
        mine + other,
        [shape((width, width), F32), shape((width, hidden), F32), shape((hidden, width), F32)]
        + [shape((width, width), F32)] * 3
        + [vector] * 3
        + [shape((1, hidden), F32)]
        + [vector] * 6
        + [shape((1, 3), F32)],
        [pltpu.VMEM((one_rows, width), BF), pltpu.VMEM((two_rows, width), BF)],
    )
    dwo, dw1, dw2, dwq, dwk, dwv = made[:6]
    (
        gain_two_grad, shift_two_grad, bias_2_grad, bias_1_grad, gain_one_grad, shift_one_grad,
        bias_o_grad, bias_q_grad, bias_v_grad, mask_embed_grad, root_means,
    ) = [a.reshape(-1) for a in made[6:]]

    return (
        result,
        tokens_grad,
        mask_embed_grad,
        dwq,
        bias_q_grad,
        dwk,
        dwv,
        bias_v_grad,
        dwo,
        bias_o_grad,
        gain_one_grad,
        shift_one_grad,
        dw1,
        bias_1_grad,
        dw2,
        bias_2_grad,
        gain_two_grad,
        shift_two_grad,
        root_means,
    )


def solution(mesh):
    dp, seq = mesh.shape["dp"], mesh.shape["seq"]
    cut = jax.sharding.Mesh(mesh.devices.reshape(dp // 4, 2, 2, seq), ("z",) + NEAR)
    dp = ("z", "x", "core")
    split = P(dp, "seq", None)
    return jax.shard_map(
        body,
        mesh=cut,
        in_specs=(split, P(dp, "seq"), P(dp), split) + (P(),) * 16,
        out_specs=(split, split) + (P(),) * 17,
        check_vma=False,
    )
```

time: 338 us -> 78.5 us (0.23); the launches traced: 332 us -> 78.2 us
  waiting for transfers between devices: 129 us -> 12.5 us
  matrix products: 78.9 us -> 0 us
  blocking collectives: 41 us -> 0 us
  local copies, waits for them, and re-layouts: 37.1 us -> 1.26 us
  Pallas kernels: 0 us -> 34.3 us
  other arithmetic: 23.5 us -> 3.49 us
  starting transfers between devices: 7.44 us -> 25.5 us
  between operations: 15.4 us -> 1.18 us
    psum x1 -> x0, waiting for transfers between devices: 84 us -> none  [body(): lax.psum((mask_embed_grad, joined_weight_grad, joined_bias_grad[:model_wi...]
    dot_general x24 -> x0, matrix products: 78.9 us -> none  [the longest x2 17.9 us: block_grads(): jnp.einsum('cqhk,cqhe->ckhe', soft_weights, grad_heads.astype(jnp.float32...]
    psum x1 -> x0, blocking collectives: 41 us -> none  [body(): lax.psum((mask_embed_grad, joined_weight_grad, joined_bias_grad[:model_wi...]
    pallas_call x0 -> x11, Pallas kernels: none -> 34.3 us  [call(): pl.pallas_call(kernel, in_specs=[smem if a.ndim == 1 else vmem for a in i...]
    ppermute x6 -> x24, waiting for transfers between devices: 38.5 us -> 12.5 us  [the longest x20 11.7 us: swap(): lax.ppermute(block, axes, [(i, i ^ step) for i in range(lax.axis_size(axe...]
    ppermute x6 -> x24, starting transfers between devices: 7.33 us -> 25.5 us  [the longest x20 20.1 us: swap(): lax.ppermute(block, axes, [(i, i ^ step) for i in range(lax.axis_size(axe...]
    unnamed x135 -> x36, local copies, waits for them, and re-layouts: 16.6 us -> 1.18 us
    reduce_sum x10 -> x0, other arithmetic: 11.6 us -> none  [the longest x1 4.67 us: fold_keys(): running_sum = jnp.sum(exp_scores, axis=3)]
  transfers between devices with their start and end apart: 9 -> 24, of which waited for: 7 -> 13; matrix products, arithmetic and copies ran while one was open for 25% -> 2% of each run, Pallas kernels for 0% -> 37%
where the time goes in v1:
time: 78.5 us; the launch traced here: 78.2 us
  Pallas kernels  34.3 us (44%)
  starting transfers between devices  25.5 us (32%)
  waiting for transfers between devices  12.5 us (16%)
  other arithmetic  3.49 us (4%)
  local copies, waits for them, and re-layouts  1.26 us (2%)
  between operations  1.18 us (2%)
    pallas_call x11, Pallas kernels, call(): pl.pallas_call(kernel, in_specs=[smem if a.ndim == 1 else vmem for a in i...  34.3 us
    ppermute x20, starting transfers between devices, swap(): lax.ppermute(block, axes, [(i, i ^ step) for i in range(lax.axis_size(axe...  20.1 us
    ppermute x20, waiting for transfers between devices, swap(): lax.ppermute(block, axes, [(i, i ^ step) for i in range(lax.axis_size(axe...  11.7 us
    ppermute x4, starting transfers between devices, send(): return lax.ppermute(block, 'seq', route)  5.42 us
  transfers between devices with their start and end apart: 24, of which 13 were waited for; matrix products, arithmetic and copies ran while one was open for 2% of the time, Pallas kernels for 37%

profile of v1, /device:TPU:0, one launch (start us, length us, event | category | flops | bytes accessed | tf_op | source)
XLA Modules:
  0.0 78.2 jit_solution(1968701907345452747)
XLA Ops:
  0.7 0.9 %compare_reduce_fusion = (pred[512]{0:T(512)(128)(4,1)S(1)}, pred[512]{0:T(512)(128)(4,1)S(1)}) fusion(s32[2,512]{1,0:T(2,128)} %param.21), kind=kLoop, calls=%fused_computation.14 | loop fusion | flops 1024 | bytes 5120 | tf_op jit(solution)/shard_map/eq | solution.py:641
  1.6 1.4 %fusion.2 = (bf16[512,256]{1,0:T(8,128)(2,1)S(1)}, f32[512,256]{1,0:T(8,128)S(1)}, bf16[512,256]{1,0:T(8,128)(2,1)S(1)}, f32[512,256]{1,0:T(8,128)S(1)}) fusion(f32[2,512,256]{2,1,0:T(8,128)} %param.20, f32[256]{0:T(256)} %param.24, pred[512]{0:T(512)(128)(4,1)S(1)} %get-tuple-element.251, pred[512]{0:T(512)(128)(4,1)S(1)} %get-tuple-element.252), kind=kLoop, calls=%fused_computation.16 | loop fusion | flops 524288 | bytes 2623488 | tf_op jit(solution)/shard_map/convert_element_type | solution.py:643
  3.0 3.0 %collective-permute-start.1 = (bf16[512,256]{1,0:T(8,128)(2,1)S(1)}, bf16[512,256]{1,0:T(8,128)(2,1)}, u32[]{:S(2)}, u32[]{:S(2)}) collective-permute-start(bf16[512,256]{1,0:T(8,128)(2,1)S(1)} %get-tuple-element.253.refs_0_.sent), channel_id=1, source_target_pairs={{0,1},{1,0},{2,3},{3,2},{4,5},{5,4},{6,7},{7,6},{8,9},{9,8},{10,11... | collective-permute-start | bytes 786440 | tf_op jit(solution)/shard_map/ppermute | solution.py:578
  6.2 0.9 %copy-done.5 = f32[256,256]{1,0:T(8,128)S(1)} copy-done((f32[256,256]{1,0:T(8,128)S(1)}, f32[256,256]{1,0:T(8,128)}, u32[]{:S(2)}) %copy-start.5) | copy-done | bytes 262168
  7.1 4.7 %shard_map.339 = (bf16[512,512]{1,0:T(8,128)(2,1)S(1)}, bf16[512,512]{1,0:T(8,128)(2,1)S(1)}, bf16[512,512]{1,0:T(8,128)(2,1)S(1)}, bf16[2048,512]{1,0:T(8,128)(...) custom-call(s32[2]{0:T(128)S(1)} %copy-done.15, ...), custom_call_target="tpu_custom_call" | custom-call | flops 2147483648 | bytes 15992840 | tf_op jit(solution)/shard_map/pallas_call | solution.py:563
  11.9 0.1 collective-permute-start
  12.1 0.4 collective-permute-done.1.x.sent
  12.5 0.1 copy-done.6
  12.6 6.9 %shard_map.340 = (bf16[512,512]{1,0:T(8,128)(2,1)S(1)}, bf16[512,512]{1,0:T(8,128)(2,1)S(1)}, f32[512,256]{1,0:T(8,128)S(1)}, bf16[512,512]{1,0:T(8,128)(2,1)S(1...) custom-call(s32[2]{0:T(128)S(1)} %copy-done.15, ...), custom_call_target="tpu_custom_call" | custom-call | flops 3758096384 | bytes 12346376 | tf_op jit(solution)/shard_map/pallas_call | solution.py:563
  19.5 0.4 collective-permute-done.carrier.x.sent
  19.9 3.6 %shard_map.341 = (f32[512,512]{1,0:T(8,128)S(1)}, bf16[512,256]{1,0:T(8,128)(2,1)S(1)}, f32[512,256]{1,0:T(8,128)S(1)}, f32[256,128]{1,0:T(8,128)S(1)}, f32[8,512]{1,0:T(8,128)S(1)}) custom-call(bf16[512,256]{1,0:T(8,128)(2,1)} %collective-permute-done.1.x.sent, bf16[528,256]{1,0:T(8,128)(2,1)S(1)} %collective-permute-done.carrier.x.sent, ...), custom_call_target="tpu_custom_call" | custom-call | flops 2684354560 | bytes 6971392 | tf_op jit(solution)/shard_map/pallas_call | solution.py:563
  23.6 1.2 %collective-permute-start.2 = (bf16[512,256]{1,0:T(8,128)(2,1)S(1)}, bf16[512,256]{1,0:T(8,128)(2,1)S(1)}, u32[]{:S(2)}, u32[]{:S(2)}) collective-permute-start(bf16[512,256]{1,0:T(8,128)(2,1)S(1)} %get-tuple-element.153), channel_id=1, source_target_pairs={{0,1},{1,0},{2,3},{3,2},{4,5},{5,4},{6,7},{7,6},{8,9},{9,8},{10,11... | collective-permute-start | bytes 786440 | tf_op jit(solution)/shard_map/ppermute | solution.py:578
  24.8 6.6 %shard_map.342 = (bf16[512,512]{1,0:T(8,128)(2,1)S(1)}, bf16[512,512]{1,0:T(8,128)(2,1)S(1)}, f32[512,256]{1,0:T(8,128)S(1)}, bf16[512,512]{1,0:T(8,128)(2,1)S(1...) custom-call(s32[2]{0:T(128)S(1)} %copy-done.15, ...), custom_call_target="tpu_custom_call" | custom-call | flops 3758096384 | bytes 13026312 | tf_op jit(solution)/shard_map/pallas_call | solution.py:563
  31.4 0.1 collective-permute-start.3
  31.5 2.5 %shard_map.343 = (f32[512,512]{1,0:T(8,128)S(1)}, bf16[512,256]{1,0:T(8,128)(2,1)S(1)}, f32[512,256]{1,0:T(8,128)S(1)}, f32[256,128]{1,0:T(8,128)S(1)}, f32[8,512]{1,0:T(8,128)S(1)}) custom-call(bf16[528,256]{1,0:T(8,128)(2,1)S(1)} %collective-permute-done.carrier.x.sent, bf16[528,256]{1,0:T(8,128)(2,1)S(1)} %collective-permute-done.carrier.x.sent, ...), custom_call_target="tpu_custom_call" | custom-call | flops 2684354560 | bytes 7651328 | tf_op jit(solution)/shard_map/pallas_call | solution.py:563
  34.0 0.1 shard_map.344
  34.1 0.9 %collective-permute-start.4 = (bf16[160,256]{1,0:T(8,128)(2,1)S(1)}, bf16[160,256]{1,0:T(8,128)(2,1)S(1)}, u32[]{:S(2)}, u32[]{:S(2)}) collective-permute-start(bf16[160,256]{1,0:T(8,128)(2,1)S(1)} %get-tuple-element.192), channel_id=1, source_target_pairs={{0,1},{1,0},{4,5},{5,4},{2,3},{3,2},{6,7},{7,6},{8,9},{9,8},{12,13... | collective-permute-start | bytes 245768 | tf_op jit(solution)/shard_map/ppermute | solution.py:586
  35.0 1.5 %collective-permute-start.5 = (bf16[160,256]{1,0:T(8,128)(2,1)S(1)}, bf16[160,256]{1,0:T(8,128)(2,1)S(1)}, u32[]{:S(2)}, u32[]{:S(2)}) collective-permute-start(bf16[160,256]{1,0:T(8,128)(2,1)S(1)} %get-tuple-element.193), channel_id=1, source_target_pairs={{0,4},{1,5},{4,0},{5,1},{2,6},{3,7},{6,2},{7,3},{8,12},{9,13},{12,... | collective-permute-start | bytes 245768 | tf_op jit(solution)/shard_map/ppermute | solution.py:586
  36.5 1.2 %collective-permute-start.6 = (bf16[160,256]{1,0:T(8,128)(2,1)S(1)}, bf16[160,256]{1,0:T(8,128)(2,1)S(1)}, u32[]{:S(2)}, u32[]{:S(2)}) collective-permute-start(bf16[160,256]{1,0:T(8,128)(2,1)S(1)} %get-tuple-element.194), channel_id=1, source_target_pairs={{0,5},{1,4},{4,1},{5,0},{2,7},{3,6},{6,3},{7,2},{8,13},{9,12},{12,... | collective-permute-start | bytes 245768 | tf_op jit(solution)/shard_map/ppermute | solution.py:586
  37.7 3.0 %shard_map.345 = (f32[512,256]{1,0:T(8,128)S(1)}, f32[512,256]{1,0:T(8,128)S(1)}, f32[256,128]{1,0:T(8,128)S(1)}, f32[8,512]{1,0:T(8,128)S(1)}, f32[256,512]{1,0:T(8,128)S(1)}) custom-call(bf16[512,256]{1,0:T(8,128)(2,1)S(1)} %get-tuple-element.253.refs_0_.sent, bf16[528,256]{1,0:T(8,128)(2,1)S(1)} %fusion.1.carrier.sent, ...), custom_call_target="tpu_custom_call" | custom-call | flops 1 | bytes 1 | tf_op jit(solution)/shard_map/pallas_call | solution.py:563
  40.7 1.3 %collective-permute-done.6 = bf16[160,256]{1,0:T(8,128)(2,1)S(1)} collective-permute-done((bf16[160,256]{1,0:T(8,128)(2,1)S(1)}, bf16[160,256]{1,0:T(8,128)(2,1)S(1)}, u32[]{:S(2)}, u32[]{:S(2)}) %collective-permute-start.6) | collective-permute-done | bytes 81952 | tf_op jit(solution)/shard_map/ppermute | solution.py:586
  42.0 1.7 %collective-permute-start.7 = (bf16[160,256]{1,0:T(8,128)(2,1)S(1)}, bf16[160,256]{1,0:T(8,128)(2,1)S(1)}, u32[]{:S(2)}, u32[]{:S(2)}) collective-permute-start(bf16[160,256]{1,0:T(8,128)(2,1)S(1)} %add_convert_fusion.2), channel_id=1, source_target_pairs={{0,8},{8,0},{16,24},{24,16},{1,9},{9,1},{17,25},{25,17},{2,10},{10... | collective-permute-start | bytes 245768 | tf_op jit(solution)/shard_map/ppermute | solution.py:586
  43.7 1.1 %collective-permute-start.9 = (bf16[512,256]{1,0:T(8,128)(2,1)S(1)}, bf16[512,256]{1,0:T(8,128)(2,1)S(1)}, u32[]{:S(2)}, u32[]{:S(2)}) collective-permute-start(bf16[512,256]{1,0:T(8,128)(2,1)S(1)} %get-tuple-element.215), channel_id=1, source_target_pairs={{0,1},{1,0},{2,3},{3,2},{4,5},{5,4},{6,7},{7,6},{8,9},{9,8},{10,11... | collective-permute-start | bytes 786440 | tf_op jit(solution)/shard_map/ppermute | solution.py:578
  44.7 3.8 %shard_map.346 = (f32[512,256]{1,0:T(8,128)S(1)}, bf16[448,256]{1,0:T(8,128)(2,1)S(1)}, bf16[448,256]{1,0:T(8,128)(2,1)S(1)}) custom-call(bf16[528,256]{1,0:T(8,128)(2,1)S(1)} %fusion.1.carrier.sent, bf16[528,256]{1,0:T(8,128)(2,1)S(1)} %fusion.1.carrier.sent, bf16[512,512]{1,0:T(8,128)(2,1)S(1)} %get-tuple-element.154.q, ...), custom_call_target="tpu_custom_call" | custom-call | flops 1 | bytes 1 | tf_op jit(solution)/shard_map/pallas_call | solution.py:563
  48.5 0.1 collective-permute-start.8
  48.6 2.7 %collective-permute-start.13 = (bf16[160,256]{1,0:T(8,128)(2,1)S(1)}, bf16[160,256]{1,0:T(8,128)(2,1)S(1)}, u32[]{:S(2)}, u32[]{:S(2)}) collective-permute-start(bf16[160,256]{1,0:T(8,128)(2,1)S(1)} %add_convert_fusion.1), channel_id=1, source_target_pairs={{0,16},{8,24},{16,0},{24,8},{1,17},{9,25},{17,1},{25,9},{2,18},{10... | collective-permute-start | bytes 245768 | tf_op jit(solution)/shard_map/ppermute | solution.py:586
  51.4 1.0 %collective-permute-start.10 = (bf16[112,256]{1,0:T(8,128)(2,1)S(1)}, bf16[112,256]{1,0:T(8,128)(2,1)S(1)}, u32[]{:S(2)}, u32[]{:S(2)}) collective-permute-start(bf16[112,256]{1,0:T(8,128)(2,1)S(1)} %get-tuple-element.217), channel_id=1, source_target_pairs={{0,1},{1,0},{4,5},{5,4},{2,3},{3,2},{6,7},{7,6},{8,9},{9,8},{12,13... | collective-permute-start | bytes 172040 | tf_op jit(solution)/shard_map/ppermute | solution.py:586
  52.4 1.5 %collective-permute-start.11 = (bf16[112,256]{1,0:T(8,128)(2,1)S(1)}, bf16[112,256]{1,0:T(8,128)(2,1)S(1)}, u32[]{:S(2)}, u32[]{:S(2)}) collective-permute-start(bf16[112,256]{1,0:T(8,128)(2,1)S(1)} %get-tuple-element.218), channel_id=1, source_target_pairs={{0,4},{1,5},{4,0},{5,1},{2,6},{3,7},{6,2},{7,3},{8,12},{9,13},{12,... | collective-permute-start | bytes 172040 | tf_op jit(solution)/shard_map/ppermute | solution.py:586
  53.9 1.0 %collective-permute-start.12 = (bf16[112,256]{1,0:T(8,128)(2,1)S(1)}, bf16[112,256]{1,0:T(8,128)(2,1)S(1)}, u32[]{:S(2)}, u32[]{:S(2)}) collective-permute-start(bf16[112,256]{1,0:T(8,128)(2,1)S(1)} %get-tuple-element.219), channel_id=1, source_target_pairs={{0,5},{1,4},{4,1},{5,0},{2,7},{3,6},{6,3},{7,2},{8,13},{9,12},{12,... | collective-permute-start | bytes 172040 | tf_op jit(solution)/shard_map/ppermute | solution.py:586
  54.9 1.2 %collective-permute-done.13 = bf16[160,256]{1,0:T(8,128)(2,1)S(1)} collective-permute-done((bf16[160,256]{1,0:T(8,128)(2,1)S(1)}, bf16[160,256]{1,0:T(8,128)(2,1)S(1)}, u32[]{:S(2)}, u32[]{:S(2)}) %collective-permute-start.13) | collective-permute-done | bytes 81952 | tf_op jit(solution)/shard_map/ppermute | solution.py:586
  56.1 0.8 collective-permute-done.11
  56.8 2.1 %collective-permute-done.12 = bf16[112,256]{1,0:T(8,128)(2,1)S(1)} collective-permute-done((bf16[112,256]{1,0:T(8,128)(2,1)S(1)}, bf16[112,256]{1,0:T(8,128)(2,1)S(1)}, u32[]{:S(2)}, u32[]{:S(2)}) %collective-permute-start.12) | collective-permute-done | bytes 57376 | tf_op jit(solution)/shard_map/ppermute | solution.py:586
  59.0 2.0 %collective-permute-start.16 = (bf16[112,256]{1,0:T(8,128)(2,1)S(1)}, bf16[112,256]{1,0:T(8,128)(2,1)S(1)}, u32[]{:S(2)}, u32[]{:S(2)}) collective-permute-start(bf16[112,256]{1,0:T(8,128)(2,1)S(1)} %add_convert_fusion.4), channel_id=1, source_target_pairs={{0,24},{8,16},{16,8},{24,0},{1,25},{9,17},{17,9},{25,1},{2,26},{10... | collective-permute-start | bytes 172040 | tf_op jit(solution)/shard_map/ppermute | solution.py:586
  61.0 0.2 collective-permute-start.15
  61.2 2.2 %collective-permute-start.14 = (bf16[112,256]{1,0:T(8,128)(2,1)S(1)}, bf16[112,256]{1,0:T(8,128)(2,1)S(1)}, u32[]{:S(2)}, u32[]{:S(2)}) collective-permute-start(bf16[112,256]{1,0:T(8,128)(2,1)S(1)} %add_convert_fusion.4), channel_id=1, source_target_pairs={{0,8},{8,0},{16,24},{24,16},{1,9},{9,1},{17,25},{25,17},{2,10},{10... | collective-permute-start | bytes 172040 | tf_op jit(solution)/shard_map/ppermute | solution.py:586
  63.5 1.6 %collective-permute-done.16 = bf16[112,256]{1,0:T(8,128)(2,1)S(1)} collective-permute-done((bf16[112,256]{1,0:T(8,128)(2,1)S(1)}, bf16[112,256]{1,0:T(8,128)(2,1)S(1)}, u32[]{:S(2)}, u32[]{:S(2)}) %collective-permute-start.16) | collective-permute-done | bytes 57376 | tf_op jit(solution)/shard_map/ppermute | solution.py:586
  65.1 1.6 %collective-permute-done.15 = bf16[112,256]{1,0:T(8,128)(2,1)S(1)} collective-permute-done((bf16[112,256]{1,0:T(8,128)(2,1)S(1)}, bf16[112,256]{1,0:T(8,128)(2,1)S(1)}, u32[]{:S(2)}, u32[]{:S(2)}) %collective-permute-start.15) | collective-permute-done | bytes 57376 | tf_op jit(solution)/shard_map/ppermute | solution.py:586
  66.8 1.3 %collective-permute-start.17 = (bf16[272,256]{1,0:T(8,128)(2,1)S(1)}, bf16[272,256]{1,0:T(8,128)(2,1)S(1)}, u32[]{:S(2)}, u32[]{:S(2)}) collective-permute-start(bf16[272,256]{1,0:T(8,128)(2,1)S(1)} %pad_maximum_fusion.1.refs_0_), channel_id=1, source_target_pairs={{0,1},{1,0},{4,5},{5,4},{2,3},{3,2},{6,7},{7,6},{8,9},{9,8},{12,13... | collective-permute-start | bytes 417800 | tf_op jit(solution)/shard_map/ppermute | solution.py:586
  68.1 0.7 collective-permute-start.19
  68.8 1.5 %collective-permute-start.18 = (bf16[272,256]{1,0:T(8,128)(2,1)S(1)}, bf16[272,256]{1,0:T(8,128)(2,1)S(1)}, u32[]{:S(2)}, u32[]{:S(2)}) collective-permute-start(bf16[272,256]{1,0:T(8,128)(2,1)S(1)} %pad_maximum_fusion.1.refs_0_), channel_id=1, source_target_pairs={{0,4},{1,5},{4,0},{5,1},{2,6},{3,7},{6,2},{7,3},{8,12},{9,13},{12,... | collective-permute-start | bytes 417800 | tf_op jit(solution)/shard_map/ppermute | solution.py:586
  70.3 1.0 %pad_maximum_fusion = f32[2,512,256]{2,1,0:T(8,128)} fusion(f32[1,512,256]{2,1,0:T(8,128)S(1)} %bitcast.33, f32[1,512,256]{2,1,0:T(8,128)S(1)} %bitcast.32), kind=kLoop, calls=%fused_computation | loop fusion | flops 262144 | bytes 2097152 | tf_op jit(solution)/shard_map/stack | solution.py:837
  71.4 1.4 %shard_map.348 = f32[2,512,256]{2,1,0:T(8,128)} custom-call(bf16[528,256]{1,0:T(8,128)(2,1)S(1)} %fusion.1.carrier.sent, f32[512,256]{1,0:T(8,128)S(1)} %get-tuple-element.225.refs_0_, f32[512,256]{1,0:T(8,128)S(1)} %get-tuple-element.226.refs_1_, bf16[512,256]{1,0:T(8,128)(2,1)S(1)} %collective-permute-done.2.refs_2_, ...), custom_call_target="tpu_custom_call" | custom-call | bytes 2891776 | tf_op jit(solution)/shard_map/pallas_call | solution.py:563
  72.7 1.3 %collective-permute-done.19.refs_3_ = bf16[272,256]{1,0:T(8,128)(2,1)S(1)} collective-permute-done((bf16[272,256]{1,0:T(8,128)(2,1)S(1)}, bf16[272,256]{1,0:T(8,128)(2,1)S(1)}, u32[]{:S(2)}, u32[]{:S(2)}) %collective-permute-start.19) | collective-permute-done | bytes 139296 | tf_op jit(solution)/shard_map/ppermute | solution.py:586
  74.0 0.8 %collective-permute-done.18.refs_2_ = bf16[272,256]{1,0:T(8,128)(2,1)S(1)} collective-permute-done((bf16[272,256]{1,0:T(8,128)(2,1)S(1)}, bf16[272,256]{1,0:T(8,128)(2,1)S(1)}, u32[]{:S(2)}, u32[]{:S(2)}) %collective-permute-start.18) | collective-permute-done | bytes 139296 | tf_op jit(solution)/shard_map/ppermute | solution.py:586
  74.8 0.5 collective-permute-start.21
  75.4 0.8 %collective-permute-done.22.refs_6_ = bf16[272,256]{1,0:T(8,128)(2,1)S(1)} collective-permute-done((bf16[272,256]{1,0:T(8,128)(2,1)S(1)}, bf16[272,256]{1,0:T(8,128)(2,1)S(1)}, u32[]{:S(2)}, u32[]{:S(2)}) %collective-permute-start.22) | collective-permute-done | bytes 139296 | tf_op jit(solution)/shard_map/ppermute | solution.py:586
  76.2 0.2 collective-permute-done.21.refs_5_
  76.4 1.7 %shard_map.349 = (f32[256,256]{1,0:T(8,128)}, f32[256,512]{1,0:T(8,128)}, f32[512,256]{1,0:T(8,128)}, f32[256,256]{1,0:T(8,128)}, f32[256,256]{1,0:T(8,128)}, /*...) custom-call(bf16[272,256]{1,0:T(8,128)(2,1)S(1)} %pad_maximum_fusion, ...), custom_call_target="tpu_custom_call" | custom-call | bytes 3222540 | tf_op jit(solution)/shard_map/pallas_call | solution.py:563
  (60 shorter events, 0.6 us)
Async XLA Ops:
  0.7 5.4 %copy-start.17 = (s32[2,512]{1,0:T(2,128)S(1)}, s32[2,512]{1,0:T(2,128)}, u32[]{:S(2)}) copy-start(s32[2,512]{1,0:T(2,128)} %param.21) | copy-start | bytes 12292
  0.7 5.4 %copy-start.15 = (s32[2]{0:T(128)S(1)}, s32[2]{0:T(128)}, u32[]{:S(2)}) copy-start(s32[2]{0:T(128)} %lengths.5) | copy-start | bytes 28
  0.7 5.4 %copy-start.1 = (f32[512,256]{1,0:T(8,128)S(1)}, f32[512,256]{1,0:T(8,128)}, u32[]{:S(2)}) copy-start(f32[512,256]{1,0:T(8,128)} %refs_9_.1) | copy-start | bytes 1572868
  0.7 5.4 %copy-start = (f32[256,512]{1,0:T(8,128)S(1)}, f32[256,512]{1,0:T(8,128)}, u32[]{:S(2)}) copy-start(f32[256,512]{1,0:T(8,128)} %refs_8_.1) | copy-start | bytes 1572868
  0.7 5.4 %copy-start.8 = (f32[256]{0:T(256)S(1)}, f32[256]{0:T(256)}, u32[]{:S(2)}) copy-start(f32[256]{0:T(256)} %param.29) | copy-start | bytes 3076
  0.7 5.4 %copy-start.4 = (f32[256,256]{1,0:T(8,128)S(1)}, f32[256,256]{1,0:T(8,128)}, u32[]{:S(2)}) copy-start(f32[256,256]{1,0:T(8,128)} %refs_4_.1) | copy-start | bytes 786436
  0.7 5.4 %copy-start.3 = (f32[256,256]{1,0:T(8,128)S(1)}, f32[256,256]{1,0:T(8,128)}, u32[]{:S(2)}) copy-start(f32[256,256]{1,0:T(8,128)} %refs_3_.1) | copy-start | bytes 786436
  0.7 5.4 %copy-start.7 = (f32[256]{0:T(256)S(1)}, f32[256]{0:T(256)}, u32[]{:S(2)}) copy-start(f32[256]{0:T(256)} %param.26) | copy-start | bytes 3076
  0.7 5.4 %copy-start.2 = (f32[256,256]{1,0:T(8,128)S(1)}, f32[256,256]{1,0:T(8,128)}, u32[]{:S(2)}) copy-start(f32[256,256]{1,0:T(8,128)} %refs_2_.1) | copy-start | bytes 786436
  3.0 9.4 %collective-permute-start.1 = (bf16[512,256]{1,0:T(8,128)(2,1)S(1)}, bf16[512,256]{1,0:T(8,128)(2,1)}, u32[]{:S(2)}, u32[]{:S(2)}) collective-permute-start(bf16[512,256]{1,0:T(8,128)(2,1)S(1)} %get-tuple-element.253.refs_0_.sent), channel_id=1, source_target_pairs={{0,1},{1,0},{2,3},{3,2},{4,5},{5,4},{6,7},{7,6},{8,9},{9,8},{10,11... | collective-permute-start | bytes 786440 | tf_op jit(solution)/shard_map/ppermute | solution.py:578
  6.2 1.0 %copy-start.5 = (f32[256,256]{1,0:T(8,128)S(1)}, f32[256,256]{1,0:T(8,128)}, u32[]{:S(2)}) copy-start(f32[256,256]{1,0:T(8,128)} %refs_7_.1) | copy-start | bytes 786436
  7.1 4.9 %copy-start.16 = (f32[2,512,256]{2,1,0:T(8,128)S(1)}, f32[2,512,256]{2,1,0:T(8,128)}, u32[]{:S(2)}) copy-start(f32[2,512,256]{2,1,0:T(8,128)} %param.23) | copy-start | bytes 3145732
  11.9 0.7 copy-start.6
  11.9 0.7 copy-start.9
  11.9 0.7 copy-start.10
  11.9 0.7 copy-start.11
  11.9 0.7 copy-start.12
  11.9 0.7 copy-start.13
  11.9 0.7 copy-start.14
  11.9 8.0 %collective-permute-start = (bf16[528,256]{1,0:T(8,128)(2,1)S(1)}, bf16[528,256]{1,0:T(8,128)(2,1)S(1)}, u32[]{:S(2)}, u32[]{:S(2)}) collective-permute-start(bf16[528,256]{1,0:T(8,128)(2,1)S(1)} %fusion.1.carrier.sent), channel_id=1, source_target_pairs={{0,1},{1,0},{2,3},{3,2},{4,5},{5,4},{6,7},{7,6},{8,9},{9,8},{10,11... | collective-permute-start | bytes 811016 | tf_op jit(solution)/shard_map/ppermute | solution.py:578
  23.6 8.0 %collective-permute-start.2 = (bf16[512,256]{1,0:T(8,128)(2,1)S(1)}, bf16[512,256]{1,0:T(8,128)(2,1)S(1)}, u32[]{:S(2)}, u32[]{:S(2)}) collective-permute-start(bf16[512,256]{1,0:T(8,128)(2,1)S(1)} %get-tuple-element.153), channel_id=1, source_target_pairs={{0,1},{1,0},{2,3},{3,2},{4,5},{5,4},{6,7},{7,6},{8,9},{9,8},{10,11... | collective-permute-start | bytes 786440 | tf_op jit(solution)/shard_map/ppermute | solution.py:578
  31.4 2.6 %collective-permute-start.3 = (bf16[640,256]{1,0:T(8,128)(2,1)S(1)}, bf16[640,256]{1,0:T(8,128)(2,1)S(1)}, u32[]{:S(2)}, u32[]{:S(2)}) collective-permute-start(bf16[640,256]{1,0:T(8,128)(2,1)S(1)} %get-tuple-element.173), channel_id=1, source_target_pairs={{0,2},{2,0},{1,3},{3,1},{4,6},{6,4},{5,7},{7,5},{8,10},{10,8},{9,1... | collective-permute-start | bytes 983048 | tf_op jit(solution)/shard_map/ppermute | solution.py:586
  34.1 6.6 %collective-permute-start.4 = (bf16[160,256]{1,0:T(8,128)(2,1)S(1)}, bf16[160,256]{1,0:T(8,128)(2,1)S(1)}, u32[]{:S(2)}, u32[]{:S(2)}) collective-permute-start(bf16[160,256]{1,0:T(8,128)(2,1)S(1)} %get-tuple-element.192), channel_id=1, source_target_pairs={{0,1},{1,0},{4,5},{5,4},{2,3},{3,2},{6,7},{7,6},{8,9},{9,8},{12,13... | collective-permute-start | bytes 245768 | tf_op jit(solution)/shard_map/ppermute | solution.py:586
  35.0 5.7 %collective-permute-start.5 = (bf16[160,256]{1,0:T(8,128)(2,1)S(1)}, bf16[160,256]{1,0:T(8,128)(2,1)S(1)}, u32[]{:S(2)}, u32[]{:S(2)}) collective-permute-start(bf16[160,256]{1,0:T(8,128)(2,1)S(1)} %get-tuple-element.193), channel_id=1, source_target_pairs={{0,4},{1,5},{4,0},{5,1},{2,6},{3,7},{6,2},{7,3},{8,12},{9,13},{12,... | collective-permute-start | bytes 245768 | tf_op jit(solution)/shard_map/ppermute | solution.py:586
  36.5 5.5 %collective-permute-start.6 = (bf16[160,256]{1,0:T(8,128)(2,1)S(1)}, bf16[160,256]{1,0:T(8,128)(2,1)S(1)}, u32[]{:S(2)}, u32[]{:S(2)}) collective-permute-start(bf16[160,256]{1,0:T(8,128)(2,1)S(1)} %get-tuple-element.194), channel_id=1, source_target_pairs={{0,5},{1,4},{4,1},{5,0},{2,7},{3,6},{6,3},{7,2},{8,13},{9,12},{12,... | collective-permute-start | bytes 245768 | tf_op jit(solution)/shard_map/ppermute | solution.py:586
  42.0 6.5 %collective-permute-start.7 = (bf16[160,256]{1,0:T(8,128)(2,1)S(1)}, bf16[160,256]{1,0:T(8,128)(2,1)S(1)}, u32[]{:S(2)}, u32[]{:S(2)}) collective-permute-start(bf16[160,256]{1,0:T(8,128)(2,1)S(1)} %add_convert_fusion.2), channel_id=1, source_target_pairs={{0,8},{8,0},{16,24},{24,16},{1,9},{9,1},{17,25},{25,17},{2,10},{10... | collective-permute-start | bytes 245768 | tf_op jit(solution)/shard_map/ppermute | solution.py:586
  43.7 7.6 %collective-permute-start.9 = (bf16[512,256]{1,0:T(8,128)(2,1)S(1)}, bf16[512,256]{1,0:T(8,128)(2,1)S(1)}, u32[]{:S(2)}, u32[]{:S(2)}) collective-permute-start(bf16[512,256]{1,0:T(8,128)(2,1)S(1)} %get-tuple-element.215), channel_id=1, source_target_pairs={{0,1},{1,0},{2,3},{3,2},{4,5},{5,4},{6,7},{7,6},{8,9},{9,8},{10,11... | collective-permute-start | bytes 786440 | tf_op jit(solution)/shard_map/ppermute | solution.py:578
  48.5 2.8 %collective-permute-start.8 = (bf16[448,256]{1,0:T(8,128)(2,1)S(1)}, bf16[448,256]{1,0:T(8,128)(2,1)S(1)}, u32[]{:S(2)}, u32[]{:S(2)}) collective-permute-start(bf16[448,256]{1,0:T(8,128)(2,1)S(1)} %get-tuple-element.213), channel_id=1, source_target_pairs={{0,2},{2,0},{1,3},{3,1},{4,6},{6,4},{5,7},{7,5},{8,10},{10,8},{9,1... | collective-permute-start | bytes 688136 | tf_op jit(solution)/shard_map/ppermute | solution.py:586
  48.6 7.4 %collective-permute-start.13 = (bf16[160,256]{1,0:T(8,128)(2,1)S(1)}, bf16[160,256]{1,0:T(8,128)(2,1)S(1)}, u32[]{:S(2)}, u32[]{:S(2)}) collective-permute-start(bf16[160,256]{1,0:T(8,128)(2,1)S(1)} %add_convert_fusion.1), channel_id=1, source_target_pairs={{0,16},{8,24},{16,0},{24,8},{1,17},{9,25},{17,1},{25,9},{2,18},{10... | collective-permute-start | bytes 245768 | tf_op jit(solution)/shard_map/ppermute | solution.py:586
  51.4 4.7 %collective-permute-start.10 = (bf16[112,256]{1,0:T(8,128)(2,1)S(1)}, bf16[112,256]{1,0:T(8,128)(2,1)S(1)}, u32[]{:S(2)}, u32[]{:S(2)}) collective-permute-start(bf16[112,256]{1,0:T(8,128)(2,1)S(1)} %get-tuple-element.217), channel_id=1, source_target_pairs={{0,1},{1,0},{4,5},{5,4},{2,3},{3,2},{6,7},{7,6},{8,9},{9,8},{12,13... | collective-permute-start | bytes 172040 | tf_op jit(solution)/shard_map/ppermute | solution.py:586
  52.4 4.5 %collective-permute-start.11 = (bf16[112,256]{1,0:T(8,128)(2,1)S(1)}, bf16[112,256]{1,0:T(8,128)(2,1)S(1)}, u32[]{:S(2)}, u32[]{:S(2)}) collective-permute-start(bf16[112,256]{1,0:T(8,128)(2,1)S(1)} %get-tuple-element.218), channel_id=1, source_target_pairs={{0,4},{1,5},{4,0},{5,1},{2,6},{3,7},{6,2},{7,3},{8,12},{9,13},{12,... | collective-permute-start | bytes 172040 | tf_op jit(solution)/shard_map/ppermute | solution.py:586
  53.9 5.1 %collective-permute-start.12 = (bf16[112,256]{1,0:T(8,128)(2,1)S(1)}, bf16[112,256]{1,0:T(8,128)(2,1)S(1)}, u32[]{:S(2)}, u32[]{:S(2)}) collective-permute-start(bf16[112,256]{1,0:T(8,128)(2,1)S(1)} %get-tuple-element.219), channel_id=1, source_target_pairs={{0,5},{1,4},{4,1},{5,0},{2,7},{3,6},{6,3},{7,2},{8,13},{9,12},{12,... | collective-permute-start | bytes 172040 | tf_op jit(solution)/shard_map/ppermute | solution.py:586
  59.0 6.1 %collective-permute-start.16 = (bf16[112,256]{1,0:T(8,128)(2,1)S(1)}, bf16[112,256]{1,0:T(8,128)(2,1)S(1)}, u32[]{:S(2)}, u32[]{:S(2)}) collective-permute-start(bf16[112,256]{1,0:T(8,128)(2,1)S(1)} %add_convert_fusion.4), channel_id=1, source_target_pairs={{0,24},{8,16},{16,8},{24,0},{1,25},{9,17},{17,9},{25,1},{2,26},{10... | collective-permute-start | bytes 172040 | tf_op jit(solution)/shard_map/ppermute | solution.py:586
  61.0 5.7 %collective-permute-start.15 = (bf16[112,256]{1,0:T(8,128)(2,1)S(1)}, bf16[112,256]{1,0:T(8,128)(2,1)S(1)}, u32[]{:S(2)}, u32[]{:S(2)}) collective-permute-start(bf16[112,256]{1,0:T(8,128)(2,1)S(1)} %add_convert_fusion.4), channel_id=1, source_target_pairs={{0,16},{8,24},{16,0},{24,8},{1,17},{9,25},{17,1},{25,9},{2,18},{10... | collective-permute-start | bytes 172040 | tf_op jit(solution)/shard_map/ppermute | solution.py:586
  61.2 5.5 %collective-permute-start.14 = (bf16[112,256]{1,0:T(8,128)(2,1)S(1)}, bf16[112,256]{1,0:T(8,128)(2,1)S(1)}, u32[]{:S(2)}, u32[]{:S(2)}) collective-permute-start(bf16[112,256]{1,0:T(8,128)(2,1)S(1)} %add_convert_fusion.4), channel_id=1, source_target_pairs={{0,8},{8,0},{16,24},{24,16},{1,9},{9,1},{17,25},{25,17},{2,10},{10... | collective-permute-start | bytes 172040 | tf_op jit(solution)/shard_map/ppermute | solution.py:586
  66.8 6.0 %collective-permute-start.17 = (bf16[272,256]{1,0:T(8,128)(2,1)S(1)}, bf16[272,256]{1,0:T(8,128)(2,1)S(1)}, u32[]{:S(2)}, u32[]{:S(2)}) collective-permute-start(bf16[272,256]{1,0:T(8,128)(2,1)S(1)} %pad_maximum_fusion.1.refs_0_), channel_id=1, source_target_pairs={{0,1},{1,0},{4,5},{5,4},{2,3},{3,2},{6,7},{7,6},{8,9},{9,8},{12,13... | collective-permute-start | bytes 417800 | tf_op jit(solution)/shard_map/ppermute | solution.py:586
  68.1 6.0 %collective-permute-start.19 = (bf16[272,256]{1,0:T(8,128)(2,1)S(1)}, bf16[272,256]{1,0:T(8,128)(2,1)S(1)}, u32[]{:S(2)}, u32[]{:S(2)}) collective-permute-start(bf16[272,256]{1,0:T(8,128)(2,1)S(1)} %pad_maximum_fusion.1.refs_0_), channel_id=1, source_target_pairs={{0,5},{1,4},{4,1},{5,0},{2,7},{3,6},{6,3},{7,2},{8,13},{9,12},{12,... | collective-permute-start | bytes 417800 | tf_op jit(solution)/shard_map/ppermute | solution.py:586
  68.8 6.0 %collective-permute-start.18 = (bf16[272,256]{1,0:T(8,128)(2,1)S(1)}, bf16[272,256]{1,0:T(8,128)(2,1)S(1)}, u32[]{:S(2)}, u32[]{:S(2)}) collective-permute-start(bf16[272,256]{1,0:T(8,128)(2,1)S(1)} %pad_maximum_fusion.1.refs_0_), channel_id=1, source_target_pairs={{0,4},{1,5},{4,0},{5,1},{2,6},{3,7},{6,2},{7,3},{8,12},{9,13},{12,... | collective-permute-start | bytes 417800 | tf_op jit(solution)/shard_map/ppermute | solution.py:586
  72.7 2.6 %collective-permute-start.20 = (bf16[272,256]{1,0:T(8,128)(2,1)S(1)}, bf16[272,256]{1,0:T(8,128)(2,1)S(1)}, u32[]{:S(2)}, u32[]{:S(2)}) collective-permute-start(bf16[272,256]{1,0:T(8,128)(2,1)S(1)} %pad_maximum_fusion.1.refs_0_), channel_id=1, source_target_pairs={{0,2},{2,0},{1,3},{3,1},{4,6},{6,4},{5,7},{7,5},{8,10},{10,8},{9,1... | collective-permute-start | bytes 417800 | tf_op jit(solution)/shard_map/ppermute | solution.py:586
  74.0 1.4 %collective-permute-start.23 = (bf16[272,256]{1,0:T(8,128)(2,1)S(1)}, bf16[272,256]{1,0:T(8,128)(2,1)S(1)}, u32[]{:S(2)}, u32[]{:S(2)}) collective-permute-start(bf16[272,256]{1,0:T(8,128)(2,1)S(1)} %collective-permute-done.19.refs_3_), channel_id=1, source_target_pairs={{0,2},{2,0},{1,3},{3,1},{4,6},{6,4},{5,7},{7,5},{8,10},{10,8},{9,1... | collective-permute-start | bytes 417800 | tf_op jit(solution)/shard_map/ppermute | solution.py:586
  74.8 1.4 %collective-permute-start.22 = (bf16[272,256]{1,0:T(8,128)(2,1)S(1)}, bf16[272,256]{1,0:T(8,128)(2,1)S(1)}, u32[]{:S(2)}, u32[]{:S(2)}) collective-permute-start(bf16[272,256]{1,0:T(8,128)(2,1)S(1)} %collective-permute-done.18.refs_2_), channel_id=1, source_target_pairs={{0,2},{2,0},{1,3},{3,1},{4,6},{6,4},{5,7},{7,5},{8,10},{10,8},{9,1... | collective-permute-start | bytes 417800 | tf_op jit(solution)/shard_map/ppermute | solution.py:586
  74.8 1.6 %collective-permute-start.21 = (bf16[272,256]{1,0:T(8,128)(2,1)S(1)}, bf16[272,256]{1,0:T(8,128)(2,1)S(1)}, u32[]{:S(2)}, u32[]{:S(2)}) collective-permute-start(bf16[272,256]{1,0:T(8,128)(2,1)S(1)} %collective-permute-done.17.refs_1_), channel_id=1, source_target_pairs={{0,2},{2,0},{1,3},{3,1},{4,6},{6,4},{5,7},{7,5},{8,10},{10,8},{9,1... | collective-permute-start | bytes 417800 | tf_op jit(solution)/shard_map/ppermute | solution.py:586

commit v2 on v1

--- a/solution.py
+++ b/solution.py
@@ -97,6 +97,40 @@
     return lax.rem(lax.axis_index("seq") - distance + ring, ring)
 
 
+def select_kernel(
+    cell, carry, tokens, masks, embed, stream_out, low_out, *refs
+):
+    held, mask_held, embed_held, arrived = refs[-4:]
+    copies = [
+        pltpu.make_async_copy(source, target, arrived.at[which])
+        for which, (source, target) in enumerate(
+            ((tokens.at[cell], held), (masks, mask_held), (embed, embed_held))
+        )
+    ]
+    for copy in copies:
+        copy.start()
+    for copy in copies[1:]:
+        copy.wait()
+    rows, width = held.shape
+    mask = mask_held[cell : cell + 1, :].astype(F32)
+    column = jnp.transpose(jnp.broadcast_to(mask, (8, rows)))[:, :1]
+    copies[0].wait()
+    stream = jnp.where(column == 1.0, embed_held[...], held[...])
+    stream_out[...] = stream
+    low_out[...] = stream.astype(BF)
+    if not carry:
+        return
+    carrier_out = refs[0]
+    pieces = [
+        mask_held[which : which + 1, at : at + width]
+        for which in range(masks.shape[0])
+        for at in range(0, rows, width)
+    ]
+    pieces.append(jnp.zeros((MASK_ROWS - len(pieces), width), masks.dtype))
+    carrier_out[:rows, :] = stream.astype(BF)
+    carrier_out[rows:, :] = jnp.concatenate(pieces, axis=0).astype(F32).astype(BF)
+
+
 def mask_of(carrier, cell):
     rows = carrier.shape[0] - MASK_ROWS
     count = rows // carrier.shape[1]
@@ -107,8 +141,8 @@
 
 def first_kernel(cells, lengths, *refs):
     xs, refs = refs[:cells], refs[cells:]
-    wq, wk, wv, bias_q, bias_v, wo, w1, w2 = refs[:8]
-    outs, (w_all, w_kv, wo_out, w1_out, w2_out) = refs[8:-5], refs[-5:]
+    wq, wk, wv, bias_q, bias_v = refs[:5]
+    outs, (w_all, w_kv) = refs[5:-2], refs[-2:]
     w_all[:, :WIDE] = spread(wq[...] * HEAD_DIM ** (-0.5)).astype(BF)
     w_all[:, WIDE : 2 * WIDE] = spread(wk[...]).astype(BF)
     w_all[:, 2 * WIDE :] = spread(wv[...]).astype(BF)
@@ -129,9 +163,6 @@
     width = wk.shape[1]
     w_kv[:, :width] = wk[...].astype(BF)
     w_kv[:, width:] = wv[...].astype(BF)
-    wo_out[...] = spread_rows(wo[...].astype(BF))
-    w1_out[...] = w1[...].astype(BF)
-    w2_out[...] = w2[...].astype(BF)
 
 
 def more_kernel(
@@ -256,8 +287,8 @@
 
 def middle_kernel(
     cell, ring, carry, finish,
-    lengths, x, q, state, peak, stream, cotangent, w_all, bias_v, wo, bias_o, gain_one, shift_one,
-    w1, bias_1, w2, bias_2, gain_two, shift_two, *refs,
+    lengths, x, q, state, peak, stream, cotangent, w_all, bias_v, wo_in, bias_o, gain_one,
+    shift_one, w1_in, bias_1, w2_in, bias_2, gain_two, shift_two, *refs,
 ):
     count = ring - 1 if ring > 2 else 0
     before, refs = refs[:count], refs[count:]
@@ -265,8 +296,16 @@
         dwo_in, dw1_in, dw2_in, vec_in = refs[:4]
         refs = refs[4:]
     do_outs, refs = refs[:ring], refs[ring:]
-    result_out, k_out, v_out, kept_out, first_out, vec_out = refs[:6]
-    refs = refs[6:]
+    result_out, k_out, v_out, kept_out, x_out, first_out, vec_out = refs[:7]
+    refs = refs[7:]
+    if carry:
+        wo, w1, w2 = wo_in, w1_in, w2_in
+    else:
+        wo, w1, w2 = refs[:3]
+        refs = refs[3:]
+        wo[...] = spread_rows(wo_in[...].astype(BF))
+        w1[...] = w1_in[...].astype(BF)
+        w2[...] = w2_in[...].astype(BF)
     if finish:
         keep_out, give_out = refs[:2]
         refs = refs[2:]
@@ -276,9 +315,10 @@
     scales, refs = refs[:ring], refs[ring:]
     (
         attended_wide, attended_low, normed_low, active_low, hidden_low, branch_low, attn_low,
-        unit_one, inverse_one, narrow_b, wide_b, acc, acc_wide, *pack_ref,
+        unit_one, inverse_one, narrow_b, wide_b, acc, *pack_ref,
     ) = refs
     rows, width = stream.shape
+    x_out[...] = x[:rows, :]
     hidden = w1.shape[1]
     length = lengths[cell]
     first_place = owner_of(ring - 1, ring) * rows
@@ -292,7 +332,7 @@
         old_scale, own_scale = jnp.exp(peak[:, cols] - top), jnp.exp(own - top)
         both = state[:, cols] * old_scale + total * own_scale
         inverse = inverse_of(both[:, HEAD_DIM : HEAD_DIM + 1])
-        attended = jnp.where(lane_of(both.shape) < HEAD_DIM, both * inverse, 0.0)
+        attended = both * inverse
         attended_wide[:, cols] = attended
         attended_low[:, cols] = attended.astype(BF)
         scales[ring - 1][:, cols] = own_scale * inverse
@@ -333,13 +373,10 @@
     branch_low[...] = branch_bf
     add(0, grad_result * unit)
     add(1, grad_result)
-    add(2, branch_bf.astype(F32))
     add(10, branch * branch * valid)
-    add(11, valid)
 
     hidden_bf = (nt(branch_low[...], w2[...]) * wide_b[...]).astype(BF)
     hidden_low[...] = hidden_bf
-    acc_wide[...] = eight_sum(hidden_bf.astype(F32))
 
     grad_normed = narrow_b[...] + nt(hidden_low[...], w1[...])
     unit = unit_one[...]
@@ -349,7 +386,6 @@
     attn_low[...] = attn_bf
     add(5, grad_normed * unit)
     add(6, grad_normed)
-    add(7, attn_bf.astype(F32))
 
     do_wide = nt(attn_low[...], wo[...]).astype(BF).astype(F32)
     for head in range(HEADS):
@@ -364,11 +400,17 @@
             scaled = jnp.where(lane == HEAD_DIM, dot, do_head * factor)
             do_out[:, cols] = jnp.where(lane == HEAD_DIM + 1, rest, scaled).astype(BF)
 
-    hidden_sum = jnp.sum(acc_wide[...], axis=0, keepdims=True)
+    ones = jnp.ones((8, rows), BF)
+    hidden_sum = nn(ones, hidden_low[...])[0:1]
+    known = {
+        2: nn(ones, branch_low[...])[0:1],
+        3: hidden_sum[:, :width],
+        4: hidden_sum[:, width:],
+        7: nn(ones, attn_low[...])[0:1],
+        11: jnp.full((1, width), jnp.clip(length - my_place, 0, rows).astype(F32)),
+    }
     sums = [
-        hidden_sum[:, (slot - 3) * width : (slot - 2) * width]
-        if slot in (3, 4)
-        else jnp.sum(acc[slot], axis=0, keepdims=True)
+        known[slot] if slot in known else jnp.sum(acc[slot], axis=0, keepdims=True)
         for slot in range(12)
     ]
     vec = jnp.concatenate(sums + [jnp.zeros((4, width), F32)], axis=0)
@@ -637,37 +679,59 @@
     weights = shape((HEADS * rows, rows), BF)
     score_flops = 2 * rows * rows * HEADS * 256
 
-    stream = [
-        jnp.where(masked[cell][:, None] == 1, mask_embed, tokens[cell]) for cell in range(cells)
-    ]
-    x_low = [part.astype(BF) for part in stream]
-    x_moved = [[part] for part in x_low]
-    x_moved[0] += [send(x_low[0], t, ring) for t in range(1, ring)]
-    under = masked.astype(BF).reshape(-1, width)
-    under = jnp.pad(under, ((0, MASK_ROWS - under.shape[0]), (0, 0)))
-    x_moved[-1] = [jnp.concatenate([x_low[-1], under], axis=0)]
+    stream, x_moved, x_low = [], [], []
+    vmem = pl.BlockSpec(memory_space=pltpu.VMEM)
+    masks = masked
+    for cell in range(cells):
+        carry = cell == cells - 1
+        outs = [full_narrow, low_narrow] + [shape((rows + MASK_ROWS, width), BF)] * carry
+        made = pl.pallas_call(
+            functools.partial(select_kernel, cell, carry),
+            in_specs=[pl.BlockSpec(memory_space=pltpu.HBM)] * 3,
+            out_specs=[vmem] * len(outs),
+            out_shape=outs,
+            scratch_shapes=[
+                pltpu.VMEM((rows, width), F32),
+                pltpu.VMEM((cells, rows), jnp.int32),
+                pltpu.VMEM((1, width), F32),
+                pltpu.SemaphoreType.DMA((3,)),
+            ],
+            compiler_params=pltpu.CompilerParams(vmem_limit_bytes=VMEM_LIMIT),
+        )(
+            *[
+                pltpu.with_memory_space_constraint(a, pltpu.HBM)
+                for a in (tokens, masks, row(mask_embed))
+            ]
+        )
+        stream.append(made[0])
+        x_low.append(made[1])
+        x_moved.append([made[-1]])
+        if cell == 0:
+            x_moved[0] += [send(x_moved[0][0], t, ring) for t in range(1, ring)]
+        masks, x_low[cell] = lax.optimization_barrier((masks, x_low[cell]))
 
     made = call(
         functools.partial(first_kernel, cells),
         [lengths]
         + x_low
-        + [query_weight, key_weight, value_weight, row(query_bias), row(value_bias)]
-        + [out_weight, expand_weight, reduce_weight],
+        + [query_weight, key_weight, value_weight, row(query_bias), row(value_bias)],
         [low_wide, low_wide, low_wide, weights, full_wide, full_wide] * cells
         + [
             shape((width, 3 * WIDE), BF),
             shape((width, 2 * width), BF),
-            shape((WIDE, width), BF),
-            shape((width, hidden), BF),
-            shape((hidden, width), BF),
         ],
         flops=2 * cells * score_flops,
     )
-    w_all, w_kv, wo, w1, w2 = made[-5:]
+    w_all, w_kv = made[-2:]
+    wo, w1, w2 = out_weight, expand_weight, reduce_weight
+    low_weights = [
+        shape((WIDE, width), BF), shape((width, hidden), BF), shape((hidden, width), BF)
+    ]
     bias_v = row(value_bias)
     for cell in range(1, cells):
         sent, w_all = lax.optimization_barrier((x_moved[cell][0], w_all))
         x_moved[cell] += [send(sent, t, ring) for t in range(1, ring)]
+    carriers = list(x_moved[-1])
     keys, values, kept, queries, states, peaks = [], [], [], [], [], []
     for cell in range(cells):
         q, k, v, p, state, peak = made[6 * cell : 6 * cell + 6]
@@ -700,7 +764,7 @@
         partial = []
         for t in range(1, ring):
             ins = [
-                x_moved[cell][t], x_moved[-1][t], queries[cell], grads_out[cell][t],
+                x_moved[cell][t], carriers[t], queries[cell], grads_out[cell][t],
                 keys[cell][t], values[cell][t], kept[cell][t], w_kv,
             ]
             ins += ([dq[cell]] if t > 1 else []) + carried_back
@@ -730,8 +794,8 @@
             states[cell], partial = lax.optimization_barrier((states[cell], partial))
             received.append(returned(partial))
         outs = [low_wide] * ring
-        outs += [full_narrow, low_wide, low_wide, weights, full_narrow]
-        outs += [shape((16, width), F32)]
+        outs += [full_narrow, low_wide, low_wide, weights, low_narrow, full_narrow]
+        outs += [shape((16, width), F32)] + (low_weights if cell == 0 else [])
         if finish:
             outs += [shape((one_rows // 2, width), BF)] * 2
         else:
@@ -749,7 +813,6 @@
             pltpu.VMEM((rows, width), F32),
             pltpu.VMEM((rows, hidden), F32),
             pltpu.VMEM((12, 8, width), F32),
-            pltpu.VMEM((8, hidden), F32),
         ]
         if finish:
             scratch.append(pltpu.VMEM((one_rows, width), BF))
@@ -767,14 +830,18 @@
             flops=7 * score_flops,
         )
         grads_out.append(made[:ring])
-        result, k, v, p, first, vec_mid = made[ring : ring + 6]
+        result, k, v, p, x_moved[cell][ring - 1], first, vec_mid = made[ring : ring + 7]
+        made = made[ring + 7 :]
+        if cell == 0:
+            wo, w1, w2 = made[:3]
+            made = made[3:]
         results.append(result)
         keys[cell].append(k)
         values[cell].append(v)
         kept[cell].append(p)
         firsts.append(first)
-        carried = list(made[ring + 6 :]) + [vec_mid]
-    keep, give = made[ring + 6 :]
+        carried = list(made) + [vec_mid]
+    keep, give = made
     received_one = swap(give, "core", 1)
     queries[-1], received = lax.optimization_barrier((queries[-1], received))
     partial = backward_of_blocks(cells - 1)
@@ -790,12 +857,11 @@
     for cell in range(cells):
         finish = cell == cells - 1
         if finish:
-            carried, got_one, partial = lax.optimization_barrier((carried, got_one, partial))
+            carried, got_one = lax.optimization_barrier((carried, got_one))
             own_one = sum_steps(own_one, got_one)
             got_one = swap(own_one, "z", depth_steps[0])
-            received.append(returned(partial))
         ins = [
-            x_moved[cell][0], x_moved[-1][0], queries[cell], grads_out[cell][0], keys[cell][0],
+            x_moved[cell][0], carriers[0], queries[cell], grads_out[cell][0], keys[cell][0],
             values[cell][0], kept[cell][0], w_all, w_kv, firsts[cell], dq[cell],
         ]
         outs = [full_narrow]
@@ -821,16 +887,18 @@
     for step in depth_steps[1:]:
         own_one = tree_sum([own_one, got_one])
         got_one = swap(own_one, "z", step)
-    other, received = lax.optimization_barrier((other, received))
     own, pieces = divide(keep, other, ring)
     got, got_one = lax.optimization_barrier((swaps(pieces, PLANE), got_one))
     own = sum_steps(own, got)
-    own = sum_steps(own, to_all(own, "z"))
+    own, partial = lax.optimization_barrier((own, partial))
+    received.append(returned(partial))
+    got, received = lax.optimization_barrier((to_all(own, "z"), received))
+    own = sum_steps(own, got)
     own_one = tree_sum([own_one, got_one])
     own = jnp.concatenate([own_one, own], axis=0)
     tokens_grad = call(
         functools.partial(finish_kernel, cells),
-        [x_moved[-1][0]] + local + sum(received, []),
+        [carriers[0]] + local + sum(received, []),
         [shape((cells, rows, width), F32)],
     )[0]
     got = to_all(own, PLANE)

time: 78.5 us -> 76 us (0.968)
  other arithmetic: 3.49 us -> 1.21 us
  Pallas kernels: 34.3 us -> 35.7 us
  waiting for transfers between devices: 12.5 us -> 11.7 us
    pallas_call x0 -> x2, Pallas kernels: none -> 2.48 us  [body(): pl.pallas_call(functools.partial(select_kernel, cell, carry), in_specs=[p...]
    convert_element_type x2 -> x0, other arithmetic: 1.41 us -> none  [the longest x1 1.41 us: body(): x_low = [part.astype(BF) for part in stream]]
    pallas_call x11, Pallas kernels: 34.3 us -> 33.2 us  [call(): pl.pallas_call(kernel, in_specs=[smem if a.ndim == 1 else vmem for a in i...]
    eq x1 -> x0, other arithmetic: 0.85 us -> none  [body(): masked[cell][:, None] == 1]
  transfers between devices with their start and end apart: 24 -> 24, of which waited for: 13 -> 11; matrix products, arithmetic and copies ran while one was open for 2% -> 2% of each run, Pallas kernels for 37% -> 40%
where the time goes in v2:
time: 76 us; the launch traced here: 75.8 us
  Pallas kernels  35.7 us (47%)
  starting transfers between devices  24.9 us (33%)
  waiting for transfers between devices  11.7 us (15%)
  other arithmetic  1.21 us (2%)
  between operations  1.2 us (2%)
  local copies, waits for them, and re-layouts  1.12 us (1%)
    pallas_call x11, Pallas kernels, call(): pl.pallas_call(kernel, in_specs=[smem if a.ndim == 1 else vmem for a in i...  33.2 us
    ppermute x20, starting transfers between devices, swap(): lax.ppermute(block, axes, [(i, i ^ step) for i in range(lax.axis_size(axe...  20 us
    ppermute x20, waiting for transfers between devices, swap(): lax.ppermute(block, axes, [(i, i ^ step) for i in range(lax.axis_size(axe...  11.4 us
    ppermute x4, starting transfers between devices, send(): return lax.ppermute(block, 'seq', route)  4.91 us
    pallas_call x2, Pallas kernels, body(): pl.pallas_call(functools.partial(select_kernel, cell, carry), in_specs=[p...  2.48 us
  transfers between devices with their start and end apart: 24, of which 11 were waited for; matrix products, arithmetic and copies ran while one was open for 2% of the time, Pallas kernels for 40%

profile of v2, /device:TPU:0, one launch (start us, length us, event | category | flops | bytes accessed | tf_op | source)
XLA Modules:
  0.0 75.8 jit_solution(7925897082747315242)
XLA Ops:
  0.7 1.3 %shard_map.339 = (f32[512,256]{1,0:T(8,128)S(1)}, bf16[512,256]{1,0:T(8,128)(2,1)S(1)}) custom-call(f32[2,512,256]{2,1,0:T(8,128)} %tokens.3, s32[2,512]{1,0:T(2,128)} %masks.2, f32[1,256]{1,0:T(1,128)} %bitcast.47), custom_call_target="tpu_custom_call" | custom-call | tf_op jit(solution)/shard_map/pallas_call | solution.py:688
  2.0 3.0 %collective-permute-start.1 = (bf16[512,256]{1,0:T(8,128)(2,1)S(1)}, bf16[512,256]{1,0:T(8,128)(2,1)S(1)}, u32[]{:S(2)}, u32[]{:S(2)}) collective-permute-start(bf16[512,256]{1,0:T(8,128)(2,1)S(1)} %get-tuple-element.151.refs_0_.sent), channel_id=1, source_target_pairs={{0,1},{1,0},{2,3},{3,2},{4,5},{5,4},{6,7},{7,6},{8,9},{9,8},{10,11... | collective-permute-start | bytes 786440 | tf_op jit(solution)/shard_map/ppermute | solution.py:620
  5.0 1.2 %shard_map.340 = (f32[512,256]{1,0:T(8,128)S(1)}, bf16[512,256]{1,0:T(8,128)(2,1)S(1)}, bf16[528,256]{1,0:T(8,128)(2,1)S(1)}) custom-call(f32[2,512,256]{2,1,0:T(8,128)} %tokens.3, s32[2,512]{1,0:T(2,128)} %masks.2, f32[1,256]{1,0:T(1,128)} %bitcast.48), custom_call_target="tpu_custom_call" | custom-call | tf_op jit(solution)/shard_map/pallas_call | solution.py:688
  6.3 4.7 %shard_map.341 = (bf16[512,512]{1,0:T(8,128)(2,1)S(1)}, bf16[512,512]{1,0:T(8,128)(2,1)S(1)}, bf16[512,512]{1,0:T(8,128)(2,1)S(1)}, bf16[2048,512]{1,0:T(8,128)(...) custom-call(s32[2]{0:T(128)S(1)} %copy-done.15, ...), custom_call_target="tpu_custom_call" | custom-call | flops 2147483648 | bytes 13895688 | tf_op jit(solution)/shard_map/pallas_call | solution.py:605
  11.1 0.1 collective-permute-start
  11.2 0.1 slice_bitcast_fusion
  11.3 0.7 copy-done
  12.1 0.2 copy-done.1
  12.3 6.6 %shard_map.342 = (bf16[512,512]{1,0:T(8,128)(2,1)S(1)}, bf16[512,512]{1,0:T(8,128)(2,1)S(1)}, f32[512,256]{1,0:T(8,128)S(1)}, bf16[512,512]{1,0:T(8,128)(2,1)S(1...) custom-call(s32[2]{0:T(128)S(1)} %copy-done.15, ...), custom_call_target="tpu_custom_call" | custom-call | flops 3758096384 | bytes 13919240 | tf_op jit(solution)/shard_map/pallas_call | solution.py:605
  18.9 0.2 collective-permute-done.carrier.x
  19.2 2.7 %shard_map.343 = (f32[512,512]{1,0:T(8,128)S(1)}, bf16[512,256]{1,0:T(8,128)(2,1)S(1)}, f32[512,256]{1,0:T(8,128)S(1)}, f32[256,128]{1,0:T(8,128)S(1)}, f32[8,512]{1,0:T(8,128)S(1)}) custom-call(bf16[512,256]{1,0:T(8,128)(2,1)S(1)} %get-tuple-element.164.sent, bf16[528,256]{1,0:T(8,128)(2,1)S(1)} %collective-permute-done.carrier.x, ...), custom_call_target="tpu_custom_call" | custom-call | flops 2684354560 | bytes 6971392 | tf_op jit(solution)/shard_map/pallas_call | solution.py:605
  21.8 0.9 %collective-permute-start.2 = (bf16[512,256]{1,0:T(8,128)(2,1)S(1)}, bf16[512,256]{1,0:T(8,128)(2,1)S(1)}, u32[]{:S(2)}, u32[]{:S(2)}) collective-permute-start(bf16[512,256]{1,0:T(8,128)(2,1)S(1)} %get-tuple-element.182), channel_id=1, source_target_pairs={{0,1},{1,0},{2,3},{3,2},{4,5},{5,4},{6,7},{7,6},{8,9},{9,8},{10,11... | collective-permute-start | bytes 786440 | tf_op jit(solution)/shard_map/ppermute | solution.py:620
  22.7 6.7 %shard_map.344 = (bf16[512,512]{1,0:T(8,128)(2,1)S(1)}, bf16[512,512]{1,0:T(8,128)(2,1)S(1)}, f32[512,256]{1,0:T(8,128)S(1)}, bf16[512,512]{1,0:T(8,128)(2,1)S(1...) custom-call(s32[2]{0:T(128)S(1)} %copy-done.15, ...), custom_call_target="tpu_custom_call" | custom-call | flops 3758096384 | bytes 13288456 | tf_op jit(solution)/shard_map/pallas_call | solution.py:605
  29.4 0.1 collective-permute-start.3
  29.5 2.5 %shard_map.345 = (f32[512,512]{1,0:T(8,128)S(1)}, bf16[512,256]{1,0:T(8,128)(2,1)S(1)}, f32[512,256]{1,0:T(8,128)S(1)}, f32[256,128]{1,0:T(8,128)S(1)}, f32[8,512]{1,0:T(8,128)S(1)}) custom-call(bf16[512,256]{1,0:T(8,128)(2,1)S(1)} %get-tuple-element.181.sent, bf16[528,256]{1,0:T(8,128)(2,1)S(1)} %collective-permute-done.carrier.x, ...), custom_call_target="tpu_custom_call" | custom-call | flops 2684354560 | bytes 7643136 | tf_op jit(solution)/shard_map/pallas_call | solution.py:605
  32.0 0.1 shard_map.346
  32.1 1.2 %collective-permute-start.4 = (bf16[160,256]{1,0:T(8,128)(2,1)S(1)}, bf16[160,256]{1,0:T(8,128)(2,1)S(1)}, u32[]{:S(2)}, u32[]{:S(2)}) collective-permute-start(bf16[160,256]{1,0:T(8,128)(2,1)S(1)} %get-tuple-element.215), channel_id=1, source_target_pairs={{0,1},{1,0},{4,5},{5,4},{2,3},{3,2},{6,7},{7,6},{8,9},{9,8},{12,13... | collective-permute-start | bytes 245768 | tf_op jit(solution)/shard_map/ppermute | solution.py:628
  33.4 1.5 %collective-permute-start.5 = (bf16[160,256]{1,0:T(8,128)(2,1)S(1)}, bf16[160,256]{1,0:T(8,128)(2,1)S(1)}, u32[]{:S(2)}, u32[]{:S(2)}) collective-permute-start(bf16[160,256]{1,0:T(8,128)(2,1)S(1)} %get-tuple-element.216), channel_id=1, source_target_pairs={{0,4},{1,5},{4,0},{5,1},{2,6},{3,7},{6,2},{7,3},{8,12},{9,13},{12,... | collective-permute-start | bytes 245768 | tf_op jit(solution)/shard_map/ppermute | solution.py:628
  34.8 0.8 %collective-permute-start.6 = (bf16[160,256]{1,0:T(8,128)(2,1)S(1)}, bf16[160,256]{1,0:T(8,128)(2,1)S(1)}, u32[]{:S(2)}, u32[]{:S(2)}) collective-permute-start(bf16[160,256]{1,0:T(8,128)(2,1)S(1)} %get-tuple-element.217), channel_id=1, source_target_pairs={{0,5},{1,4},{4,1},{5,0},{2,7},{3,6},{6,3},{7,2},{8,13},{9,12},{12,... | collective-permute-start | bytes 245768 | tf_op jit(solution)/shard_map/ppermute | solution.py:628
  35.7 3.0 %shard_map.347 = (f32[512,256]{1,0:T(8,128)S(1)}, f32[512,256]{1,0:T(8,128)S(1)}, f32[256,128]{1,0:T(8,128)S(1)}, f32[8,512]{1,0:T(8,128)S(1)}, f32[256,512]{1,0:T(8,128)S(1)}) custom-call(bf16[512,256]{1,0:T(8,128)(2,1)S(1)} %get-tuple-element.151.refs_0_.sent, bf16[528,256]{1,0:T(8,128)(2,1)S(1)} %get-tuple-element.155.carrier.sent, ...), custom_call_target="tpu_custom_call" | custom-call | flops 1 | bytes 1 | tf_op jit(solution)/shard_map/pallas_call | solution.py:605
  38.7 1.5 %collective-permute-done.6 = bf16[160,256]{1,0:T(8,128)(2,1)S(1)} collective-permute-done((bf16[160,256]{1,0:T(8,128)(2,1)S(1)}, bf16[160,256]{1,0:T(8,128)(2,1)S(1)}, u32[]{:S(2)}, u32[]{:S(2)}) %collective-permute-start.6) | collective-permute-done | bytes 81952 | tf_op jit(solution)/shard_map/ppermute | solution.py:628
  40.2 1.7 %collective-permute-start.7 = (bf16[160,256]{1,0:T(8,128)(2,1)S(1)}, bf16[160,256]{1,0:T(8,128)(2,1)S(1)}, u32[]{:S(2)}, u32[]{:S(2)}) collective-permute-start(bf16[160,256]{1,0:T(8,128)(2,1)S(1)} %add_convert_fusion.2), channel_id=1, source_target_pairs={{0,8},{8,0},{16,24},{24,16},{1,9},{9,1},{17,25},{25,17},{2,10},{10... | collective-permute-start | bytes 245768 | tf_op jit(solution)/shard_map/ppermute | solution.py:628
  41.9 3.8 %shard_map.348 = (f32[512,256]{1,0:T(8,128)S(1)}, bf16[448,256]{1,0:T(8,128)(2,1)S(1)}, bf16[448,256]{1,0:T(8,128)(2,1)S(1)}) custom-call(bf16[528,256]{1,0:T(8,128)(2,1)S(1)} %get-tuple-element.155.carrier.sent, bf16[528,256]{1,0:T(8,128)(2,1)S(1)} %get-tuple-element.155.carrier.sent, bf16[512,512]{1,0:T(8,128)(2,1)S(1)} %get-tuple-element.183.q, ...), custom_call_target="tpu_custom_call" | custom-call | flops 1 | bytes 1 | tf_op jit(solution)/shard_map/pallas_call | solution.py:605
  45.7 0.1 collective-permute-start.8
  45.8 2.6 %collective-permute-start.12 = (bf16[160,256]{1,0:T(8,128)(2,1)S(1)}, bf16[160,256]{1,0:T(8,128)(2,1)S(1)}, u32[]{:S(2)}, u32[]{:S(2)}) collective-permute-start(bf16[160,256]{1,0:T(8,128)(2,1)S(1)} %add_convert_fusion.1), channel_id=1, source_target_pairs={{0,16},{8,24},{16,0},{24,8},{1,17},{9,25},{17,1},{25,9},{2,18},{10... | collective-permute-start | bytes 245768 | tf_op jit(solution)/shard_map/ppermute | solution.py:628
  48.5 1.0 %collective-permute-start.9 = (bf16[112,256]{1,0:T(8,128)(2,1)S(1)}, bf16[112,256]{1,0:T(8,128)(2,1)S(1)}, u32[]{:S(2)}, u32[]{:S(2)}) collective-permute-start(bf16[112,256]{1,0:T(8,128)(2,1)S(1)} %get-tuple-element.236), channel_id=1, source_target_pairs={{0,1},{1,0},{4,5},{5,4},{2,3},{3,2},{6,7},{7,6},{8,9},{9,8},{12,13... | collective-permute-start | bytes 172040 | tf_op jit(solution)/shard_map/ppermute | solution.py:628
  49.5 1.5 %collective-permute-start.10 = (bf16[112,256]{1,0:T(8,128)(2,1)S(1)}, bf16[112,256]{1,0:T(8,128)(2,1)S(1)}, u32[]{:S(2)}, u32[]{:S(2)}) collective-permute-start(bf16[112,256]{1,0:T(8,128)(2,1)S(1)} %get-tuple-element.237), channel_id=1, source_target_pairs={{0,4},{1,5},{4,0},{5,1},{2,6},{3,7},{6,2},{7,3},{8,12},{9,13},{12,... | collective-permute-start | bytes 172040 | tf_op jit(solution)/shard_map/ppermute | solution.py:628
  51.0 1.1 %collective-permute-start.11 = (bf16[112,256]{1,0:T(8,128)(2,1)S(1)}, bf16[112,256]{1,0:T(8,128)(2,1)S(1)}, u32[]{:S(2)}, u32[]{:S(2)}) collective-permute-start(bf16[112,256]{1,0:T(8,128)(2,1)S(1)} %get-tuple-element.238), channel_id=1, source_target_pairs={{0,5},{1,4},{4,1},{5,0},{2,7},{3,6},{6,3},{7,2},{8,13},{9,12},{12,... | collective-permute-start | bytes 172040 | tf_op jit(solution)/shard_map/ppermute | solution.py:628
  52.1 1.3 %collective-permute-done.12 = bf16[160,256]{1,0:T(8,128)(2,1)S(1)} collective-permute-done((bf16[160,256]{1,0:T(8,128)(2,1)S(1)}, bf16[160,256]{1,0:T(8,128)(2,1)S(1)}, u32[]{:S(2)}, u32[]{:S(2)}) %collective-permute-start.12) | collective-permute-done | bytes 81952 | tf_op jit(solution)/shard_map/ppermute | solution.py:628
  53.4 0.5 collective-permute-done.10
  53.9 2.2 %collective-permute-done.11 = bf16[112,256]{1,0:T(8,128)(2,1)S(1)} collective-permute-done((bf16[112,256]{1,0:T(8,128)(2,1)S(1)}, bf16[112,256]{1,0:T(8,128)(2,1)S(1)}, u32[]{:S(2)}, u32[]{:S(2)}) %collective-permute-start.11) | collective-permute-done | bytes 57376 | tf_op jit(solution)/shard_map/ppermute | solution.py:628
  56.1 0.9 %collective-permute-start.16 = (bf16[512,256]{1,0:T(8,128)(2,1)S(1)}, bf16[512,256]{1,0:T(8,128)(2,1)S(1)}, u32[]{:S(2)}, u32[]{:S(2)}) collective-permute-start(bf16[512,256]{1,0:T(8,128)(2,1)S(1)} %get-tuple-element.247), channel_id=1, source_target_pairs={{0,1},{1,0},{2,3},{3,2},{4,5},{5,4},{6,7},{7,6},{8,9},{9,8},{10,11... | collective-permute-start | bytes 786440 | tf_op jit(solution)/shard_map/ppermute | solution.py:620
  57.0 1.4 %collective-permute-start.15 = (bf16[112,256]{1,0:T(8,128)(2,1)S(1)}, bf16[112,256]{1,0:T(8,128)(2,1)S(1)}, u32[]{:S(2)}, u32[]{:S(2)}) collective-permute-start(bf16[112,256]{1,0:T(8,128)(2,1)S(1)} %add_convert_fusion.4), channel_id=1, source_target_pairs={{0,24},{8,16},{16,8},{24,0},{1,25},{9,17},{17,9},{25,1},{2,26},{10... | collective-permute-start | bytes 172040 | tf_op jit(solution)/shard_map/ppermute | solution.py:628
  58.4 0.6 collective-permute-start.14
  59.1 2.4 %collective-permute-start.13 = (bf16[112,256]{1,0:T(8,128)(2,1)S(1)}, bf16[112,256]{1,0:T(8,128)(2,1)S(1)}, u32[]{:S(2)}, u32[]{:S(2)}) collective-permute-start(bf16[112,256]{1,0:T(8,128)(2,1)S(1)} %add_convert_fusion.4), channel_id=1, source_target_pairs={{0,8},{8,0},{16,24},{24,16},{1,9},{9,1},{17,25},{25,17},{2,10},{10... | collective-permute-start | bytes 172040 | tf_op jit(solution)/shard_map/ppermute | solution.py:628
  61.4 1.6 %collective-permute-done.15 = bf16[112,256]{1,0:T(8,128)(2,1)S(1)} collective-permute-done((bf16[112,256]{1,0:T(8,128)(2,1)S(1)}, bf16[112,256]{1,0:T(8,128)(2,1)S(1)}, u32[]{:S(2)}, u32[]{:S(2)}) %collective-permute-start.15) | collective-permute-done | bytes 57376 | tf_op jit(solution)/shard_map/ppermute | solution.py:628
  63.0 1.2 %collective-permute-done.14 = bf16[112,256]{1,0:T(8,128)(2,1)S(1)} collective-permute-done((bf16[112,256]{1,0:T(8,128)(2,1)S(1)}, bf16[112,256]{1,0:T(8,128)(2,1)S(1)}, u32[]{:S(2)}, u32[]{:S(2)}) %collective-permute-start.14) | collective-permute-done | bytes 57376 | tf_op jit(solution)/shard_map/ppermute | solution.py:628
  64.3 1.2 %collective-permute-start.17 = (bf16[272,256]{1,0:T(8,128)(2,1)S(1)}, bf16[272,256]{1,0:T(8,128)(2,1)S(1)}, u32[]{:S(2)}, u32[]{:S(2)}) collective-permute-start(bf16[272,256]{1,0:T(8,128)(2,1)S(1)} %pad_maximum_fusion.1.refs_0_), channel_id=1, source_target_pairs={{0,1},{1,0},{4,5},{5,4},{2,3},{3,2},{6,7},{7,6},{8,9},{9,8},{12,13... | collective-permute-start | bytes 417800 | tf_op jit(solution)/shard_map/ppermute | solution.py:628
  65.5 1.1 %collective-permute-start.19 = (bf16[272,256]{1,0:T(8,128)(2,1)S(1)}, bf16[272,256]{1,0:T(8,128)(2,1)S(1)}, u32[]{:S(2)}, u32[]{:S(2)}) collective-permute-start(bf16[272,256]{1,0:T(8,128)(2,1)S(1)} %pad_maximum_fusion.1.refs_0_), channel_id=1, source_target_pairs={{0,5},{1,4},{4,1},{5,0},{2,7},{3,6},{6,3},{7,2},{8,13},{9,12},{12,... | collective-permute-start | bytes 417800 | tf_op jit(solution)/shard_map/ppermute | solution.py:628
  66.7 1.2 %collective-permute-start.18 = (bf16[272,256]{1,0:T(8,128)(2,1)S(1)}, bf16[272,256]{1,0:T(8,128)(2,1)S(1)}, u32[]{:S(2)}, u32[]{:S(2)}) collective-permute-start(bf16[272,256]{1,0:T(8,128)(2,1)S(1)} %pad_maximum_fusion.1.refs_0_), channel_id=1, source_target_pairs={{0,4},{1,5},{4,0},{5,1},{2,6},{3,7},{6,2},{7,3},{8,12},{9,13},{12,... | collective-permute-start | bytes 417800 | tf_op jit(solution)/shard_map/ppermute | solution.py:628
  67.9 1.0 %pad_maximum_fusion = f32[2,512,256]{2,1,0:T(8,128)} fusion(f32[1,512,256]{2,1,0:T(8,128)S(1)} %bitcast.28, f32[1,512,256]{2,1,0:T(8,128)S(1)} %bitcast.27), kind=kLoop, calls=%fused_computation | loop fusion | flops 262144 | bytes 2097152 | tf_op jit(solution)/shard_map/stack | solution.py:905
  68.9 1.4 %shard_map.350 = f32[2,512,256]{2,1,0:T(8,128)} custom-call(bf16[528,256]{1,0:T(8,128)(2,1)S(1)} %get-tuple-element.155.carrier.sent, f32[512,256]{1,0:T(8,128)S(1)} %get-tuple-element.251.refs_0_, f32[512,256]{1,0:T(8,128)S(1)} %get-tuple-element.252.refs_1_, bf16[512,256]{1,0:T(8,128)(2,1)S(1)} %collective-permute-done.2.refs_2_, ...), custom_call_target="tpu_custom_call" | custom-call | bytes 2891776 | tf_op jit(solution)/shard_map/pallas_call | solution.py:605
  70.3 1.2 %collective-permute-done.19.refs_3_ = bf16[272,256]{1,0:T(8,128)(2,1)S(1)} collective-permute-done((bf16[272,256]{1,0:T(8,128)(2,1)S(1)}, bf16[272,256]{1,0:T(8,128)(2,1)S(1)}, u32[]{:S(2)}, u32[]{:S(2)}) %collective-permute-start.19) | collective-permute-done | bytes 139296 | tf_op jit(solution)/shard_map/ppermute | solution.py:628
  71.5 0.9 %collective-permute-done.18.refs_2_ = bf16[272,256]{1,0:T(8,128)(2,1)S(1)} collective-permute-done((bf16[272,256]{1,0:T(8,128)(2,1)S(1)}, bf16[272,256]{1,0:T(8,128)(2,1)S(1)}, u32[]{:S(2)}, u32[]{:S(2)}) %collective-permute-start.18) | collective-permute-done | bytes 139296 | tf_op jit(solution)/shard_map/ppermute | solution.py:628
  72.4 0.5 collective-permute-start.21
  72.9 0.8 %collective-permute-done.22.refs_6_ = bf16[272,256]{1,0:T(8,128)(2,1)S(1)} collective-permute-done((bf16[272,256]{1,0:T(8,128)(2,1)S(1)}, bf16[272,256]{1,0:T(8,128)(2,1)S(1)}, u32[]{:S(2)}, u32[]{:S(2)}) %collective-permute-start.22) | collective-permute-done | bytes 139296 | tf_op jit(solution)/shard_map/ppermute | solution.py:628
  73.7 0.2 collective-permute-done.21.refs_5_
  73.9 1.7 %shard_map.351 = (f32[256,256]{1,0:T(8,128)}, f32[256,512]{1,0:T(8,128)}, f32[512,256]{1,0:T(8,128)}, f32[256,256]{1,0:T(8,128)}, f32[256,256]{1,0:T(8,128)}, /*...) custom-call(bf16[272,256]{1,0:T(8,128)(2,1)S(1)} %pad_maximum_fusion, ...), custom_call_target="tpu_custom_call" | custom-call | bytes 3222540 | tf_op jit(solution)/shard_map/pallas_call | solution.py:605
  (55 shorter events, 0.4 us)
Async XLA Ops:
  0.7 5.6 %copy-start.15 = (s32[2]{0:T(128)S(1)}, s32[2]{0:T(128)}, u32[]{:S(2)}) copy-start(s32[2]{0:T(128)} %lengths.5) | copy-start | bytes 28
  0.7 5.6 %copy-start.8 = (f32[256]{0:T(256)S(1)}, f32[256]{0:T(256)}, u32[]{:S(2)}) copy-start(f32[256]{0:T(256)} %param.29) | copy-start | bytes 3076
  0.7 5.6 %copy-start.4 = (f32[256,256]{1,0:T(8,128)S(1)}, f32[256,256]{1,0:T(8,128)}, u32[]{:S(2)}) copy-start(f32[256,256]{1,0:T(8,128)} %refs_4_.1) | copy-start | bytes 786436
  0.7 5.6 %copy-start.3 = (f32[256,256]{1,0:T(8,128)S(1)}, f32[256,256]{1,0:T(8,128)}, u32[]{:S(2)}) copy-start(f32[256,256]{1,0:T(8,128)} %refs_3_.1) | copy-start | bytes 786436
  0.7 5.6 %copy-start.7 = (f32[256]{0:T(256)S(1)}, f32[256]{0:T(256)}, u32[]{:S(2)}) copy-start(f32[256]{0:T(256)} %param.26) | copy-start | bytes 3076
  0.7 5.6 %copy-start.2 = (f32[256,256]{1,0:T(8,128)S(1)}, f32[256,256]{1,0:T(8,128)}, u32[]{:S(2)}) copy-start(f32[256,256]{1,0:T(8,128)} %refs_2_.1) | copy-start | bytes 786436
  2.0 9.3 %collective-permute-start.1 = (bf16[512,256]{1,0:T(8,128)(2,1)S(1)}, bf16[512,256]{1,0:T(8,128)(2,1)S(1)}, u32[]{:S(2)}, u32[]{:S(2)}) collective-permute-start(bf16[512,256]{1,0:T(8,128)(2,1)S(1)} %get-tuple-element.151.refs_0_.sent), channel_id=1, source_target_pairs={{0,1},{1,0},{2,3},{3,2},{4,5},{5,4},{6,7},{7,6},{8,9},{9,8},{10,11... | collective-permute-start | bytes 786440 | tf_op jit(solution)/shard_map/ppermute | solution.py:620
  6.3 4.9 %copy-start.16 = (f32[2,512,256]{2,1,0:T(8,128)S(1)}, f32[2,512,256]{2,1,0:T(8,128)}, u32[]{:S(2)}) copy-start(f32[2,512,256]{2,1,0:T(8,128)} %param.23) | copy-start | bytes 3145732
  11.0 1.0 %copy-start = (f32[256,512]{1,0:T(8,128)S(1)}, f32[256,512]{1,0:T(8,128)}, u32[]{:S(2)}) copy-start(f32[256,512]{1,0:T(8,128)} %w1_in.1) | copy-start | bytes 1572868
  11.0 1.2 %copy-start.1 = (f32[512,256]{1,0:T(8,128)S(1)}, f32[512,256]{1,0:T(8,128)}, u32[]{:S(2)}) copy-start(f32[512,256]{1,0:T(8,128)} %w2_in.1) | copy-start | bytes 1572868
  11.1 1.2 %copy-start.5 = (f32[256,256]{1,0:T(8,128)S(1)}, f32[256,256]{1,0:T(8,128)}, u32[]{:S(2)}) copy-start(f32[256,256]{1,0:T(8,128)} %wo_in.1) | copy-start | bytes 786436
  11.1 1.2 %copy-start.6 = (f32[512]{0:T(512)S(1)}, f32[512]{0:T(512)}, u32[]{:S(2)}) copy-start(f32[512]{0:T(512)} %param.35) | copy-start | bytes 6148
  11.1 1.2 %copy-start.9 = (f32[256]{0:T(256)S(1)}, f32[256]{0:T(256)}, u32[]{:S(2)}) copy-start(f32[256]{0:T(256)} %param.31) | copy-start | bytes 3076
  11.1 1.2 %copy-start.10 = (f32[256]{0:T(256)S(1)}, f32[256]{0:T(256)}, u32[]{:S(2)}) copy-start(f32[256]{0:T(256)} %param.32) | copy-start | bytes 3076
  11.1 1.2 %copy-start.11 = (f32[256]{0:T(256)S(1)}, f32[256]{0:T(256)}, u32[]{:S(2)}) copy-start(f32[256]{0:T(256)} %param.33) | copy-start | bytes 3076
  11.1 1.2 %copy-start.12 = (f32[256]{0:T(256)S(1)}, f32[256]{0:T(256)}, u32[]{:S(2)}) copy-start(f32[256]{0:T(256)} %param.37) | copy-start | bytes 3076
  11.1 1.2 %copy-start.13 = (f32[256]{0:T(256)S(1)}, f32[256]{0:T(256)}, u32[]{:S(2)}) copy-start(f32[256]{0:T(256)} %param.38) | copy-start | bytes 3076
  11.1 1.2 %copy-start.14 = (f32[256]{0:T(256)S(1)}, f32[256]{0:T(256)}, u32[]{:S(2)}) copy-start(f32[256]{0:T(256)} %param.39) | copy-start | bytes 3076
  11.1 8.0 %collective-permute-start = (bf16[528,256]{1,0:T(8,128)(2,1)S(1)}, bf16[528,256]{1,0:T(8,128)(2,1)S(1)}, u32[]{:S(2)}, u32[]{:S(2)}) collective-permute-start(bf16[528,256]{1,0:T(8,128)(2,1)S(1)} %get-tuple-element.155.carrier.sent), channel_id=1, source_target_pairs={{0,1},{1,0},{2,3},{3,2},{4,5},{5,4},{6,7},{7,6},{8,9},{9,8},{10,11... | collective-permute-start | bytes 811016 | tf_op jit(solution)/shard_map/ppermute | solution.py:620
  21.8 7.7 %collective-permute-start.2 = (bf16[512,256]{1,0:T(8,128)(2,1)S(1)}, bf16[512,256]{1,0:T(8,128)(2,1)S(1)}, u32[]{:S(2)}, u32[]{:S(2)}) collective-permute-start(bf16[512,256]{1,0:T(8,128)(2,1)S(1)} %get-tuple-element.182), channel_id=1, source_target_pairs={{0,1},{1,0},{2,3},{3,2},{4,5},{5,4},{6,7},{7,6},{8,9},{9,8},{10,11... | collective-permute-start | bytes 786440 | tf_op jit(solution)/shard_map/ppermute | solution.py:620
  29.4 2.6 %collective-permute-start.3 = (bf16[640,256]{1,0:T(8,128)(2,1)S(1)}, bf16[640,256]{1,0:T(8,128)(2,1)S(1)}, u32[]{:S(2)}, u32[]{:S(2)}) collective-permute-start(bf16[640,256]{1,0:T(8,128)(2,1)S(1)} %get-tuple-element.196), channel_id=1, source_target_pairs={{0,2},{2,0},{1,3},{3,1},{4,6},{6,4},{5,7},{7,5},{8,10},{10,8},{9,1... | collective-permute-start | bytes 983048 | tf_op jit(solution)/shard_map/ppermute | solution.py:628
  32.1 6.6 %collective-permute-start.4 = (bf16[160,256]{1,0:T(8,128)(2,1)S(1)}, bf16[160,256]{1,0:T(8,128)(2,1)S(1)}, u32[]{:S(2)}, u32[]{:S(2)}) collective-permute-start(bf16[160,256]{1,0:T(8,128)(2,1)S(1)} %get-tuple-element.215), channel_id=1, source_target_pairs={{0,1},{1,0},{4,5},{5,4},{2,3},{3,2},{6,7},{7,6},{8,9},{9,8},{12,13... | collective-permute-start | bytes 245768 | tf_op jit(solution)/shard_map/ppermute | solution.py:628
  33.4 5.4 %collective-permute-start.5 = (bf16[160,256]{1,0:T(8,128)(2,1)S(1)}, bf16[160,256]{1,0:T(8,128)(2,1)S(1)}, u32[]{:S(2)}, u32[]{:S(2)}) collective-permute-start(bf16[160,256]{1,0:T(8,128)(2,1)S(1)} %get-tuple-element.216), channel_id=1, source_target_pairs={{0,4},{1,5},{4,0},{5,1},{2,6},{3,7},{6,2},{7,3},{8,12},{9,13},{12,... | collective-permute-start | bytes 245768 | tf_op jit(solution)/shard_map/ppermute | solution.py:628
  34.8 5.3 %collective-permute-start.6 = (bf16[160,256]{1,0:T(8,128)(2,1)S(1)}, bf16[160,256]{1,0:T(8,128)(2,1)S(1)}, u32[]{:S(2)}, u32[]{:S(2)}) collective-permute-start(bf16[160,256]{1,0:T(8,128)(2,1)S(1)} %get-tuple-element.217), channel_id=1, source_target_pairs={{0,5},{1,4},{4,1},{5,0},{2,7},{3,6},{6,3},{7,2},{8,13},{9,12},{12,... | collective-permute-start | bytes 245768 | tf_op jit(solution)/shard_map/ppermute | solution.py:628
  40.2 5.4 %collective-permute-start.7 = (bf16[160,256]{1,0:T(8,128)(2,1)S(1)}, bf16[160,256]{1,0:T(8,128)(2,1)S(1)}, u32[]{:S(2)}, u32[]{:S(2)}) collective-permute-start(bf16[160,256]{1,0:T(8,128)(2,1)S(1)} %add_convert_fusion.2), channel_id=1, source_target_pairs={{0,8},{8,0},{16,24},{24,16},{1,9},{9,1},{17,25},{25,17},{2,10},{10... | collective-permute-start | bytes 245768 | tf_op jit(solution)/shard_map/ppermute | solution.py:628
  45.7 2.8 %collective-permute-start.8 = (bf16[448,256]{1,0:T(8,128)(2,1)S(1)}, bf16[448,256]{1,0:T(8,128)(2,1)S(1)}, u32[]{:S(2)}, u32[]{:S(2)}) collective-permute-start(bf16[448,256]{1,0:T(8,128)(2,1)S(1)} %get-tuple-element.235), channel_id=1, source_target_pairs={{0,2},{2,0},{1,3},{3,1},{4,6},{6,4},{5,7},{7,5},{8,10},{10,8},{9,1... | collective-permute-start | bytes 688136 | tf_op jit(solution)/shard_map/ppermute | solution.py:628
  45.8 7.6 %collective-permute-start.12 = (bf16[160,256]{1,0:T(8,128)(2,1)S(1)}, bf16[160,256]{1,0:T(8,128)(2,1)S(1)}, u32[]{:S(2)}, u32[]{:S(2)}) collective-permute-start(bf16[160,256]{1,0:T(8,128)(2,1)S(1)} %add_convert_fusion.1), channel_id=1, source_target_pairs={{0,16},{8,24},{16,0},{24,8},{1,17},{9,25},{17,1},{25,9},{2,18},{10... | collective-permute-start | bytes 245768 | tf_op jit(solution)/shard_map/ppermute | solution.py:628
  48.5 4.9 %collective-permute-start.9 = (bf16[112,256]{1,0:T(8,128)(2,1)S(1)}, bf16[112,256]{1,0:T(8,128)(2,1)S(1)}, u32[]{:S(2)}, u32[]{:S(2)}) collective-permute-start(bf16[112,256]{1,0:T(8,128)(2,1)S(1)} %get-tuple-element.236), channel_id=1, source_target_pairs={{0,1},{1,0},{4,5},{5,4},{2,3},{3,2},{6,7},{7,6},{8,9},{9,8},{12,13... | collective-permute-start | bytes 172040 | tf_op jit(solution)/shard_map/ppermute | solution.py:628
  49.5 4.4 %collective-permute-start.10 = (bf16[112,256]{1,0:T(8,128)(2,1)S(1)}, bf16[112,256]{1,0:T(8,128)(2,1)S(1)}, u32[]{:S(2)}, u32[]{:S(2)}) collective-permute-start(bf16[112,256]{1,0:T(8,128)(2,1)S(1)} %get-tuple-element.237), channel_id=1, source_target_pairs={{0,4},{1,5},{4,0},{5,1},{2,6},{3,7},{6,2},{7,3},{8,12},{9,13},{12,... | collective-permute-start | bytes 172040 | tf_op jit(solution)/shard_map/ppermute | solution.py:628
  51.0 5.1 %collective-permute-start.11 = (bf16[112,256]{1,0:T(8,128)(2,1)S(1)}, bf16[112,256]{1,0:T(8,128)(2,1)S(1)}, u32[]{:S(2)}, u32[]{:S(2)}) collective-permute-start(bf16[112,256]{1,0:T(8,128)(2,1)S(1)} %get-tuple-element.238), channel_id=1, source_target_pairs={{0,5},{1,4},{4,1},{5,0},{2,7},{3,6},{6,3},{7,2},{8,13},{9,12},{12,... | collective-permute-start | bytes 172040 | tf_op jit(solution)/shard_map/ppermute | solution.py:628
  56.1 8.1 %collective-permute-start.16 = (bf16[512,256]{1,0:T(8,128)(2,1)S(1)}, bf16[512,256]{1,0:T(8,128)(2,1)S(1)}, u32[]{:S(2)}, u32[]{:S(2)}) collective-permute-start(bf16[512,256]{1,0:T(8,128)(2,1)S(1)} %get-tuple-element.247), channel_id=1, source_target_pairs={{0,1},{1,0},{2,3},{3,2},{4,5},{5,4},{6,7},{7,6},{8,9},{9,8},{10,11... | collective-permute-start | bytes 786440 | tf_op jit(solution)/shard_map/ppermute | solution.py:620
  57.0 6.0 %collective-permute-start.15 = (bf16[112,256]{1,0:T(8,128)(2,1)S(1)}, bf16[112,256]{1,0:T(8,128)(2,1)S(1)}, u32[]{:S(2)}, u32[]{:S(2)}) collective-permute-start(bf16[112,256]{1,0:T(8,128)(2,1)S(1)} %add_convert_fusion.4), channel_id=1, source_target_pairs={{0,24},{8,16},{16,8},{24,0},{1,25},{9,17},{17,9},{25,1},{2,26},{10... | collective-permute-start | bytes 172040 | tf_op jit(solution)/shard_map/ppermute | solution.py:628
  58.4 5.8 %collective-permute-start.14 = (bf16[112,256]{1,0:T(8,128)(2,1)S(1)}, bf16[112,256]{1,0:T(8,128)(2,1)S(1)}, u32[]{:S(2)}, u32[]{:S(2)}) collective-permute-start(bf16[112,256]{1,0:T(8,128)(2,1)S(1)} %add_convert_fusion.4), channel_id=1, source_target_pairs={{0,16},{8,24},{16,0},{24,8},{1,17},{9,25},{17,1},{25,9},{2,18},{10... | collective-permute-start | bytes 172040 | tf_op jit(solution)/shard_map/ppermute | solution.py:628
  59.1 5.2 %collective-permute-start.13 = (bf16[112,256]{1,0:T(8,128)(2,1)S(1)}, bf16[112,256]{1,0:T(8,128)(2,1)S(1)}, u32[]{:S(2)}, u32[]{:S(2)}) collective-permute-start(bf16[112,256]{1,0:T(8,128)(2,1)S(1)} %add_convert_fusion.4), channel_id=1, source_target_pairs={{0,8},{8,0},{16,24},{24,16},{1,9},{9,1},{17,25},{25,17},{2,10},{10... | collective-permute-start | bytes 172040 | tf_op jit(solution)/shard_map/ppermute | solution.py:628
  64.3 6.0 %collective-permute-start.17 = (bf16[272,256]{1,0:T(8,128)(2,1)S(1)}, bf16[272,256]{1,0:T(8,128)(2,1)S(1)}, u32[]{:S(2)}, u32[]{:S(2)}) collective-permute-start(bf16[272,256]{1,0:T(8,128)(2,1)S(1)} %pad_maximum_fusion.1.refs_0_), channel_id=1, source_target_pairs={{0,1},{1,0},{4,5},{5,4},{2,3},{3,2},{6,7},{7,6},{8,9},{9,8},{12,13... | collective-permute-start | bytes 417800 | tf_op jit(solution)/shard_map/ppermute | solution.py:628
  65.5 6.0 %collective-permute-start.19 = (bf16[272,256]{1,0:T(8,128)(2,1)S(1)}, bf16[272,256]{1,0:T(8,128)(2,1)S(1)}, u32[]{:S(2)}, u32[]{:S(2)}) collective-permute-start(bf16[272,256]{1,0:T(8,128)(2,1)S(1)} %pad_maximum_fusion.1.refs_0_), channel_id=1, source_target_pairs={{0,5},{1,4},{4,1},{5,0},{2,7},{3,6},{6,3},{7,2},{8,13},{9,12},{12,... | collective-permute-start | bytes 417800 | tf_op jit(solution)/shard_map/ppermute | solution.py:628
  66.7 5.7 %collective-permute-start.18 = (bf16[272,256]{1,0:T(8,128)(2,1)S(1)}, bf16[272,256]{1,0:T(8,128)(2,1)S(1)}, u32[]{:S(2)}, u32[]{:S(2)}) collective-permute-start(bf16[272,256]{1,0:T(8,128)(2,1)S(1)} %pad_maximum_fusion.1.refs_0_), channel_id=1, source_target_pairs={{0,4},{1,5},{4,0},{5,1},{2,6},{3,7},{6,2},{7,3},{8,12},{9,13},{12,... | collective-permute-start | bytes 417800 | tf_op jit(solution)/shard_map/ppermute | solution.py:628
  68.9 4.0 %collective-permute-start.20 = (bf16[272,256]{1,0:T(8,128)(2,1)S(1)}, bf16[272,256]{1,0:T(8,128)(2,1)S(1)}, u32[]{:S(2)}, u32[]{:S(2)}) collective-permute-start(bf16[272,256]{1,0:T(8,128)(2,1)S(1)} %pad_maximum_fusion.1.refs_0_), channel_id=1, source_target_pairs={{0,2},{2,0},{1,3},{3,1},{4,6},{6,4},{5,7},{7,5},{8,10},{10,8},{9,1... | collective-permute-start | bytes 417800 | tf_op jit(solution)/shard_map/ppermute | solution.py:628
  71.5 1.4 %collective-permute-start.23 = (bf16[272,256]{1,0:T(8,128)(2,1)S(1)}, bf16[272,256]{1,0:T(8,128)(2,1)S(1)}, u32[]{:S(2)}, u32[]{:S(2)}) collective-permute-start(bf16[272,256]{1,0:T(8,128)(2,1)S(1)} %collective-permute-done.19.refs_3_), channel_id=1, source_target_pairs={{0,2},{2,0},{1,3},{3,1},{4,6},{6,4},{5,7},{7,5},{8,10},{10,8},{9,1... | collective-permute-start | bytes 417800 | tf_op jit(solution)/shard_map/ppermute | solution.py:628
  72.4 1.4 %collective-permute-start.22 = (bf16[272,256]{1,0:T(8,128)(2,1)S(1)}, bf16[272,256]{1,0:T(8,128)(2,1)S(1)}, u32[]{:S(2)}, u32[]{:S(2)}) collective-permute-start(bf16[272,256]{1,0:T(8,128)(2,1)S(1)} %collective-permute-done.18.refs_2_), channel_id=1, source_target_pairs={{0,2},{2,0},{1,3},{3,1},{4,6},{6,4},{5,7},{7,5},{8,10},{10,8},{9,1... | collective-permute-start | bytes 417800 | tf_op jit(solution)/shard_map/ppermute | solution.py:628
  72.4 1.6 %collective-permute-start.21 = (bf16[272,256]{1,0:T(8,128)(2,1)S(1)}, bf16[272,256]{1,0:T(8,128)(2,1)S(1)}, u32[]{:S(2)}, u32[]{:S(2)}) collective-permute-start(bf16[272,256]{1,0:T(8,128)(2,1)S(1)} %collective-permute-done.17.refs_1_), channel_id=1, source_target_pairs={{0,2},{2,0},{1,3},{3,1},{4,6},{6,4},{5,7},{7,5},{8,10},{10,8},{9,1... | collective-permute-start | bytes 417800 | tf_op jit(solution)/shard_map/ppermute | solution.py:628

commit v3 on v2

--- a/solution.py
+++ b/solution.py
@@ -19,6 +19,7 @@
 F32 = jnp.float32
 VMEM_LIMIT = 16 * 1024 * 1024
 MASK_ROWS = 16
+PARTS = 2
 
 
 def nn(left, right):
@@ -344,61 +345,69 @@
 
     my_place = lax.axis_index("seq") * rows
 
-    valid = jnp.where(row_of((rows, width)) + my_place < length, 1.0, 0.0)
-
-    def add(slot, matrix):
-        acc[slot] = eight_sum(matrix)
-
-    attn_out = nn(attended_low[...], wo[...]) + bias_o[...]
-    unit, inverse = norm_parts(stream[...] + attn_out)
-    unit_one[...] = unit
-    inverse_one[...] = jnp.broadcast_to(inverse, (rows, SLOT))
-    normed = unit * gain_one[...] + shift_one[...]
-    narrow_b[...] = normed
-    normed_low[...] = normed.astype(BF)
-    add(8, stream[...] * stream[...] * valid)
-    add(9, attn_out * attn_out * valid)
-
-    active, slope = gelu_parts(nn(normed_low[...], w1[...]) + bias_1[...])
-    active_low[...] = active.astype(BF)
-    wide_b[...] = slope
-
-    branch = nn(active_low[...], w2[...]) + bias_2[...]
-    unit, inverse = norm_parts(narrow_b[...] + branch)
-    result_out[...] = unit * gain_two[...] + shift_two[...]
-    grad_result = cotangent[...] * valid
-    grad_second = norm_back(grad_result * gain_two[...], unit, inverse)
-    narrow_b[...] = grad_second
-    branch_bf = grad_second.astype(BF)
-    branch_low[...] = branch_bf
-    add(0, grad_result * unit)
-    add(1, grad_result)
-    add(10, branch * branch * valid)
-
-    hidden_bf = (nt(branch_low[...], w2[...]) * wide_b[...]).astype(BF)
-    hidden_low[...] = hidden_bf
-
-    grad_normed = narrow_b[...] + nt(hidden_low[...], w1[...])
-    unit = unit_one[...]
-    grad_first = norm_back(grad_normed * gain_one[...], unit, inverse_one[:, :1])
-    first_out[...] = grad_first
-    attn_bf = grad_first.astype(BF)
-    attn_low[...] = attn_bf
-    add(5, grad_normed * unit)
-    add(6, grad_normed)
-
-    do_wide = nt(attn_low[...], wo[...]).astype(BF).astype(F32)
-    for head in range(HEADS):
-        cols = head_cols(head)
-        do_head = do_wide[:, cols]
-        row_dot = jnp.sum(do_head * attended_wide[:, cols], axis=1, keepdims=True)
-        lane = lane_of(do_head.shape)
-        for scale, do_out in zip(scales, do_outs):
-            factor = scale[:, cols]
-            dot = -row_dot * factor
-            rest = dot - dot.astype(BF).astype(F32)
-            scaled = jnp.where(lane == HEAD_DIM, dot, do_head * factor)
-            do_out[:, cols] = jnp.where(lane == HEAD_DIM + 1, rest, scaled).astype(BF)
+    def part_steps(part):
+        count = rows // PARTS
+        span = slice(part * count, (part + 1) * count)
+        place = row_of((count, width)) + (my_place + part * count)
+        valid = jnp.where(place < length, 1.0, 0.0)
+
+        def add(slot, matrix):
+            sums = eight_sum(matrix)
+            acc[slot] = acc[slot] + sums if part else sums
+
+        attn_out = nn(attended_low[span, :], wo[...]) + bias_o[...]
+        unit, inverse = norm_parts(stream[span, :] + attn_out)
+        unit_one[span, :] = unit
+        inverse_one[span, :] = jnp.broadcast_to(inverse, (count, SLOT))
+        normed = unit * gain_one[...] + shift_one[...]
+        narrow_b[span, :] = normed
+        normed_low[span, :] = normed.astype(BF)
+        add(8, stream[span, :] * stream[span, :] * valid)
+        add(9, attn_out * attn_out * valid)
+        yield
+        active, slope = gelu_parts(nn(normed_low[span, :], w1[...]) + bias_1[...])
+        active_low[span, :] = active.astype(BF)
+        wide_b[span, :] = slope
+        yield
+        branch = nn(active_low[span, :], w2[...]) + bias_2[...]
+        unit, inverse = norm_parts(narrow_b[span, :] + branch)
+        result_out[span, :] = unit * gain_two[...] + shift_two[...]
+        grad_result = cotangent[span, :] * valid
+        grad_second = norm_back(grad_result * gain_two[...], unit, inverse)
+        narrow_b[span, :] = grad_second
+        branch_low[span, :] = grad_second.astype(BF)
+        add(0, grad_result * unit)
+        add(1, grad_result)
+        add(10, branch * branch * valid)
+        yield
+        hidden_low[span, :] = (nt(branch_low[span, :], w2[...]) * wide_b[span, :]).astype(BF)
+        yield
+        grad_normed = narrow_b[span, :] + nt(hidden_low[span, :], w1[...])
+        unit = unit_one[span, :]
+        grad_first = norm_back(grad_normed * gain_one[...], unit, inverse_one[span, :1])
+        first_out[span, :] = grad_first
+        attn_low[span, :] = grad_first.astype(BF)
+        add(5, grad_normed * unit)
+        add(6, grad_normed)
+        yield
+        do_wide = nt(attn_low[span, :], wo[...]).astype(BF).astype(F32)
+        for head in range(HEADS):
+            cols = head_cols(head)
+            do_head = do_wide[:, cols]
+            row_dot = jnp.sum(do_head * attended_wide[span, cols], axis=1, keepdims=True)
+            lane = lane_of(do_head.shape)
+            for scale, do_out in zip(scales, do_outs):
+                factor = scale[span, cols]
+                dot = -row_dot * factor
+                rest = dot - dot.astype(BF).astype(F32)
+                scaled = jnp.where(lane == HEAD_DIM, dot, do_head * factor)
+                do_out[span, cols] = jnp.where(lane == HEAD_DIM + 1, rest, scaled).astype(BF)
+        yield
+
+    parts = [part_steps(part) for part in range(PARTS)]
+    for _ in range(6):
+        for part in parts:
+            next(part)
 
     ones = jnp.ones((8, rows), BF)
     hidden_sum = nn(ones, hidden_low[...])[0:1]

time: 76 us -> 76.2 us (level)
  no operation moved by 1% of the time
where the time goes in v3:
time: 76.2 us; the launch traced here: 76.1 us
  Pallas kernels  35.9 us (47%)
  starting transfers between devices  25.2 us (33%)
  waiting for transfers between devices  11.5 us (15%)
  other arithmetic  1.21 us (2%)
  between operations  1.2 us (2%)
  local copies, waits for them, and re-layouts  1.12 us (1%)
    pallas_call x11, Pallas kernels, call(): pl.pallas_call(kernel, in_specs=[smem if a.ndim == 1 else vmem for a in i...  33.4 us
    ppermute x20, starting transfers between devices, swap(): lax.ppermute(block, axes, [(i, i ^ step) for i in range(lax.axis_size(axe...  20 us
    ppermute x20, waiting for transfers between devices, swap(): lax.ppermute(block, axes, [(i, i ^ step) for i in range(lax.axis_size(axe...  11.3 us
    ppermute x4, starting transfers between devices, send(): return lax.ppermute(block, 'seq', route)  5.16 us
    pallas_call x2, Pallas kernels, body(): pl.pallas_call(functools.partial(select_kernel, cell, carry), in_specs=[p...  2.48 us
  transfers between devices with their start and end apart: 24, of which 11 were waited for; matrix products, arithmetic and copies ran while one was open for 2% of the time, Pallas kernels for 40%

profile of v3, /device:TPU:0, one launch (start us, length us, event | category | flops | bytes accessed | tf_op | source)
XLA Modules:
  0.0 76.1 jit_solution(1863436055356611212)
XLA Ops:
  0.7 1.3 %shard_map.339 = (f32[512,256]{1,0:T(8,128)S(1)}, bf16[512,256]{1,0:T(8,128)(2,1)S(1)}) custom-call(f32[2,512,256]{2,1,0:T(8,128)} %tokens.3, s32[2,512]{1,0:T(2,128)} %masks.2, f32[1,256]{1,0:T(1,128)} %bitcast.47), custom_call_target="tpu_custom_call" | custom-call | tf_op jit(solution)/shard_map/pallas_call | solution.py:697
  2.0 3.0 %collective-permute-start.1 = (bf16[512,256]{1,0:T(8,128)(2,1)S(1)}, bf16[512,256]{1,0:T(8,128)(2,1)S(1)}, u32[]{:S(2)}, u32[]{:S(2)}) collective-permute-start(bf16[512,256]{1,0:T(8,128)(2,1)S(1)} %get-tuple-element.151.refs_0_.sent), channel_id=1, source_target_pairs={{0,1},{1,0},{2,3},{3,2},{4,5},{5,4},{6,7},{7,6},{8,9},{9,8},{10,11... | collective-permute-start | bytes 786440 | tf_op jit(solution)/shard_map/ppermute | solution.py:629
  5.0 1.2 %shard_map.340 = (f32[512,256]{1,0:T(8,128)S(1)}, bf16[512,256]{1,0:T(8,128)(2,1)S(1)}, bf16[528,256]{1,0:T(8,128)(2,1)S(1)}) custom-call(f32[2,512,256]{2,1,0:T(8,128)} %tokens.3, s32[2,512]{1,0:T(2,128)} %masks.2, f32[1,256]{1,0:T(1,128)} %bitcast.48), custom_call_target="tpu_custom_call" | custom-call | tf_op jit(solution)/shard_map/pallas_call | solution.py:697
  6.3 4.7 %shard_map.341 = (bf16[512,512]{1,0:T(8,128)(2,1)S(1)}, bf16[512,512]{1,0:T(8,128)(2,1)S(1)}, bf16[512,512]{1,0:T(8,128)(2,1)S(1)}, bf16[2048,512]{1,0:T(8,128)(...) custom-call(s32[2]{0:T(128)S(1)} %copy-done.15, ...), custom_call_target="tpu_custom_call" | custom-call | flops 2147483648 | bytes 13895688 | tf_op jit(solution)/shard_map/pallas_call | solution.py:614
  11.1 0.1 collective-permute-start
  11.2 0.1 slice_bitcast_fusion
  11.3 0.7 copy-done
  12.1 0.2 copy-done.1
  12.3 6.7 %shard_map.342 = (bf16[512,512]{1,0:T(8,128)(2,1)S(1)}, bf16[512,512]{1,0:T(8,128)(2,1)S(1)}, f32[512,256]{1,0:T(8,128)S(1)}, bf16[512,512]{1,0:T(8,128)(2,1)S(1...) custom-call(s32[2]{0:T(128)S(1)} %copy-done.15, ...), custom_call_target="tpu_custom_call" | custom-call | flops 3758096384 | bytes 13919240 | tf_op jit(solution)/shard_map/pallas_call | solution.py:614
  19.1 0.1 collective-permute-done.carrier.x
  19.2 2.7 %shard_map.343 = (f32[512,512]{1,0:T(8,128)S(1)}, bf16[512,256]{1,0:T(8,128)(2,1)S(1)}, f32[512,256]{1,0:T(8,128)S(1)}, f32[256,128]{1,0:T(8,128)S(1)}, f32[8,512]{1,0:T(8,128)S(1)}) custom-call(bf16[512,256]{1,0:T(8,128)(2,1)S(1)} %get-tuple-element.164.sent, bf16[528,256]{1,0:T(8,128)(2,1)S(1)} %collective-permute-done.carrier.x, ...), custom_call_target="tpu_custom_call" | custom-call | flops 2684354560 | bytes 6971392 | tf_op jit(solution)/shard_map/pallas_call | solution.py:614
  21.8 1.0 %collective-permute-start.2 = (bf16[512,256]{1,0:T(8,128)(2,1)S(1)}, bf16[512,256]{1,0:T(8,128)(2,1)S(1)}, u32[]{:S(2)}, u32[]{:S(2)}) collective-permute-start(bf16[512,256]{1,0:T(8,128)(2,1)S(1)} %get-tuple-element.182), channel_id=1, source_target_pairs={{0,1},{1,0},{2,3},{3,2},{4,5},{5,4},{6,7},{7,6},{8,9},{9,8},{10,11... | collective-permute-start | bytes 786440 | tf_op jit(solution)/shard_map/ppermute | solution.py:629
  22.8 6.9 %shard_map.344 = (bf16[512,512]{1,0:T(8,128)(2,1)S(1)}, bf16[512,512]{1,0:T(8,128)(2,1)S(1)}, f32[512,256]{1,0:T(8,128)S(1)}, bf16[512,512]{1,0:T(8,128)(2,1)S(1...) custom-call(s32[2]{0:T(128)S(1)} %copy-done.15, ...), custom_call_target="tpu_custom_call" | custom-call | flops 3758096384 | bytes 13288456 | tf_op jit(solution)/shard_map/pallas_call | solution.py:614
  29.7 0.1 collective-permute-start.3
  29.8 2.5 %shard_map.345 = (f32[512,512]{1,0:T(8,128)S(1)}, bf16[512,256]{1,0:T(8,128)(2,1)S(1)}, f32[512,256]{1,0:T(8,128)S(1)}, f32[256,128]{1,0:T(8,128)S(1)}, f32[8,512]{1,0:T(8,128)S(1)}) custom-call(bf16[512,256]{1,0:T(8,128)(2,1)S(1)} %get-tuple-element.181.sent, bf16[528,256]{1,0:T(8,128)(2,1)S(1)} %collective-permute-done.carrier.x, ...), custom_call_target="tpu_custom_call" | custom-call | flops 2684354560 | bytes 7643136 | tf_op jit(solution)/shard_map/pallas_call | solution.py:614
  32.3 0.1 shard_map.346
  32.4 1.1 %collective-permute-start.4 = (bf16[160,256]{1,0:T(8,128)(2,1)S(1)}, bf16[160,256]{1,0:T(8,128)(2,1)S(1)}, u32[]{:S(2)}, u32[]{:S(2)}) collective-permute-start(bf16[160,256]{1,0:T(8,128)(2,1)S(1)} %get-tuple-element.215), channel_id=1, source_target_pairs={{0,1},{1,0},{4,5},{5,4},{2,3},{3,2},{6,7},{7,6},{8,9},{9,8},{12,13... | collective-permute-start | bytes 245768 | tf_op jit(solution)/shard_map/ppermute | solution.py:637
  33.5 1.5 %collective-permute-start.5 = (bf16[160,256]{1,0:T(8,128)(2,1)S(1)}, bf16[160,256]{1,0:T(8,128)(2,1)S(1)}, u32[]{:S(2)}, u32[]{:S(2)}) collective-permute-start(bf16[160,256]{1,0:T(8,128)(2,1)S(1)} %get-tuple-element.216), channel_id=1, source_target_pairs={{0,4},{1,5},{4,0},{5,1},{2,6},{3,7},{6,2},{7,3},{8,12},{9,13},{12,... | collective-permute-start | bytes 245768 | tf_op jit(solution)/shard_map/ppermute | solution.py:637
  35.0 1.0 %collective-permute-start.6 = (bf16[160,256]{1,0:T(8,128)(2,1)S(1)}, bf16[160,256]{1,0:T(8,128)(2,1)S(1)}, u32[]{:S(2)}, u32[]{:S(2)}) collective-permute-start(bf16[160,256]{1,0:T(8,128)(2,1)S(1)} %get-tuple-element.217), channel_id=1, source_target_pairs={{0,5},{1,4},{4,1},{5,0},{2,7},{3,6},{6,3},{7,2},{8,13},{9,12},{12,... | collective-permute-start | bytes 245768 | tf_op jit(solution)/shard_map/ppermute | solution.py:637
  35.9 3.0 %shard_map.347 = (f32[512,256]{1,0:T(8,128)S(1)}, f32[512,256]{1,0:T(8,128)S(1)}, f32[256,128]{1,0:T(8,128)S(1)}, f32[8,512]{1,0:T(8,128)S(1)}, f32[256,512]{1,0:T(8,128)S(1)}) custom-call(bf16[512,256]{1,0:T(8,128)(2,1)S(1)} %get-tuple-element.151.refs_0_.sent, bf16[528,256]{1,0:T(8,128)(2,1)S(1)} %get-tuple-element.155.carrier.sent, ...), custom_call_target="tpu_custom_call" | custom-call | flops 1 | bytes 1 | tf_op jit(solution)/shard_map/pallas_call | solution.py:614
  39.0 1.3 %collective-permute-done.6 = bf16[160,256]{1,0:T(8,128)(2,1)S(1)} collective-permute-done((bf16[160,256]{1,0:T(8,128)(2,1)S(1)}, bf16[160,256]{1,0:T(8,128)(2,1)S(1)}, u32[]{:S(2)}, u32[]{:S(2)}) %collective-permute-start.6) | collective-permute-done | bytes 81952 | tf_op jit(solution)/shard_map/ppermute | solution.py:637
  40.4 1.7 %collective-permute-start.7 = (bf16[160,256]{1,0:T(8,128)(2,1)S(1)}, bf16[160,256]{1,0:T(8,128)(2,1)S(1)}, u32[]{:S(2)}, u32[]{:S(2)}) collective-permute-start(bf16[160,256]{1,0:T(8,128)(2,1)S(1)} %add_convert_fusion.2), channel_id=1, source_target_pairs={{0,8},{8,0},{16,24},{24,16},{1,9},{9,1},{17,25},{25,17},{2,10},{10... | collective-permute-start | bytes 245768 | tf_op jit(solution)/shard_map/ppermute | solution.py:637
  42.0 3.8 %shard_map.348 = (f32[512,256]{1,0:T(8,128)S(1)}, bf16[448,256]{1,0:T(8,128)(2,1)S(1)}, bf16[448,256]{1,0:T(8,128)(2,1)S(1)}) custom-call(bf16[528,256]{1,0:T(8,128)(2,1)S(1)} %get-tuple-element.155.carrier.sent, bf16[528,256]{1,0:T(8,128)(2,1)S(1)} %get-tuple-element.155.carrier.sent, bf16[512,512]{1,0:T(8,128)(2,1)S(1)} %get-tuple-element.183.q, ...), custom_call_target="tpu_custom_call" | custom-call | flops 1 | bytes 1 | tf_op jit(solution)/shard_map/pallas_call | solution.py:614
  45.8 0.1 collective-permute-start.8
  45.9 2.7 %collective-permute-start.12 = (bf16[160,256]{1,0:T(8,128)(2,1)S(1)}, bf16[160,256]{1,0:T(8,128)(2,1)S(1)}, u32[]{:S(2)}, u32[]{:S(2)}) collective-permute-start(bf16[160,256]{1,0:T(8,128)(2,1)S(1)} %add_convert_fusion.1), channel_id=1, source_target_pairs={{0,16},{8,24},{16,0},{24,8},{1,17},{9,25},{17,1},{25,9},{2,18},{10... | collective-permute-start | bytes 245768 | tf_op jit(solution)/shard_map/ppermute | solution.py:637
  48.6 1.0 %collective-permute-start.9 = (bf16[112,256]{1,0:T(8,128)(2,1)S(1)}, bf16[112,256]{1,0:T(8,128)(2,1)S(1)}, u32[]{:S(2)}, u32[]{:S(2)}) collective-permute-start(bf16[112,256]{1,0:T(8,128)(2,1)S(1)} %get-tuple-element.236), channel_id=1, source_target_pairs={{0,1},{1,0},{4,5},{5,4},{2,3},{3,2},{6,7},{7,6},{8,9},{9,8},{12,13... | collective-permute-start | bytes 172040 | tf_op jit(solution)/shard_map/ppermute | solution.py:637
  49.7 1.5 %collective-permute-start.10 = (bf16[112,256]{1,0:T(8,128)(2,1)S(1)}, bf16[112,256]{1,0:T(8,128)(2,1)S(1)}, u32[]{:S(2)}, u32[]{:S(2)}) collective-permute-start(bf16[112,256]{1,0:T(8,128)(2,1)S(1)} %get-tuple-element.237), channel_id=1, source_target_pairs={{0,4},{1,5},{4,0},{5,1},{2,6},{3,7},{6,2},{7,3},{8,12},{9,13},{12,... | collective-permute-start | bytes 172040 | tf_op jit(solution)/shard_map/ppermute | solution.py:637
  51.1 1.1 %collective-permute-start.11 = (bf16[112,256]{1,0:T(8,128)(2,1)S(1)}, bf16[112,256]{1,0:T(8,128)(2,1)S(1)}, u32[]{:S(2)}, u32[]{:S(2)}) collective-permute-start(bf16[112,256]{1,0:T(8,128)(2,1)S(1)} %get-tuple-element.238), channel_id=1, source_target_pairs={{0,5},{1,4},{4,1},{5,0},{2,7},{3,6},{6,3},{7,2},{8,13},{9,12},{12,... | collective-permute-start | bytes 172040 | tf_op jit(solution)/shard_map/ppermute | solution.py:637
  52.2 1.3 %collective-permute-done.12 = bf16[160,256]{1,0:T(8,128)(2,1)S(1)} collective-permute-done((bf16[160,256]{1,0:T(8,128)(2,1)S(1)}, bf16[160,256]{1,0:T(8,128)(2,1)S(1)}, u32[]{:S(2)}, u32[]{:S(2)}) %collective-permute-start.12) | collective-permute-done | bytes 81952 | tf_op jit(solution)/shard_map/ppermute | solution.py:637
  53.5 0.5 collective-permute-done.10
  54.0 2.2 %collective-permute-done.11 = bf16[112,256]{1,0:T(8,128)(2,1)S(1)} collective-permute-done((bf16[112,256]{1,0:T(8,128)(2,1)S(1)}, bf16[112,256]{1,0:T(8,128)(2,1)S(1)}, u32[]{:S(2)}, u32[]{:S(2)}) %collective-permute-start.11) | collective-permute-done | bytes 57376 | tf_op jit(solution)/shard_map/ppermute | solution.py:637
  56.3 1.1 %collective-permute-start.16 = (bf16[512,256]{1,0:T(8,128)(2,1)S(1)}, bf16[512,256]{1,0:T(8,128)(2,1)S(1)}, u32[]{:S(2)}, u32[]{:S(2)}) collective-permute-start(bf16[512,256]{1,0:T(8,128)(2,1)S(1)} %get-tuple-element.247), channel_id=1, source_target_pairs={{0,1},{1,0},{2,3},{3,2},{4,5},{5,4},{6,7},{7,6},{8,9},{9,8},{10,11... | collective-permute-start | bytes 786440 | tf_op jit(solution)/shard_map/ppermute | solution.py:629
  57.3 1.4 %collective-permute-start.15 = (bf16[112,256]{1,0:T(8,128)(2,1)S(1)}, bf16[112,256]{1,0:T(8,128)(2,1)S(1)}, u32[]{:S(2)}, u32[]{:S(2)}) collective-permute-start(bf16[112,256]{1,0:T(8,128)(2,1)S(1)} %add_convert_fusion.4), channel_id=1, source_target_pairs={{0,24},{8,16},{16,8},{24,0},{1,25},{9,17},{17,9},{25,1},{2,26},{10... | collective-permute-start | bytes 172040 | tf_op jit(solution)/shard_map/ppermute | solution.py:637
  58.7 0.6 collective-permute-start.14
  59.3 2.4 %collective-permute-start.13 = (bf16[112,256]{1,0:T(8,128)(2,1)S(1)}, bf16[112,256]{1,0:T(8,128)(2,1)S(1)}, u32[]{:S(2)}, u32[]{:S(2)}) collective-permute-start(bf16[112,256]{1,0:T(8,128)(2,1)S(1)} %add_convert_fusion.4), channel_id=1, source_target_pairs={{0,8},{8,0},{16,24},{24,16},{1,9},{9,1},{17,25},{25,17},{2,10},{10... | collective-permute-start | bytes 172040 | tf_op jit(solution)/shard_map/ppermute | solution.py:637
  61.7 1.6 %collective-permute-done.15 = bf16[112,256]{1,0:T(8,128)(2,1)S(1)} collective-permute-done((bf16[112,256]{1,0:T(8,128)(2,1)S(1)}, bf16[112,256]{1,0:T(8,128)(2,1)S(1)}, u32[]{:S(2)}, u32[]{:S(2)}) %collective-permute-start.15) | collective-permute-done | bytes 57376 | tf_op jit(solution)/shard_map/ppermute | solution.py:637
  63.3 1.2 %collective-permute-done.14 = bf16[112,256]{1,0:T(8,128)(2,1)S(1)} collective-permute-done((bf16[112,256]{1,0:T(8,128)(2,1)S(1)}, bf16[112,256]{1,0:T(8,128)(2,1)S(1)}, u32[]{:S(2)}, u32[]{:S(2)}) %collective-permute-start.14) | collective-permute-done | bytes 57376 | tf_op jit(solution)/shard_map/ppermute | solution.py:637
  64.6 1.1 %collective-permute-start.17 = (bf16[272,256]{1,0:T(8,128)(2,1)S(1)}, bf16[272,256]{1,0:T(8,128)(2,1)S(1)}, u32[]{:S(2)}, u32[]{:S(2)}) collective-permute-start(bf16[272,256]{1,0:T(8,128)(2,1)S(1)} %pad_maximum_fusion.1.refs_0_), channel_id=1, source_target_pairs={{0,1},{1,0},{4,5},{5,4},{2,3},{3,2},{6,7},{7,6},{8,9},{9,8},{12,13... | collective-permute-start | bytes 417800 | tf_op jit(solution)/shard_map/ppermute | solution.py:637
  65.7 1.1 %collective-permute-start.19 = (bf16[272,256]{1,0:T(8,128)(2,1)S(1)}, bf16[272,256]{1,0:T(8,128)(2,1)S(1)}, u32[]{:S(2)}, u32[]{:S(2)}) collective-permute-start(bf16[272,256]{1,0:T(8,128)(2,1)S(1)} %pad_maximum_fusion.1.refs_0_), channel_id=1, source_target_pairs={{0,5},{1,4},{4,1},{5,0},{2,7},{3,6},{6,3},{7,2},{8,13},{9,12},{12,... | collective-permute-start | bytes 417800 | tf_op jit(solution)/shard_map/ppermute | solution.py:637
  66.8 1.3 %collective-permute-start.18 = (bf16[272,256]{1,0:T(8,128)(2,1)S(1)}, bf16[272,256]{1,0:T(8,128)(2,1)S(1)}, u32[]{:S(2)}, u32[]{:S(2)}) collective-permute-start(bf16[272,256]{1,0:T(8,128)(2,1)S(1)} %pad_maximum_fusion.1.refs_0_), channel_id=1, source_target_pairs={{0,4},{1,5},{4,0},{5,1},{2,6},{3,7},{6,2},{7,3},{8,12},{9,13},{12,... | collective-permute-start | bytes 417800 | tf_op jit(solution)/shard_map/ppermute | solution.py:637
  68.1 1.0 %pad_maximum_fusion = f32[2,512,256]{2,1,0:T(8,128)} fusion(f32[1,512,256]{2,1,0:T(8,128)S(1)} %bitcast.28, f32[1,512,256]{2,1,0:T(8,128)S(1)} %bitcast.27), kind=kLoop, calls=%fused_computation | loop fusion | flops 262144 | bytes 2097152 | tf_op jit(solution)/shard_map/stack | solution.py:914
  69.2 1.4 %shard_map.350 = f32[2,512,256]{2,1,0:T(8,128)} custom-call(bf16[528,256]{1,0:T(8,128)(2,1)S(1)} %get-tuple-element.155.carrier.sent, f32[512,256]{1,0:T(8,128)S(1)} %get-tuple-element.251.refs_0_, f32[512,256]{1,0:T(8,128)S(1)} %get-tuple-element.252.refs_1_, bf16[512,256]{1,0:T(8,128)(2,1)S(1)} %collective-permute-done.2.refs_2_, ...), custom_call_target="tpu_custom_call" | custom-call | bytes 2891776 | tf_op jit(solution)/shard_map/pallas_call | solution.py:614
  70.6 1.1 %collective-permute-done.19.refs_3_ = bf16[272,256]{1,0:T(8,128)(2,1)S(1)} collective-permute-done((bf16[272,256]{1,0:T(8,128)(2,1)S(1)}, bf16[272,256]{1,0:T(8,128)(2,1)S(1)}, u32[]{:S(2)}, u32[]{:S(2)}) %collective-permute-start.19) | collective-permute-done | bytes 139296 | tf_op jit(solution)/shard_map/ppermute | solution.py:637
  71.6 1.0 %collective-permute-done.18.refs_2_ = bf16[272,256]{1,0:T(8,128)(2,1)S(1)} collective-permute-done((bf16[272,256]{1,0:T(8,128)(2,1)S(1)}, bf16[272,256]{1,0:T(8,128)(2,1)S(1)}, u32[]{:S(2)}, u32[]{:S(2)}) %collective-permute-start.18) | collective-permute-done | bytes 139296 | tf_op jit(solution)/shard_map/ppermute | solution.py:637
  72.7 0.5 collective-permute-start.21
  73.2 0.8 %collective-permute-done.22.refs_6_ = bf16[272,256]{1,0:T(8,128)(2,1)S(1)} collective-permute-done((bf16[272,256]{1,0:T(8,128)(2,1)S(1)}, bf16[272,256]{1,0:T(8,128)(2,1)S(1)}, u32[]{:S(2)}, u32[]{:S(2)}) %collective-permute-start.22) | collective-permute-done | bytes 139296 | tf_op jit(solution)/shard_map/ppermute | solution.py:637
  74.0 0.2 collective-permute-done.21.refs_5_
  74.2 1.7 %shard_map.351 = (f32[256,256]{1,0:T(8,128)}, f32[256,512]{1,0:T(8,128)}, f32[512,256]{1,0:T(8,128)}, f32[256,256]{1,0:T(8,128)}, f32[256,256]{1,0:T(8,128)}, /*...) custom-call(bf16[272,256]{1,0:T(8,128)(2,1)S(1)} %pad_maximum_fusion, ...), custom_call_target="tpu_custom_call" | custom-call | bytes 3222540 | tf_op jit(solution)/shard_map/pallas_call | solution.py:614
  (55 shorter events, 0.4 us)
Async XLA Ops:
  0.7 5.6 %copy-start.15 = (s32[2]{0:T(128)S(1)}, s32[2]{0:T(128)}, u32[]{:S(2)}) copy-start(s32[2]{0:T(128)} %lengths.5) | copy-start | bytes 28
  0.7 5.6 %copy-start.8 = (f32[256]{0:T(256)S(1)}, f32[256]{0:T(256)}, u32[]{:S(2)}) copy-start(f32[256]{0:T(256)} %param.29) | copy-start | bytes 3076
  0.7 5.6 %copy-start.4 = (f32[256,256]{1,0:T(8,128)S(1)}, f32[256,256]{1,0:T(8,128)}, u32[]{:S(2)}) copy-start(f32[256,256]{1,0:T(8,128)} %refs_4_.1) | copy-start | bytes 786436
  0.7 5.6 %copy-start.3 = (f32[256,256]{1,0:T(8,128)S(1)}, f32[256,256]{1,0:T(8,128)}, u32[]{:S(2)}) copy-start(f32[256,256]{1,0:T(8,128)} %refs_3_.1) | copy-start | bytes 786436
  0.7 5.6 %copy-start.7 = (f32[256]{0:T(256)S(1)}, f32[256]{0:T(256)}, u32[]{:S(2)}) copy-start(f32[256]{0:T(256)} %param.26) | copy-start | bytes 3076
  0.7 5.6 %copy-start.2 = (f32[256,256]{1,0:T(8,128)S(1)}, f32[256,256]{1,0:T(8,128)}, u32[]{:S(2)}) copy-start(f32[256,256]{1,0:T(8,128)} %refs_2_.1) | copy-start | bytes 786436
  2.0 9.3 %collective-permute-start.1 = (bf16[512,256]{1,0:T(8,128)(2,1)S(1)}, bf16[512,256]{1,0:T(8,128)(2,1)S(1)}, u32[]{:S(2)}, u32[]{:S(2)}) collective-permute-start(bf16[512,256]{1,0:T(8,128)(2,1)S(1)} %get-tuple-element.151.refs_0_.sent), channel_id=1, source_target_pairs={{0,1},{1,0},{2,3},{3,2},{4,5},{5,4},{6,7},{7,6},{8,9},{9,8},{10,11... | collective-permute-start | bytes 786440 | tf_op jit(solution)/shard_map/ppermute | solution.py:629
  6.3 4.9 %copy-start.16 = (f32[2,512,256]{2,1,0:T(8,128)S(1)}, f32[2,512,256]{2,1,0:T(8,128)}, u32[]{:S(2)}) copy-start(f32[2,512,256]{2,1,0:T(8,128)} %param.23) | copy-start | bytes 3145732
  11.0 1.0 %copy-start = (f32[256,512]{1,0:T(8,128)S(1)}, f32[256,512]{1,0:T(8,128)}, u32[]{:S(2)}) copy-start(f32[256,512]{1,0:T(8,128)} %w1_in.1) | copy-start | bytes 1572868
  11.0 1.2 %copy-start.1 = (f32[512,256]{1,0:T(8,128)S(1)}, f32[512,256]{1,0:T(8,128)}, u32[]{:S(2)}) copy-start(f32[512,256]{1,0:T(8,128)} %w2_in.1) | copy-start | bytes 1572868
  11.1 1.2 %copy-start.5 = (f32[256,256]{1,0:T(8,128)S(1)}, f32[256,256]{1,0:T(8,128)}, u32[]{:S(2)}) copy-start(f32[256,256]{1,0:T(8,128)} %wo_in.1) | copy-start | bytes 786436
  11.1 1.2 %copy-start.6 = (f32[512]{0:T(512)S(1)}, f32[512]{0:T(512)}, u32[]{:S(2)}) copy-start(f32[512]{0:T(512)} %param.35) | copy-start | bytes 6148
  11.1 1.2 %copy-start.9 = (f32[256]{0:T(256)S(1)}, f32[256]{0:T(256)}, u32[]{:S(2)}) copy-start(f32[256]{0:T(256)} %param.31) | copy-start | bytes 3076
  11.1 1.2 %copy-start.10 = (f32[256]{0:T(256)S(1)}, f32[256]{0:T(256)}, u32[]{:S(2)}) copy-start(f32[256]{0:T(256)} %param.32) | copy-start | bytes 3076
  11.1 1.2 %copy-start.11 = (f32[256]{0:T(256)S(1)}, f32[256]{0:T(256)}, u32[]{:S(2)}) copy-start(f32[256]{0:T(256)} %param.33) | copy-start | bytes 3076
  11.1 1.2 %copy-start.12 = (f32[256]{0:T(256)S(1)}, f32[256]{0:T(256)}, u32[]{:S(2)}) copy-start(f32[256]{0:T(256)} %param.37) | copy-start | bytes 3076
  11.1 1.2 %copy-start.13 = (f32[256]{0:T(256)S(1)}, f32[256]{0:T(256)}, u32[]{:S(2)}) copy-start(f32[256]{0:T(256)} %param.38) | copy-start | bytes 3076
  11.1 1.2 %copy-start.14 = (f32[256]{0:T(256)S(1)}, f32[256]{0:T(256)}, u32[]{:S(2)}) copy-start(f32[256]{0:T(256)} %param.39) | copy-start | bytes 3076
  11.1 8.0 %collective-permute-start = (bf16[528,256]{1,0:T(8,128)(2,1)S(1)}, bf16[528,256]{1,0:T(8,128)(2,1)S(1)}, u32[]{:S(2)}, u32[]{:S(2)}) collective-permute-start(bf16[528,256]{1,0:T(8,128)(2,1)S(1)} %get-tuple-element.155.carrier.sent), channel_id=1, source_target_pairs={{0,1},{1,0},{2,3},{3,2},{4,5},{5,4},{6,7},{7,6},{8,9},{9,8},{10,11... | collective-permute-start | bytes 811016 | tf_op jit(solution)/shard_map/ppermute | solution.py:629
  21.8 7.9 %collective-permute-start.2 = (bf16[512,256]{1,0:T(8,128)(2,1)S(1)}, bf16[512,256]{1,0:T(8,128)(2,1)S(1)}, u32[]{:S(2)}, u32[]{:S(2)}) collective-permute-start(bf16[512,256]{1,0:T(8,128)(2,1)S(1)} %get-tuple-element.182), channel_id=1, source_target_pairs={{0,1},{1,0},{2,3},{3,2},{4,5},{5,4},{6,7},{7,6},{8,9},{9,8},{10,11... | collective-permute-start | bytes 786440 | tf_op jit(solution)/shard_map/ppermute | solution.py:629
  29.7 2.6 %collective-permute-start.3 = (bf16[640,256]{1,0:T(8,128)(2,1)S(1)}, bf16[640,256]{1,0:T(8,128)(2,1)S(1)}, u32[]{:S(2)}, u32[]{:S(2)}) collective-permute-start(bf16[640,256]{1,0:T(8,128)(2,1)S(1)} %get-tuple-element.196), channel_id=1, source_target_pairs={{0,2},{2,0},{1,3},{3,1},{4,6},{6,4},{5,7},{7,5},{8,10},{10,8},{9,1... | collective-permute-start | bytes 983048 | tf_op jit(solution)/shard_map/ppermute | solution.py:637
  32.4 6.6 %collective-permute-start.4 = (bf16[160,256]{1,0:T(8,128)(2,1)S(1)}, bf16[160,256]{1,0:T(8,128)(2,1)S(1)}, u32[]{:S(2)}, u32[]{:S(2)}) collective-permute-start(bf16[160,256]{1,0:T(8,128)(2,1)S(1)} %get-tuple-element.215), channel_id=1, source_target_pairs={{0,1},{1,0},{4,5},{5,4},{2,3},{3,2},{6,7},{7,6},{8,9},{9,8},{12,13... | collective-permute-start | bytes 245768 | tf_op jit(solution)/shard_map/ppermute | solution.py:637
  33.5 5.5 %collective-permute-start.5 = (bf16[160,256]{1,0:T(8,128)(2,1)S(1)}, bf16[160,256]{1,0:T(8,128)(2,1)S(1)}, u32[]{:S(2)}, u32[]{:S(2)}) collective-permute-start(bf16[160,256]{1,0:T(8,128)(2,1)S(1)} %get-tuple-element.216), channel_id=1, source_target_pairs={{0,4},{1,5},{4,0},{5,1},{2,6},{3,7},{6,2},{7,3},{8,12},{9,13},{12,... | collective-permute-start | bytes 245768 | tf_op jit(solution)/shard_map/ppermute | solution.py:637
  35.0 5.3 %collective-permute-start.6 = (bf16[160,256]{1,0:T(8,128)(2,1)S(1)}, bf16[160,256]{1,0:T(8,128)(2,1)S(1)}, u32[]{:S(2)}, u32[]{:S(2)}) collective-permute-start(bf16[160,256]{1,0:T(8,128)(2,1)S(1)} %get-tuple-element.217), channel_id=1, source_target_pairs={{0,5},{1,4},{4,1},{5,0},{2,7},{3,6},{6,3},{7,2},{8,13},{9,12},{12,... | collective-permute-start | bytes 245768 | tf_op jit(solution)/shard_map/ppermute | solution.py:637
  40.4 5.4 %collective-permute-start.7 = (bf16[160,256]{1,0:T(8,128)(2,1)S(1)}, bf16[160,256]{1,0:T(8,128)(2,1)S(1)}, u32[]{:S(2)}, u32[]{:S(2)}) collective-permute-start(bf16[160,256]{1,0:T(8,128)(2,1)S(1)} %add_convert_fusion.2), channel_id=1, source_target_pairs={{0,8},{8,0},{16,24},{24,16},{1,9},{9,1},{17,25},{25,17},{2,10},{10... | collective-permute-start | bytes 245768 | tf_op jit(solution)/shard_map/ppermute | solution.py:637
  45.8 2.8 %collective-permute-start.8 = (bf16[448,256]{1,0:T(8,128)(2,1)S(1)}, bf16[448,256]{1,0:T(8,128)(2,1)S(1)}, u32[]{:S(2)}, u32[]{:S(2)}) collective-permute-start(bf16[448,256]{1,0:T(8,128)(2,1)S(1)} %get-tuple-element.235), channel_id=1, source_target_pairs={{0,2},{2,0},{1,3},{3,1},{4,6},{6,4},{5,7},{7,5},{8,10},{10,8},{9,1... | collective-permute-start | bytes 688136 | tf_op jit(solution)/shard_map/ppermute | solution.py:637
  45.9 7.6 %collective-permute-start.12 = (bf16[160,256]{1,0:T(8,128)(2,1)S(1)}, bf16[160,256]{1,0:T(8,128)(2,1)S(1)}, u32[]{:S(2)}, u32[]{:S(2)}) collective-permute-start(bf16[160,256]{1,0:T(8,128)(2,1)S(1)} %add_convert_fusion.1), channel_id=1, source_target_pairs={{0,16},{8,24},{16,0},{24,8},{1,17},{9,25},{17,1},{25,9},{2,18},{10... | collective-permute-start | bytes 245768 | tf_op jit(solution)/shard_map/ppermute | solution.py:637
  48.6 4.8 %collective-permute-start.9 = (bf16[112,256]{1,0:T(8,128)(2,1)S(1)}, bf16[112,256]{1,0:T(8,128)(2,1)S(1)}, u32[]{:S(2)}, u32[]{:S(2)}) collective-permute-start(bf16[112,256]{1,0:T(8,128)(2,1)S(1)} %get-tuple-element.236), channel_id=1, source_target_pairs={{0,1},{1,0},{4,5},{5,4},{2,3},{3,2},{6,7},{7,6},{8,9},{9,8},{12,13... | collective-permute-start | bytes 172040 | tf_op jit(solution)/shard_map/ppermute | solution.py:637
  49.7 4.3 %collective-permute-start.10 = (bf16[112,256]{1,0:T(8,128)(2,1)S(1)}, bf16[112,256]{1,0:T(8,128)(2,1)S(1)}, u32[]{:S(2)}, u32[]{:S(2)}) collective-permute-start(bf16[112,256]{1,0:T(8,128)(2,1)S(1)} %get-tuple-element.237), channel_id=1, source_target_pairs={{0,4},{1,5},{4,0},{5,1},{2,6},{3,7},{6,2},{7,3},{8,12},{9,13},{12,... | collective-permute-start | bytes 172040 | tf_op jit(solution)/shard_map/ppermute | solution.py:637
  51.1 5.1 %collective-permute-start.11 = (bf16[112,256]{1,0:T(8,128)(2,1)S(1)}, bf16[112,256]{1,0:T(8,128)(2,1)S(1)}, u32[]{:S(2)}, u32[]{:S(2)}) collective-permute-start(bf16[112,256]{1,0:T(8,128)(2,1)S(1)} %get-tuple-element.238), channel_id=1, source_target_pairs={{0,5},{1,4},{4,1},{5,0},{2,7},{3,6},{6,3},{7,2},{8,13},{9,12},{12,... | collective-permute-start | bytes 172040 | tf_op jit(solution)/shard_map/ppermute | solution.py:637
  56.3 8.3 %collective-permute-start.16 = (bf16[512,256]{1,0:T(8,128)(2,1)S(1)}, bf16[512,256]{1,0:T(8,128)(2,1)S(1)}, u32[]{:S(2)}, u32[]{:S(2)}) collective-permute-start(bf16[512,256]{1,0:T(8,128)(2,1)S(1)} %get-tuple-element.247), channel_id=1, source_target_pairs={{0,1},{1,0},{2,3},{3,2},{4,5},{5,4},{6,7},{7,6},{8,9},{9,8},{10,11... | collective-permute-start | bytes 786440 | tf_op jit(solution)/shard_map/ppermute | solution.py:629
  57.3 6.0 %collective-permute-start.15 = (bf16[112,256]{1,0:T(8,128)(2,1)S(1)}, bf16[112,256]{1,0:T(8,128)(2,1)S(1)}, u32[]{:S(2)}, u32[]{:S(2)}) collective-permute-start(bf16[112,256]{1,0:T(8,128)(2,1)S(1)} %add_convert_fusion.4), channel_id=1, source_target_pairs={{0,24},{8,16},{16,8},{24,0},{1,25},{9,17},{17,9},{25,1},{2,26},{10... | collective-permute-start | bytes 172040 | tf_op jit(solution)/shard_map/ppermute | solution.py:637
  58.7 5.8 %collective-permute-start.14 = (bf16[112,256]{1,0:T(8,128)(2,1)S(1)}, bf16[112,256]{1,0:T(8,128)(2,1)S(1)}, u32[]{:S(2)}, u32[]{:S(2)}) collective-permute-start(bf16[112,256]{1,0:T(8,128)(2,1)S(1)} %add_convert_fusion.4), channel_id=1, source_target_pairs={{0,16},{8,24},{16,0},{24,8},{1,17},{9,25},{17,1},{25,9},{2,18},{10... | collective-permute-start | bytes 172040 | tf_op jit(solution)/shard_map/ppermute | solution.py:637
  59.3 5.2 %collective-permute-start.13 = (bf16[112,256]{1,0:T(8,128)(2,1)S(1)}, bf16[112,256]{1,0:T(8,128)(2,1)S(1)}, u32[]{:S(2)}, u32[]{:S(2)}) collective-permute-start(bf16[112,256]{1,0:T(8,128)(2,1)S(1)} %add_convert_fusion.4), channel_id=1, source_target_pairs={{0,8},{8,0},{16,24},{24,16},{1,9},{9,1},{17,25},{25,17},{2,10},{10... | collective-permute-start | bytes 172040 | tf_op jit(solution)/shard_map/ppermute | solution.py:637
  64.6 6.0 %collective-permute-start.17 = (bf16[272,256]{1,0:T(8,128)(2,1)S(1)}, bf16[272,256]{1,0:T(8,128)(2,1)S(1)}, u32[]{:S(2)}, u32[]{:S(2)}) collective-permute-start(bf16[272,256]{1,0:T(8,128)(2,1)S(1)} %pad_maximum_fusion.1.refs_0_), channel_id=1, source_target_pairs={{0,1},{1,0},{4,5},{5,4},{2,3},{3,2},{6,7},{7,6},{8,9},{9,8},{12,13... | collective-permute-start | bytes 417800 | tf_op jit(solution)/shard_map/ppermute | solution.py:637
  65.7 6.0 %collective-permute-start.19 = (bf16[272,256]{1,0:T(8,128)(2,1)S(1)}, bf16[272,256]{1,0:T(8,128)(2,1)S(1)}, u32[]{:S(2)}, u32[]{:S(2)}) collective-permute-start(bf16[272,256]{1,0:T(8,128)(2,1)S(1)} %pad_maximum_fusion.1.refs_0_), channel_id=1, source_target_pairs={{0,5},{1,4},{4,1},{5,0},{2,7},{3,6},{6,3},{7,2},{8,13},{9,12},{12,... | collective-permute-start | bytes 417800 | tf_op jit(solution)/shard_map/ppermute | solution.py:637
  66.8 5.9 %collective-permute-start.18 = (bf16[272,256]{1,0:T(8,128)(2,1)S(1)}, bf16[272,256]{1,0:T(8,128)(2,1)S(1)}, u32[]{:S(2)}, u32[]{:S(2)}) collective-permute-start(bf16[272,256]{1,0:T(8,128)(2,1)S(1)} %pad_maximum_fusion.1.refs_0_), channel_id=1, source_target_pairs={{0,4},{1,5},{4,0},{5,1},{2,6},{3,7},{6,2},{7,3},{8,12},{9,13},{12,... | collective-permute-start | bytes 417800 | tf_op jit(solution)/shard_map/ppermute | solution.py:637
  69.2 4.0 %collective-permute-start.20 = (bf16[272,256]{1,0:T(8,128)(2,1)S(1)}, bf16[272,256]{1,0:T(8,128)(2,1)S(1)}, u32[]{:S(2)}, u32[]{:S(2)}) collective-permute-start(bf16[272,256]{1,0:T(8,128)(2,1)S(1)} %pad_maximum_fusion.1.refs_0_), channel_id=1, source_target_pairs={{0,2},{2,0},{1,3},{3,1},{4,6},{6,4},{5,7},{7,5},{8,10},{10,8},{9,1... | collective-permute-start | bytes 417800 | tf_op jit(solution)/shard_map/ppermute | solution.py:637
  71.6 1.5 %collective-permute-start.23 = (bf16[272,256]{1,0:T(8,128)(2,1)S(1)}, bf16[272,256]{1,0:T(8,128)(2,1)S(1)}, u32[]{:S(2)}, u32[]{:S(2)}) collective-permute-start(bf16[272,256]{1,0:T(8,128)(2,1)S(1)} %collective-permute-done.19.refs_3_), channel_id=1, source_target_pairs={{0,2},{2,0},{1,3},{3,1},{4,6},{6,4},{5,7},{7,5},{8,10},{10,8},{9,1... | collective-permute-start | bytes 417800 | tf_op jit(solution)/shard_map/ppermute | solution.py:637
  72.7 1.4 %collective-permute-start.22 = (bf16[272,256]{1,0:T(8,128)(2,1)S(1)}, bf16[272,256]{1,0:T(8,128)(2,1)S(1)}, u32[]{:S(2)}, u32[]{:S(2)}) collective-permute-start(bf16[272,256]{1,0:T(8,128)(2,1)S(1)} %collective-permute-done.18.refs_2_), channel_id=1, source_target_pairs={{0,2},{2,0},{1,3},{3,1},{4,6},{6,4},{5,7},{7,5},{8,10},{10,8},{9,1... | collective-permute-start | bytes 417800 | tf_op jit(solution)/shard_map/ppermute | solution.py:637
  72.7 1.6 %collective-permute-start.21 = (bf16[272,256]{1,0:T(8,128)(2,1)S(1)}, bf16[272,256]{1,0:T(8,128)(2,1)S(1)}, u32[]{:S(2)}, u32[]{:S(2)}) collective-permute-start(bf16[272,256]{1,0:T(8,128)(2,1)S(1)} %collective-permute-done.17.refs_1_), channel_id=1, source_target_pairs={{0,2},{2,0},{1,3},{3,1},{4,6},{6,4},{5,7},{7,5},{8,10},{10,8},{9,1... | collective-permute-start | bytes 417800 | tf_op jit(solution)/shard_map/ppermute | solution.py:637

commit v4 on v2

--- a/solution.py
+++ b/solution.py
@@ -15,6 +15,7 @@
 EPSILON = 1e-05
 NEGATIVE = -1e30
 INV_ROOT_TWO_PI = 0.3989422804014327
+LOG2_E = 1.4426950408889634
 BF = jnp.bfloat16
 F32 = jnp.float32
 VMEM_LIMIT = 16 * 1024 * 1024
@@ -74,11 +75,13 @@
 
 def project_keys(x, w_all, bias_v, first_place, length, k_out, v_out):
     raw = nn(x, w_all[:, WIDE : 2 * WIDE])
-    shut = lane_of(raw.shape) % SLOT == HEAD_DIM + 2
-    shut &= row_of(raw.shape) + first_place >= length
-    k_out[...] = jnp.where(shut, NEGATIVE, raw).astype(BF)
-    one_row = lane_of((1, WIDE)) % SLOT
-    ones_row = jnp.where((one_row == HEAD_DIM) | (one_row == HEAD_DIM + 1), 1.0, 0.0)
+    one_head = (raw.shape[0], SLOT)
+    shut = jnp.where(row_of(one_head) + first_place >= length, NEGATIVE, 0.0)
+    here = lane_of(one_head) == HEAD_DIM + 2
+    for head in range(HEADS):
+        cols = head_cols(head)
+        k_out[:, cols] = jnp.where(here, shut, raw[:, cols]).astype(BF)
+    ones_row = jnp.where(lane_of((1, WIDE)) % SLOT == HEAD_DIM, 1.0, 0.0)
     v_out[...] = (nn(x, w_all[:, 2 * WIDE :]) + (spread(bias_v) + ones_row)).astype(BF)
 
 
@@ -193,10 +196,12 @@
     return centred * inverse, inverse
 
 
-def norm_back(grad, unit, inverse):
-    shift = jnp.mean(grad, axis=1, keepdims=True)
-    scale = jnp.mean(grad * unit, axis=1, keepdims=True)
-    return (grad - shift - unit * scale) * inverse
+def norm_back(grad, gain, unit, inverse):
+    product = grad * unit
+    scaled = grad * gain
+    shift = jnp.mean(scaled, axis=1, keepdims=True)
+    scale = jnp.mean(product * gain, axis=1, keepdims=True)
+    return (scaled - shift - unit * scale) * inverse, product
 
 
 def eight_sum(matrix):
@@ -209,7 +214,7 @@
 
 
 def gelu_parts(pre):
-    bell = jnp.exp(pre * pre * (-0.5))
+    bell = jnp.exp2(pre * pre * (-0.5 * LOG2_E))
     t = inverse_of(1.0 + (0.3275911 * 0.7071067811865476) * jnp.abs(pre))
     poly = 0.5 * 1.061405429
     for factor in (-1.453152027, 1.421413741, -0.284496736, 0.254829592):
@@ -295,7 +300,7 @@
     if carry:
         dwo_in, dw1_in, dw2_in, vec_in = refs[:4]
         refs = refs[4:]
-    do_outs, refs = refs[:ring], refs[ring:]
+    do_outs, dot_outs, refs = refs[:ring], refs[ring : 2 * ring], refs[2 * ring :]
     result_out, k_out, v_out, kept_out, x_out, first_out, vec_out = refs[:7]
     refs = refs[7:]
     if carry:
@@ -344,7 +349,8 @@
 
     my_place = lax.axis_index("seq") * rows
 
-    valid = jnp.where(row_of((rows, width)) + my_place < length, 1.0, 0.0)
+    valid = jnp.where(row_of((rows, SLOT)) + my_place < length, 1.0, 0.0)
+    valid = jnp.concatenate([valid] * (width // SLOT), axis=1)
 
     def add(slot, matrix):
         acc[slot] = eight_sum(matrix)
@@ -367,11 +373,11 @@
     unit, inverse = norm_parts(narrow_b[...] + branch)
     result_out[...] = unit * gain_two[...] + shift_two[...]
     grad_result = cotangent[...] * valid
-    grad_second = norm_back(grad_result * gain_two[...], unit, inverse)
+    grad_second, product = norm_back(grad_result, gain_two[...], unit, inverse)
     narrow_b[...] = grad_second
     branch_bf = grad_second.astype(BF)
     branch_low[...] = branch_bf
-    add(0, grad_result * unit)
+    add(0, product)
     add(1, grad_result)
     add(10, branch * branch * valid)
 
@@ -380,11 +386,11 @@
 
     grad_normed = narrow_b[...] + nt(hidden_low[...], w1[...])
     unit = unit_one[...]
-    grad_first = norm_back(grad_normed * gain_one[...], unit, inverse_one[:, :1])
+    grad_first, product = norm_back(grad_normed, gain_one[...], unit, inverse_one[:, :1])
     first_out[...] = grad_first
     attn_bf = grad_first.astype(BF)
     attn_low[...] = attn_bf
-    add(5, grad_normed * unit)
+    add(5, product)
     add(6, grad_normed)
 
     do_wide = nt(attn_low[...], wo[...]).astype(BF).astype(F32)
@@ -392,13 +398,10 @@
         cols = head_cols(head)
         do_head = do_wide[:, cols]
         row_dot = jnp.sum(do_head * attended_wide[:, cols], axis=1, keepdims=True)
-        lane = lane_of(do_head.shape)
-        for scale, do_out in zip(scales, do_outs):
+        for scale, do_out, dot_out in zip(scales, do_outs, dot_outs):
             factor = scale[:, cols]
-            dot = -row_dot * factor
-            rest = dot - dot.astype(BF).astype(F32)
-            scaled = jnp.where(lane == HEAD_DIM, dot, do_head * factor)
-            do_out[:, cols] = jnp.where(lane == HEAD_DIM + 1, rest, scaled).astype(BF)
+            do_out[:, cols] = (do_head * factor).astype(BF)
+            dot_out[:, cols] = row_dot * factor
 
     ones = jnp.ones((8, rows), BF)
     hidden_sum = nn(ones, hidden_low[...])[0:1]
@@ -440,8 +443,9 @@
     halve(pack, keep_out, give_out)
 
 
-def head_grads(q, k, v, do, kept):
-    score_grad = (kept.astype(F32) * nt(do, v)).astype(BF)
+def head_grads(q, k, v, do, dot, kept):
+    dots = jnp.concatenate([dot] * (kept.shape[1] // SLOT), axis=1)
+    score_grad = (kept.astype(F32) * (nt(do, v) - dots)).astype(BF)
     return (
         nn(score_grad, k),
         tn(q[:, :HEAD_DIM], score_grad),
@@ -449,12 +453,13 @@
     )
 
 
-def all_heads(q, k, v, do, kept, low, put_query):
+def all_heads(q, k, v, do, dot, kept, low, put_query):
     rows = q.shape[0]
     for head in range(HEADS):
         cols = head_cols(head)
         dq, dk, dv = head_grads(
-            q[:, cols], k[:, cols], v[:, cols], do[:, cols], kept[kept_rows(head, rows), :]
+            q[:, cols], k[:, cols], v[:, cols], do[:, cols], dot[:, cols],
+            kept[kept_rows(head, rows), :],
         )
         put_query(cols, dq)
         low[head * HEAD_DIM : (head + 1) * HEAD_DIM, :] = dk.astype(BF)
@@ -474,7 +479,7 @@
     return jnp.broadcast_to(sums, (half, SLOT))
 
 
-def block_kernel(cell, carry_dq, carry, sent, carrier, q, do, k, v, kept, w_kv, *refs):
+def block_kernel(cell, carry_dq, carry, sent, carrier, q, do, dot, k, v, kept, w_kv, *refs):
     if carry_dq:
         dq_in, refs = refs[0], refs[1:]
     if carry:
@@ -484,7 +489,7 @@
     def put_query(cols, dq):
         dq_out[:, cols] = dq + dq_in[:, cols] if carry_dq else dq
 
-    all_heads(q, k, v, do, kept, low, put_query)
+    all_heads(q, k, v, do, dot, kept, low, put_query)
     x = sent[: q.shape[0], :]
     dx_bf = jnp.transpose(nn(w_kv[...], low[...])).astype(BF)
     dx_out[...] = dx_bf
@@ -498,7 +503,7 @@
 
 def last_kernel(
     cell, carry, finish,
-    sent, carrier, q, do, k, v, kept, w_all, w_kv, first, dq_in, dw_in, sum_in, vec_in, *refs
+    sent, carrier, q, do, dot, k, v, kept, w_all, w_kv, first, dq_in, dw_in, sum_in, vec_in, *refs
 ):
     if carry:
         dwq_in, refs = refs[0], refs[1:]
@@ -510,7 +515,7 @@
     def put_query(cols, dq):
         low_q[:, cols] = ((dq + dq_in[:, cols]) * HEAD_DIM ** (-0.5)).astype(BF)
 
-    all_heads(q, k, v, do, kept, low, put_query)
+    all_heads(q, k, v, do, dot, kept, low, put_query)
     grads = first[...] + nt(low_q[...], w_all[:, :WIDE]) * HEAD_DIM**0.5
     grads += jnp.transpose(nn(w_kv[...], low[...]))
     dx_out[...] = grads
@@ -764,7 +769,7 @@
         partial = []
         for t in range(1, ring):
             ins = [
-                x_moved[cell][t], carriers[t], queries[cell], grads_out[cell][t],
+                x_moved[cell][t], carriers[t], queries[cell], *grads_out[cell][t],
                 keys[cell][t], values[cell][t], kept[cell][t], w_kv,
             ]
             ins += ([dq[cell]] if t > 1 else []) + carried_back
@@ -793,7 +798,7 @@
             partial = backward_of_blocks(cell - 1)
             states[cell], partial = lax.optimization_barrier((states[cell], partial))
             received.append(returned(partial))
-        outs = [low_wide] * ring
+        outs = [low_wide] * ring + [full_wide] * ring
         outs += [full_narrow, low_wide, low_wide, weights, low_narrow, full_narrow]
         outs += [shape((16, width), F32)] + (low_weights if cell == 0 else [])
         if finish:
@@ -829,7 +834,8 @@
             scratch,
             flops=7 * score_flops,
         )
-        grads_out.append(made[:ring])
+        grads_out.append(list(zip(made[:ring], made[ring : 2 * ring])))
+        made = made[ring:]
         result, k, v, p, x_moved[cell][ring - 1], first, vec_mid = made[ring : ring + 7]
         made = made[ring + 7 :]
         if cell == 0:
@@ -861,8 +867,8 @@
             own_one = sum_steps(own_one, got_one)
             got_one = swap(own_one, "z", depth_steps[0])
         ins = [
-            x_moved[cell][0], carriers[0], queries[cell], grads_out[cell][0], keys[cell][0],
-            values[cell][0], kept[cell][0], w_all, w_kv, firsts[cell], dq[cell],
+            x_moved[cell][0], carriers[0], queries[cell], *grads_out[cell][0],
+            keys[cell][0], values[cell][0], kept[cell][0], w_all, w_kv, firsts[cell], dq[cell],
         ]
         outs = [full_narrow]
         scratch = [pltpu.VMEM((rows, WIDE), BF), pltpu.VMEM((2 * width, rows), BF)]

time: 76 us -> 75.7 us (level)
  transfers between devices with their start and end apart: 24 -> 24, of which waited for: 11 -> 12; matrix products, arithmetic and copies ran while one was open for 2% -> 2% of each run, Pallas kernels for 40% -> 39%
where the time goes in v4:
time: 75.7 us; the launch traced here: 75.5 us
  Pallas kernels  35.4 us (47%)
  starting transfers between devices  24.8 us (33%)
  waiting for transfers between devices  11.9 us (16%)
  other arithmetic  1.21 us (2%)
  between operations  1.18 us (2%)
  local copies, waits for them, and re-layouts  1.11 us (1%)
    pallas_call x11, Pallas kernels, call(): pl.pallas_call(kernel, in_specs=[smem if a.ndim == 1 else vmem for a in i...  32.9 us
    ppermute x20, starting transfers between devices, swap(): lax.ppermute(block, axes, [(i, i ^ step) for i in range(lax.axis_size(axe...  20 us
    ppermute x20, waiting for transfers between devices, swap(): lax.ppermute(block, axes, [(i, i ^ step) for i in range(lax.axis_size(axe...  11.4 us
    ppermute x4, starting transfers between devices, send(): return lax.ppermute(block, 'seq', route)  4.77 us
    pallas_call x2, Pallas kernels, body(): pl.pallas_call(functools.partial(select_kernel, cell, carry), in_specs=[p...  2.48 us
  transfers between devices with their start and end apart: 24, of which 12 were waited for; matrix products, arithmetic and copies ran while one was open for 2% of the time, Pallas kernels for 39%

profile of v4, /device:TPU:0, one launch (start us, length us, event | category | flops | bytes accessed | tf_op | source)
XLA Modules:
  0.0 75.5 jit_solution(8072278576512461548)
XLA Ops:
  0.7 1.3 %shard_map.339 = (f32[512,256]{1,0:T(8,128)S(1)}, bf16[512,256]{1,0:T(8,128)(2,1)S(1)}) custom-call(f32[2,512,256]{2,1,0:T(8,128)} %tokens.3, s32[2,512]{1,0:T(2,128)} %masks.2, f32[1,256]{1,0:T(1,128)} %bitcast.47), custom_call_target="tpu_custom_call" | custom-call | tf_op jit(solution)/shard_map/pallas_call | solution.py:693
  2.0 3.0 %collective-permute-start.1 = (bf16[512,256]{1,0:T(8,128)(2,1)S(1)}, bf16[512,256]{1,0:T(8,128)(2,1)S(1)}, u32[]{:S(2)}, u32[]{:S(2)}) collective-permute-start(bf16[512,256]{1,0:T(8,128)(2,1)S(1)} %get-tuple-element.155.refs_0_.sent), channel_id=1, source_target_pairs={{0,1},{1,0},{2,3},{3,2},{4,5},{5,4},{6,7},{7,6},{8,9},{9,8},{10,11... | collective-permute-start | bytes 786440 | tf_op jit(solution)/shard_map/ppermute | solution.py:625
  5.0 1.2 %shard_map.340 = (f32[512,256]{1,0:T(8,128)S(1)}, bf16[512,256]{1,0:T(8,128)(2,1)S(1)}, bf16[528,256]{1,0:T(8,128)(2,1)S(1)}) custom-call(f32[2,512,256]{2,1,0:T(8,128)} %tokens.3, s32[2,512]{1,0:T(2,128)} %masks.2, f32[1,256]{1,0:T(1,128)} %bitcast.48), custom_call_target="tpu_custom_call" | custom-call | tf_op jit(solution)/shard_map/pallas_call | solution.py:693
  6.3 4.7 %shard_map.341 = (bf16[512,512]{1,0:T(8,128)(2,1)S(1)}, bf16[512,512]{1,0:T(8,128)(2,1)S(1)}, bf16[512,512]{1,0:T(8,128)(2,1)S(1)}, bf16[2048,512]{1,0:T(8,128)(...) custom-call(s32[2]{0:T(128)S(1)} %copy-done.15, ...), custom_call_target="tpu_custom_call" | custom-call | flops 2147483648 | bytes 13895688 | tf_op jit(solution)/shard_map/pallas_call | solution.py:610
  11.1 0.1 collective-permute-start
  11.2 0.1 slice_bitcast_fusion
  11.3 0.7 copy-done
  12.1 0.2 copy-done.1
  12.3 6.5 %shard_map.342 = (bf16[512,512]{1,0:T(8,128)(2,1)S(1)}, bf16[512,512]{1,0:T(8,128)(2,1)S(1)}, f32[512,512]{1,0:T(8,128)S(1)}, f32[512,512]{1,0:T(8,128)S(1)}, f3...) custom-call(s32[2]{0:T(128)S(1)} %copy-done.15, ...), custom_call_target="tpu_custom_call" | custom-call | flops 3758096384 | bytes 16016392 | tf_op jit(solution)/shard_map/pallas_call | solution.py:610
  18.9 0.3 collective-permute-done.carrier.x
  19.1 2.7 %shard_map.343 = (f32[512,512]{1,0:T(8,128)S(1)}, bf16[512,256]{1,0:T(8,128)(2,1)S(1)}, f32[512,256]{1,0:T(8,128)S(1)}, f32[256,128]{1,0:T(8,128)S(1)}, f32[8,512]{1,0:T(8,128)S(1)}) custom-call(bf16[512,256]{1,0:T(8,128)(2,1)S(1)} %get-tuple-element.168.sent, bf16[528,256]{1,0:T(8,128)(2,1)S(1)} %collective-permute-done.carrier.x, ...), custom_call_target="tpu_custom_call" | custom-call | flops 2684354560 | bytes 8019968 | tf_op jit(solution)/shard_map/pallas_call | solution.py:610
  21.8 0.8 %collective-permute-start.2 = (bf16[512,256]{1,0:T(8,128)(2,1)S(1)}, bf16[512,256]{1,0:T(8,128)(2,1)S(1)}, u32[]{:S(2)}, u32[]{:S(2)}) collective-permute-start(bf16[512,256]{1,0:T(8,128)(2,1)S(1)} %get-tuple-element.187), channel_id=1, source_target_pairs={{0,1},{1,0},{2,3},{3,2},{4,5},{5,4},{6,7},{7,6},{8,9},{9,8},{10,11... | collective-permute-start | bytes 786440 | tf_op jit(solution)/shard_map/ppermute | solution.py:625
  22.6 6.5 %shard_map.344 = (bf16[512,512]{1,0:T(8,128)(2,1)S(1)}, bf16[512,512]{1,0:T(8,128)(2,1)S(1)}, f32[512,512]{1,0:T(8,128)S(1)}, f32[512,512]{1,0:T(8,128)S(1)}, f3...) custom-call(s32[2]{0:T(128)S(1)} %copy-done.15, ...), custom_call_target="tpu_custom_call" | custom-call | flops 3758096384 | bytes 15385608 | tf_op jit(solution)/shard_map/pallas_call | solution.py:610
  29.2 0.1 collective-permute-done.2.refs_2_
  29.3 2.5 %shard_map.345 = (f32[512,512]{1,0:T(8,128)S(1)}, bf16[512,256]{1,0:T(8,128)(2,1)S(1)}, f32[512,256]{1,0:T(8,128)S(1)}, f32[256,128]{1,0:T(8,128)S(1)}, f32[8,512]{1,0:T(8,128)S(1)}) custom-call(bf16[512,256]{1,0:T(8,128)(2,1)S(1)} %get-tuple-element.186.sent, bf16[528,256]{1,0:T(8,128)(2,1)S(1)} %collective-permute-done.carrier.x, ...), custom_call_target="tpu_custom_call" | custom-call | flops 2684354560 | bytes 8691712 | tf_op jit(solution)/shard_map/pallas_call | solution.py:610
  31.8 0.1 shard_map.346
  31.9 1.2 %collective-permute-start.4 = (bf16[160,256]{1,0:T(8,128)(2,1)S(1)}, bf16[160,256]{1,0:T(8,128)(2,1)S(1)}, u32[]{:S(2)}, u32[]{:S(2)}) collective-permute-start(bf16[160,256]{1,0:T(8,128)(2,1)S(1)} %get-tuple-element.222), channel_id=1, source_target_pairs={{0,1},{1,0},{4,5},{5,4},{2,3},{3,2},{6,7},{7,6},{8,9},{9,8},{12,13... | collective-permute-start | bytes 245768 | tf_op jit(solution)/shard_map/ppermute | solution.py:633
  33.1 1.5 %collective-permute-start.5 = (bf16[160,256]{1,0:T(8,128)(2,1)S(1)}, bf16[160,256]{1,0:T(8,128)(2,1)S(1)}, u32[]{:S(2)}, u32[]{:S(2)}) collective-permute-start(bf16[160,256]{1,0:T(8,128)(2,1)S(1)} %get-tuple-element.223), channel_id=1, source_target_pairs={{0,4},{1,5},{4,0},{5,1},{2,6},{3,7},{6,2},{7,3},{8,12},{9,13},{12,... | collective-permute-start | bytes 245768 | tf_op jit(solution)/shard_map/ppermute | solution.py:633
  34.6 0.9 %collective-permute-start.6 = (bf16[160,256]{1,0:T(8,128)(2,1)S(1)}, bf16[160,256]{1,0:T(8,128)(2,1)S(1)}, u32[]{:S(2)}, u32[]{:S(2)}) collective-permute-start(bf16[160,256]{1,0:T(8,128)(2,1)S(1)} %get-tuple-element.224), channel_id=1, source_target_pairs={{0,5},{1,4},{4,1},{5,0},{2,7},{3,6},{6,3},{7,2},{8,13},{9,12},{12,... | collective-permute-start | bytes 245768 | tf_op jit(solution)/shard_map/ppermute | solution.py:633
  35.5 3.0 %shard_map.347 = (f32[512,256]{1,0:T(8,128)S(1)}, f32[512,256]{1,0:T(8,128)S(1)}, f32[256,128]{1,0:T(8,128)S(1)}, f32[8,512]{1,0:T(8,128)S(1)}, f32[256,512]{1,0:T(8,128)S(1)}) custom-call(bf16[512,256]{1,0:T(8,128)(2,1)S(1)} %get-tuple-element.155.refs_0_.sent, bf16[528,256]{1,0:T(8,128)(2,1)S(1)} %get-tuple-element.159.carrier.sent, ...), custom_call_target="tpu_custom_call" | custom-call | flops 1 | bytes 1 | tf_op jit(solution)/shard_map/pallas_call | solution.py:610
  38.5 1.4 %collective-permute-done.6 = bf16[160,256]{1,0:T(8,128)(2,1)S(1)} collective-permute-done((bf16[160,256]{1,0:T(8,128)(2,1)S(1)}, bf16[160,256]{1,0:T(8,128)(2,1)S(1)}, u32[]{:S(2)}, u32[]{:S(2)}) %collective-permute-start.6) | collective-permute-done | bytes 81952 | tf_op jit(solution)/shard_map/ppermute | solution.py:633
  40.0 1.6 %collective-permute-start.7 = (bf16[160,256]{1,0:T(8,128)(2,1)S(1)}, bf16[160,256]{1,0:T(8,128)(2,1)S(1)}, u32[]{:S(2)}, u32[]{:S(2)}) collective-permute-start(bf16[160,256]{1,0:T(8,128)(2,1)S(1)} %add_convert_fusion.2), channel_id=1, source_target_pairs={{0,8},{8,0},{16,24},{24,16},{1,9},{9,1},{17,25},{25,17},{2,10},{10... | collective-permute-start | bytes 245768 | tf_op jit(solution)/shard_map/ppermute | solution.py:633
  41.7 3.8 %shard_map.348 = (f32[512,256]{1,0:T(8,128)S(1)}, bf16[448,256]{1,0:T(8,128)(2,1)S(1)}, bf16[448,256]{1,0:T(8,128)(2,1)S(1)}) custom-call(bf16[528,256]{1,0:T(8,128)(2,1)S(1)} %get-tuple-element.159.carrier.sent, bf16[528,256]{1,0:T(8,128)(2,1)S(1)} %get-tuple-element.159.carrier.sent, bf16[512,512]{1,0:T(8,128)(2,1)S(1)} %get-tuple-element.188.q, ...), custom_call_target="tpu_custom_call" | custom-call | flops 1 | bytes 1 | tf_op jit(solution)/shard_map/pallas_call | solution.py:610
  45.4 0.1 collective-permute-start.8
  45.5 2.7 %collective-permute-start.12 = (bf16[160,256]{1,0:T(8,128)(2,1)S(1)}, bf16[160,256]{1,0:T(8,128)(2,1)S(1)}, u32[]{:S(2)}, u32[]{:S(2)}) collective-permute-start(bf16[160,256]{1,0:T(8,128)(2,1)S(1)} %add_convert_fusion.1), channel_id=1, source_target_pairs={{0,16},{8,24},{16,0},{24,8},{1,17},{9,25},{17,1},{25,9},{2,18},{10... | collective-permute-start | bytes 245768 | tf_op jit(solution)/shard_map/ppermute | solution.py:633
  48.3 1.0 %collective-permute-start.9 = (bf16[112,256]{1,0:T(8,128)(2,1)S(1)}, bf16[112,256]{1,0:T(8,128)(2,1)S(1)}, u32[]{:S(2)}, u32[]{:S(2)}) collective-permute-start(bf16[112,256]{1,0:T(8,128)(2,1)S(1)} %get-tuple-element.244), channel_id=1, source_target_pairs={{0,1},{1,0},{4,5},{5,4},{2,3},{3,2},{6,7},{7,6},{8,9},{9,8},{12,13... | collective-permute-start | bytes 172040 | tf_op jit(solution)/shard_map/ppermute | solution.py:633
  49.3 1.5 %collective-permute-start.10 = (bf16[112,256]{1,0:T(8,128)(2,1)S(1)}, bf16[112,256]{1,0:T(8,128)(2,1)S(1)}, u32[]{:S(2)}, u32[]{:S(2)}) collective-permute-start(bf16[112,256]{1,0:T(8,128)(2,1)S(1)} %get-tuple-element.245), channel_id=1, source_target_pairs={{0,4},{1,5},{4,0},{5,1},{2,6},{3,7},{6,2},{7,3},{8,12},{9,13},{12,... | collective-permute-start | bytes 172040 | tf_op jit(solution)/shard_map/ppermute | solution.py:633
  50.8 1.0 %collective-permute-start.11 = (bf16[112,256]{1,0:T(8,128)(2,1)S(1)}, bf16[112,256]{1,0:T(8,128)(2,1)S(1)}, u32[]{:S(2)}, u32[]{:S(2)}) collective-permute-start(bf16[112,256]{1,0:T(8,128)(2,1)S(1)} %get-tuple-element.246), channel_id=1, source_target_pairs={{0,5},{1,4},{4,1},{5,0},{2,7},{3,6},{6,3},{7,2},{8,13},{9,12},{12,... | collective-permute-start | bytes 172040 | tf_op jit(solution)/shard_map/ppermute | solution.py:633
  51.8 1.3 %collective-permute-done.12 = bf16[160,256]{1,0:T(8,128)(2,1)S(1)} collective-permute-done((bf16[160,256]{1,0:T(8,128)(2,1)S(1)}, bf16[160,256]{1,0:T(8,128)(2,1)S(1)}, u32[]{:S(2)}, u32[]{:S(2)}) %collective-permute-start.12) | collective-permute-done | bytes 81952 | tf_op jit(solution)/shard_map/ppermute | solution.py:633
  53.1 0.6 collective-permute-done.10
  53.7 2.1 %collective-permute-done.11 = bf16[112,256]{1,0:T(8,128)(2,1)S(1)} collective-permute-done((bf16[112,256]{1,0:T(8,128)(2,1)S(1)}, bf16[112,256]{1,0:T(8,128)(2,1)S(1)}, u32[]{:S(2)}, u32[]{:S(2)}) %collective-permute-start.11) | collective-permute-done | bytes 57376 | tf_op jit(solution)/shard_map/ppermute | solution.py:633
  55.9 0.8 %collective-permute-start.16 = (bf16[512,256]{1,0:T(8,128)(2,1)S(1)}, bf16[512,256]{1,0:T(8,128)(2,1)S(1)}, u32[]{:S(2)}, u32[]{:S(2)}) collective-permute-start(bf16[512,256]{1,0:T(8,128)(2,1)S(1)} %get-tuple-element.255), channel_id=1, source_target_pairs={{0,1},{1,0},{2,3},{3,2},{4,5},{5,4},{6,7},{7,6},{8,9},{9,8},{10,11... | collective-permute-start | bytes 786440 | tf_op jit(solution)/shard_map/ppermute | solution.py:625
  56.7 1.4 %collective-permute-start.15 = (bf16[112,256]{1,0:T(8,128)(2,1)S(1)}, bf16[112,256]{1,0:T(8,128)(2,1)S(1)}, u32[]{:S(2)}, u32[]{:S(2)}) collective-permute-start(bf16[112,256]{1,0:T(8,128)(2,1)S(1)} %add_convert_fusion.4), channel_id=1, source_target_pairs={{0,24},{8,16},{16,8},{24,0},{1,25},{9,17},{17,9},{25,1},{2,26},{10... | collective-permute-start | bytes 172040 | tf_op jit(solution)/shard_map/ppermute | solution.py:633
  58.1 0.6 collective-permute-start.14
  58.8 2.3 %collective-permute-start.13 = (bf16[112,256]{1,0:T(8,128)(2,1)S(1)}, bf16[112,256]{1,0:T(8,128)(2,1)S(1)}, u32[]{:S(2)}, u32[]{:S(2)}) collective-permute-start(bf16[112,256]{1,0:T(8,128)(2,1)S(1)} %add_convert_fusion.4), channel_id=1, source_target_pairs={{0,8},{8,0},{16,24},{24,16},{1,9},{9,1},{17,25},{25,17},{2,10},{10... | collective-permute-start | bytes 172040 | tf_op jit(solution)/shard_map/ppermute | solution.py:633
  61.2 1.6 %collective-permute-done.15 = bf16[112,256]{1,0:T(8,128)(2,1)S(1)} collective-permute-done((bf16[112,256]{1,0:T(8,128)(2,1)S(1)}, bf16[112,256]{1,0:T(8,128)(2,1)S(1)}, u32[]{:S(2)}, u32[]{:S(2)}) %collective-permute-start.15) | collective-permute-done | bytes 57376 | tf_op jit(solution)/shard_map/ppermute | solution.py:633
  62.7 1.2 %collective-permute-done.14 = bf16[112,256]{1,0:T(8,128)(2,1)S(1)} collective-permute-done((bf16[112,256]{1,0:T(8,128)(2,1)S(1)}, bf16[112,256]{1,0:T(8,128)(2,1)S(1)}, u32[]{:S(2)}, u32[]{:S(2)}) %collective-permute-start.14) | collective-permute-done | bytes 57376 | tf_op jit(solution)/shard_map/ppermute | solution.py:633
  64.0 1.3 %collective-permute-start.17 = (bf16[272,256]{1,0:T(8,128)(2,1)S(1)}, bf16[272,256]{1,0:T(8,128)(2,1)S(1)}, u32[]{:S(2)}, u32[]{:S(2)}) collective-permute-start(bf16[272,256]{1,0:T(8,128)(2,1)S(1)} %pad_maximum_fusion.1.refs_0_), channel_id=1, source_target_pairs={{0,1},{1,0},{4,5},{5,4},{2,3},{3,2},{6,7},{7,6},{8,9},{9,8},{12,13... | collective-permute-start | bytes 417800 | tf_op jit(solution)/shard_map/ppermute | solution.py:633
  65.3 1.1 %collective-permute-start.19 = (bf16[272,256]{1,0:T(8,128)(2,1)S(1)}, bf16[272,256]{1,0:T(8,128)(2,1)S(1)}, u32[]{:S(2)}, u32[]{:S(2)}) collective-permute-start(bf16[272,256]{1,0:T(8,128)(2,1)S(1)} %pad_maximum_fusion.1.refs_0_), channel_id=1, source_target_pairs={{0,5},{1,4},{4,1},{5,0},{2,7},{3,6},{6,3},{7,2},{8,13},{9,12},{12,... | collective-permute-start | bytes 417800 | tf_op jit(solution)/shard_map/ppermute | solution.py:633
  66.4 1.2 %collective-permute-start.18 = (bf16[272,256]{1,0:T(8,128)(2,1)S(1)}, bf16[272,256]{1,0:T(8,128)(2,1)S(1)}, u32[]{:S(2)}, u32[]{:S(2)}) collective-permute-start(bf16[272,256]{1,0:T(8,128)(2,1)S(1)} %pad_maximum_fusion.1.refs_0_), channel_id=1, source_target_pairs={{0,4},{1,5},{4,0},{5,1},{2,6},{3,7},{6,2},{7,3},{8,12},{9,13},{12,... | collective-permute-start | bytes 417800 | tf_op jit(solution)/shard_map/ppermute | solution.py:633
  67.6 1.0 %pad_maximum_fusion = f32[2,512,256]{2,1,0:T(8,128)} fusion(f32[1,512,256]{2,1,0:T(8,128)S(1)} %bitcast.28, f32[1,512,256]{2,1,0:T(8,128)S(1)} %bitcast.27), kind=kLoop, calls=%fused_computation | loop fusion | flops 262144 | bytes 2097152 | tf_op jit(solution)/shard_map/stack | solution.py:911
  68.6 1.4 %shard_map.350 = f32[2,512,256]{2,1,0:T(8,128)} custom-call(bf16[528,256]{1,0:T(8,128)(2,1)S(1)} %get-tuple-element.159.carrier.sent, f32[512,256]{1,0:T(8,128)S(1)} %get-tuple-element.259.refs_0_, f32[512,256]{1,0:T(8,128)S(1)} %get-tuple-element.260.refs_1_, bf16[512,256]{1,0:T(8,128)(2,1)S(1)} %collective-permute-done.2.refs_2_, ...), custom_call_target="tpu_custom_call" | custom-call | bytes 2891776 | tf_op jit(solution)/shard_map/pallas_call | solution.py:610
  70.0 1.3 %collective-permute-done.19.refs_3_ = bf16[272,256]{1,0:T(8,128)(2,1)S(1)} collective-permute-done((bf16[272,256]{1,0:T(8,128)(2,1)S(1)}, bf16[272,256]{1,0:T(8,128)(2,1)S(1)}, u32[]{:S(2)}, u32[]{:S(2)}) %collective-permute-start.19) | collective-permute-done | bytes 139296 | tf_op jit(solution)/shard_map/ppermute | solution.py:633
  71.3 0.8 %collective-permute-done.18.refs_2_ = bf16[272,256]{1,0:T(8,128)(2,1)S(1)} collective-permute-done((bf16[272,256]{1,0:T(8,128)(2,1)S(1)}, bf16[272,256]{1,0:T(8,128)(2,1)S(1)}, u32[]{:S(2)}, u32[]{:S(2)}) %collective-permute-start.18) | collective-permute-done | bytes 139296 | tf_op jit(solution)/shard_map/ppermute | solution.py:633
  72.1 0.5 collective-permute-start.21
  72.6 0.8 %collective-permute-done.22.refs_6_ = bf16[272,256]{1,0:T(8,128)(2,1)S(1)} collective-permute-done((bf16[272,256]{1,0:T(8,128)(2,1)S(1)}, bf16[272,256]{1,0:T(8,128)(2,1)S(1)}, u32[]{:S(2)}, u32[]{:S(2)}) %collective-permute-start.22) | collective-permute-done | bytes 139296 | tf_op jit(solution)/shard_map/ppermute | solution.py:633
  73.4 0.2 collective-permute-done.21.refs_5_
  73.6 1.7 %shard_map.351 = (f32[256,256]{1,0:T(8,128)}, f32[256,512]{1,0:T(8,128)}, f32[512,256]{1,0:T(8,128)}, f32[256,256]{1,0:T(8,128)}, f32[256,256]{1,0:T(8,128)}, /*...) custom-call(bf16[272,256]{1,0:T(8,128)(2,1)S(1)} %pad_maximum_fusion, ...), custom_call_target="tpu_custom_call" | custom-call | bytes 3222540 | tf_op jit(solution)/shard_map/pallas_call | solution.py:610
  (55 shorter events, 0.6 us)
Async XLA Ops:
  0.7 5.6 %copy-start.15 = (s32[2]{0:T(128)S(1)}, s32[2]{0:T(128)}, u32[]{:S(2)}) copy-start(s32[2]{0:T(128)} %lengths.5) | copy-start | bytes 28
  0.7 5.6 %copy-start.8 = (f32[256]{0:T(256)S(1)}, f32[256]{0:T(256)}, u32[]{:S(2)}) copy-start(f32[256]{0:T(256)} %param.29) | copy-start | bytes 3076
  0.7 5.6 %copy-start.4 = (f32[256,256]{1,0:T(8,128)S(1)}, f32[256,256]{1,0:T(8,128)}, u32[]{:S(2)}) copy-start(f32[256,256]{1,0:T(8,128)} %refs_4_.1) | copy-start | bytes 786436
  0.7 5.6 %copy-start.3 = (f32[256,256]{1,0:T(8,128)S(1)}, f32[256,256]{1,0:T(8,128)}, u32[]{:S(2)}) copy-start(f32[256,256]{1,0:T(8,128)} %refs_3_.1) | copy-start | bytes 786436
  0.7 5.6 %copy-start.7 = (f32[256]{0:T(256)S(1)}, f32[256]{0:T(256)}, u32[]{:S(2)}) copy-start(f32[256]{0:T(256)} %param.26) | copy-start | bytes 3076
  0.7 5.6 %copy-start.2 = (f32[256,256]{1,0:T(8,128)S(1)}, f32[256,256]{1,0:T(8,128)}, u32[]{:S(2)}) copy-start(f32[256,256]{1,0:T(8,128)} %refs_2_.1) | copy-start | bytes 786436
  2.0 9.3 %collective-permute-start.1 = (bf16[512,256]{1,0:T(8,128)(2,1)S(1)}, bf16[512,256]{1,0:T(8,128)(2,1)S(1)}, u32[]{:S(2)}, u32[]{:S(2)}) collective-permute-start(bf16[512,256]{1,0:T(8,128)(2,1)S(1)} %get-tuple-element.155.refs_0_.sent), channel_id=1, source_target_pairs={{0,1},{1,0},{2,3},{3,2},{4,5},{5,4},{6,7},{7,6},{8,9},{9,8},{10,11... | collective-permute-start | bytes 786440 | tf_op jit(solution)/shard_map/ppermute | solution.py:625
  6.3 4.9 %copy-start.16 = (f32[2,512,256]{2,1,0:T(8,128)S(1)}, f32[2,512,256]{2,1,0:T(8,128)}, u32[]{:S(2)}) copy-start(f32[2,512,256]{2,1,0:T(8,128)} %param.23) | copy-start | bytes 3145732
  11.0 1.0 %copy-start = (f32[256,512]{1,0:T(8,128)S(1)}, f32[256,512]{1,0:T(8,128)}, u32[]{:S(2)}) copy-start(f32[256,512]{1,0:T(8,128)} %w1_in.1) | copy-start | bytes 1572868
  11.0 1.2 %copy-start.1 = (f32[512,256]{1,0:T(8,128)S(1)}, f32[512,256]{1,0:T(8,128)}, u32[]{:S(2)}) copy-start(f32[512,256]{1,0:T(8,128)} %w2_in.1) | copy-start | bytes 1572868
  11.0 1.2 %copy-start.5 = (f32[256,256]{1,0:T(8,128)S(1)}, f32[256,256]{1,0:T(8,128)}, u32[]{:S(2)}) copy-start(f32[256,256]{1,0:T(8,128)} %wo_in.1) | copy-start | bytes 786436
  11.1 1.2 %copy-start.6 = (f32[512]{0:T(512)S(1)}, f32[512]{0:T(512)}, u32[]{:S(2)}) copy-start(f32[512]{0:T(512)} %param.35) | copy-start | bytes 6148
  11.1 1.2 %copy-start.9 = (f32[256]{0:T(256)S(1)}, f32[256]{0:T(256)}, u32[]{:S(2)}) copy-start(f32[256]{0:T(256)} %param.31) | copy-start | bytes 3076
  11.1 1.2 %copy-start.10 = (f32[256]{0:T(256)S(1)}, f32[256]{0:T(256)}, u32[]{:S(2)}) copy-start(f32[256]{0:T(256)} %param.32) | copy-start | bytes 3076
  11.1 1.2 %copy-start.11 = (f32[256]{0:T(256)S(1)}, f32[256]{0:T(256)}, u32[]{:S(2)}) copy-start(f32[256]{0:T(256)} %param.33) | copy-start | bytes 3076
  11.1 1.2 %copy-start.12 = (f32[256]{0:T(256)S(1)}, f32[256]{0:T(256)}, u32[]{:S(2)}) copy-start(f32[256]{0:T(256)} %param.37) | copy-start | bytes 3076
  11.1 1.2 %copy-start.13 = (f32[256]{0:T(256)S(1)}, f32[256]{0:T(256)}, u32[]{:S(2)}) copy-start(f32[256]{0:T(256)} %param.38) | copy-start | bytes 3076
  11.1 1.2 %copy-start.14 = (f32[256]{0:T(256)S(1)}, f32[256]{0:T(256)}, u32[]{:S(2)}) copy-start(f32[256]{0:T(256)} %param.39) | copy-start | bytes 3076
  11.1 8.0 %collective-permute-start = (bf16[528,256]{1,0:T(8,128)(2,1)S(1)}, bf16[528,256]{1,0:T(8,128)(2,1)S(1)}, u32[]{:S(2)}, u32[]{:S(2)}) collective-permute-start(bf16[528,256]{1,0:T(8,128)(2,1)S(1)} %get-tuple-element.159.carrier.sent), channel_id=1, source_target_pairs={{0,1},{1,0},{2,3},{3,2},{4,5},{5,4},{6,7},{7,6},{8,9},{9,8},{10,11... | collective-permute-start | bytes 811016 | tf_op jit(solution)/shard_map/ppermute | solution.py:625
  21.8 7.5 %collective-permute-start.2 = (bf16[512,256]{1,0:T(8,128)(2,1)S(1)}, bf16[512,256]{1,0:T(8,128)(2,1)S(1)}, u32[]{:S(2)}, u32[]{:S(2)}) collective-permute-start(bf16[512,256]{1,0:T(8,128)(2,1)S(1)} %get-tuple-element.187), channel_id=1, source_target_pairs={{0,1},{1,0},{2,3},{3,2},{4,5},{5,4},{6,7},{7,6},{8,9},{9,8},{10,11... | collective-permute-start | bytes 786440 | tf_op jit(solution)/shard_map/ppermute | solution.py:625
  29.1 2.7 %collective-permute-start.3 = (bf16[640,256]{1,0:T(8,128)(2,1)S(1)}, bf16[640,256]{1,0:T(8,128)(2,1)S(1)}, u32[]{:S(2)}, u32[]{:S(2)}) collective-permute-start(bf16[640,256]{1,0:T(8,128)(2,1)S(1)} %get-tuple-element.202), channel_id=1, source_target_pairs={{0,2},{2,0},{1,3},{3,1},{4,6},{6,4},{5,7},{7,5},{8,10},{10,8},{9,1... | collective-permute-start | bytes 983048 | tf_op jit(solution)/shard_map/ppermute | solution.py:633
  31.9 6.6 %collective-permute-start.4 = (bf16[160,256]{1,0:T(8,128)(2,1)S(1)}, bf16[160,256]{1,0:T(8,128)(2,1)S(1)}, u32[]{:S(2)}, u32[]{:S(2)}) collective-permute-start(bf16[160,256]{1,0:T(8,128)(2,1)S(1)} %get-tuple-element.222), channel_id=1, source_target_pairs={{0,1},{1,0},{4,5},{5,4},{2,3},{3,2},{6,7},{7,6},{8,9},{9,8},{12,13... | collective-permute-start | bytes 245768 | tf_op jit(solution)/shard_map/ppermute | solution.py:633
  33.1 5.4 %collective-permute-start.5 = (bf16[160,256]{1,0:T(8,128)(2,1)S(1)}, bf16[160,256]{1,0:T(8,128)(2,1)S(1)}, u32[]{:S(2)}, u32[]{:S(2)}) collective-permute-start(bf16[160,256]{1,0:T(8,128)(2,1)S(1)} %get-tuple-element.223), channel_id=1, source_target_pairs={{0,4},{1,5},{4,0},{5,1},{2,6},{3,7},{6,2},{7,3},{8,12},{9,13},{12,... | collective-permute-start | bytes 245768 | tf_op jit(solution)/shard_map/ppermute | solution.py:633
  34.6 5.3 %collective-permute-start.6 = (bf16[160,256]{1,0:T(8,128)(2,1)S(1)}, bf16[160,256]{1,0:T(8,128)(2,1)S(1)}, u32[]{:S(2)}, u32[]{:S(2)}) collective-permute-start(bf16[160,256]{1,0:T(8,128)(2,1)S(1)} %get-tuple-element.224), channel_id=1, source_target_pairs={{0,5},{1,4},{4,1},{5,0},{2,7},{3,6},{6,3},{7,2},{8,13},{9,12},{12,... | collective-permute-start | bytes 245768 | tf_op jit(solution)/shard_map/ppermute | solution.py:633
  40.0 5.4 %collective-permute-start.7 = (bf16[160,256]{1,0:T(8,128)(2,1)S(1)}, bf16[160,256]{1,0:T(8,128)(2,1)S(1)}, u32[]{:S(2)}, u32[]{:S(2)}) collective-permute-start(bf16[160,256]{1,0:T(8,128)(2,1)S(1)} %add_convert_fusion.2), channel_id=1, source_target_pairs={{0,8},{8,0},{16,24},{24,16},{1,9},{9,1},{17,25},{25,17},{2,10},{10... | collective-permute-start | bytes 245768 | tf_op jit(solution)/shard_map/ppermute | solution.py:633
  45.4 2.8 %collective-permute-start.8 = (bf16[448,256]{1,0:T(8,128)(2,1)S(1)}, bf16[448,256]{1,0:T(8,128)(2,1)S(1)}, u32[]{:S(2)}, u32[]{:S(2)}) collective-permute-start(bf16[448,256]{1,0:T(8,128)(2,1)S(1)} %get-tuple-element.243), channel_id=1, source_target_pairs={{0,2},{2,0},{1,3},{3,1},{4,6},{6,4},{5,7},{7,5},{8,10},{10,8},{9,1... | collective-permute-start | bytes 688136 | tf_op jit(solution)/shard_map/ppermute | solution.py:633
  45.5 7.6 %collective-permute-start.12 = (bf16[160,256]{1,0:T(8,128)(2,1)S(1)}, bf16[160,256]{1,0:T(8,128)(2,1)S(1)}, u32[]{:S(2)}, u32[]{:S(2)}) collective-permute-start(bf16[160,256]{1,0:T(8,128)(2,1)S(1)} %add_convert_fusion.1), channel_id=1, source_target_pairs={{0,16},{8,24},{16,0},{24,8},{1,17},{9,25},{17,1},{25,9},{2,18},{10... | collective-permute-start | bytes 245768 | tf_op jit(solution)/shard_map/ppermute | solution.py:633
  48.3 4.8 %collective-permute-start.9 = (bf16[112,256]{1,0:T(8,128)(2,1)S(1)}, bf16[112,256]{1,0:T(8,128)(2,1)S(1)}, u32[]{:S(2)}, u32[]{:S(2)}) collective-permute-start(bf16[112,256]{1,0:T(8,128)(2,1)S(1)} %get-tuple-element.244), channel_id=1, source_target_pairs={{0,1},{1,0},{4,5},{5,4},{2,3},{3,2},{6,7},{7,6},{8,9},{9,8},{12,13... | collective-permute-start | bytes 172040 | tf_op jit(solution)/shard_map/ppermute | solution.py:633
  49.3 4.5 %collective-permute-start.10 = (bf16[112,256]{1,0:T(8,128)(2,1)S(1)}, bf16[112,256]{1,0:T(8,128)(2,1)S(1)}, u32[]{:S(2)}, u32[]{:S(2)}) collective-permute-start(bf16[112,256]{1,0:T(8,128)(2,1)S(1)} %get-tuple-element.245), channel_id=1, source_target_pairs={{0,4},{1,5},{4,0},{5,1},{2,6},{3,7},{6,2},{7,3},{8,12},{9,13},{12,... | collective-permute-start | bytes 172040 | tf_op jit(solution)/shard_map/ppermute | solution.py:633
  50.8 5.1 %collective-permute-start.11 = (bf16[112,256]{1,0:T(8,128)(2,1)S(1)}, bf16[112,256]{1,0:T(8,128)(2,1)S(1)}, u32[]{:S(2)}, u32[]{:S(2)}) collective-permute-start(bf16[112,256]{1,0:T(8,128)(2,1)S(1)} %get-tuple-element.246), channel_id=1, source_target_pairs={{0,5},{1,4},{4,1},{5,0},{2,7},{3,6},{6,3},{7,2},{8,13},{9,12},{12,... | collective-permute-start | bytes 172040 | tf_op jit(solution)/shard_map/ppermute | solution.py:633
  55.9 8.1 %collective-permute-start.16 = (bf16[512,256]{1,0:T(8,128)(2,1)S(1)}, bf16[512,256]{1,0:T(8,128)(2,1)S(1)}, u32[]{:S(2)}, u32[]{:S(2)}) collective-permute-start(bf16[512,256]{1,0:T(8,128)(2,1)S(1)} %get-tuple-element.255), channel_id=1, source_target_pairs={{0,1},{1,0},{2,3},{3,2},{4,5},{5,4},{6,7},{7,6},{8,9},{9,8},{10,11... | collective-permute-start | bytes 786440 | tf_op jit(solution)/shard_map/ppermute | solution.py:625
  56.7 6.0 %collective-permute-start.15 = (bf16[112,256]{1,0:T(8,128)(2,1)S(1)}, bf16[112,256]{1,0:T(8,128)(2,1)S(1)}, u32[]{:S(2)}, u32[]{:S(2)}) collective-permute-start(bf16[112,256]{1,0:T(8,128)(2,1)S(1)} %add_convert_fusion.4), channel_id=1, source_target_pairs={{0,24},{8,16},{16,8},{24,0},{1,25},{9,17},{17,9},{25,1},{2,26},{10... | collective-permute-start | bytes 172040 | tf_op jit(solution)/shard_map/ppermute | solution.py:633
  58.1 5.8 %collective-permute-start.14 = (bf16[112,256]{1,0:T(8,128)(2,1)S(1)}, bf16[112,256]{1,0:T(8,128)(2,1)S(1)}, u32[]{:S(2)}, u32[]{:S(2)}) collective-permute-start(bf16[112,256]{1,0:T(8,128)(2,1)S(1)} %add_convert_fusion.4), channel_id=1, source_target_pairs={{0,16},{8,24},{16,0},{24,8},{1,17},{9,25},{17,1},{25,9},{2,18},{10... | collective-permute-start | bytes 172040 | tf_op jit(solution)/shard_map/ppermute | solution.py:633
  58.8 5.2 %collective-permute-start.13 = (bf16[112,256]{1,0:T(8,128)(2,1)S(1)}, bf16[112,256]{1,0:T(8,128)(2,1)S(1)}, u32[]{:S(2)}, u32[]{:S(2)}) collective-permute-start(bf16[112,256]{1,0:T(8,128)(2,1)S(1)} %add_convert_fusion.4), channel_id=1, source_target_pairs={{0,8},{8,0},{16,24},{24,16},{1,9},{9,1},{17,25},{25,17},{2,10},{10... | collective-permute-start | bytes 172040 | tf_op jit(solution)/shard_map/ppermute | solution.py:633
  64.0 6.0 %collective-permute-start.17 = (bf16[272,256]{1,0:T(8,128)(2,1)S(1)}, bf16[272,256]{1,0:T(8,128)(2,1)S(1)}, u32[]{:S(2)}, u32[]{:S(2)}) collective-permute-start(bf16[272,256]{1,0:T(8,128)(2,1)S(1)} %pad_maximum_fusion.1.refs_0_), channel_id=1, source_target_pairs={{0,1},{1,0},{4,5},{5,4},{2,3},{3,2},{6,7},{7,6},{8,9},{9,8},{12,13... | collective-permute-start | bytes 417800 | tf_op jit(solution)/shard_map/ppermute | solution.py:633
  65.3 6.0 %collective-permute-start.19 = (bf16[272,256]{1,0:T(8,128)(2,1)S(1)}, bf16[272,256]{1,0:T(8,128)(2,1)S(1)}, u32[]{:S(2)}, u32[]{:S(2)}) collective-permute-start(bf16[272,256]{1,0:T(8,128)(2,1)S(1)} %pad_maximum_fusion.1.refs_0_), channel_id=1, source_target_pairs={{0,5},{1,4},{4,1},{5,0},{2,7},{3,6},{6,3},{7,2},{8,13},{9,12},{12,... | collective-permute-start | bytes 417800 | tf_op jit(solution)/shard_map/ppermute | solution.py:633
  66.4 5.7 %collective-permute-start.18 = (bf16[272,256]{1,0:T(8,128)(2,1)S(1)}, bf16[272,256]{1,0:T(8,128)(2,1)S(1)}, u32[]{:S(2)}, u32[]{:S(2)}) collective-permute-start(bf16[272,256]{1,0:T(8,128)(2,1)S(1)} %pad_maximum_fusion.1.refs_0_), channel_id=1, source_target_pairs={{0,4},{1,5},{4,0},{5,1},{2,6},{3,7},{6,2},{7,3},{8,12},{9,13},{12,... | collective-permute-start | bytes 417800 | tf_op jit(solution)/shard_map/ppermute | solution.py:633
  68.6 4.0 %collective-permute-start.20 = (bf16[272,256]{1,0:T(8,128)(2,1)S(1)}, bf16[272,256]{1,0:T(8,128)(2,1)S(1)}, u32[]{:S(2)}, u32[]{:S(2)}) collective-permute-start(bf16[272,256]{1,0:T(8,128)(2,1)S(1)} %pad_maximum_fusion.1.refs_0_), channel_id=1, source_target_pairs={{0,2},{2,0},{1,3},{3,1},{4,6},{6,4},{5,7},{7,5},{8,10},{10,8},{9,1... | collective-permute-start | bytes 417800 | tf_op jit(solution)/shard_map/ppermute | solution.py:633
  71.3 1.4 %collective-permute-start.23 = (bf16[272,256]{1,0:T(8,128)(2,1)S(1)}, bf16[272,256]{1,0:T(8,128)(2,1)S(1)}, u32[]{:S(2)}, u32[]{:S(2)}) collective-permute-start(bf16[272,256]{1,0:T(8,128)(2,1)S(1)} %collective-permute-done.19.refs_3_), channel_id=1, source_target_pairs={{0,2},{2,0},{1,3},{3,1},{4,6},{6,4},{5,7},{7,5},{8,10},{10,8},{9,1... | collective-permute-start | bytes 417800 | tf_op jit(solution)/shard_map/ppermute | solution.py:633
  72.1 1.4 %collective-permute-start.22 = (bf16[272,256]{1,0:T(8,128)(2,1)S(1)}, bf16[272,256]{1,0:T(8,128)(2,1)S(1)}, u32[]{:S(2)}, u32[]{:S(2)}) collective-permute-start(bf16[272,256]{1,0:T(8,128)(2,1)S(1)} %collective-permute-done.18.refs_2_), channel_id=1, source_target_pairs={{0,2},{2,0},{1,3},{3,1},{4,6},{6,4},{5,7},{7,5},{8,10},{10,8},{9,1... | collective-permute-start | bytes 417800 | tf_op jit(solution)/shard_map/ppermute | solution.py:633
  72.1 1.6 %collective-permute-start.21 = (bf16[272,256]{1,0:T(8,128)(2,1)S(1)}, bf16[272,256]{1,0:T(8,128)(2,1)S(1)}, u32[]{:S(2)}, u32[]{:S(2)}) collective-permute-start(bf16[272,256]{1,0:T(8,128)(2,1)S(1)} %collective-permute-done.17.refs_1_), channel_id=1, source_target_pairs={{0,2},{2,0},{1,3},{3,1},{4,6},{6,4},{5,7},{7,5},{8,10},{10,8},{9,1... | collective-permute-start | bytes 417800 | tf_op jit(solution)/shard_map/ppermute | solution.py:633

commit v5 on v4

--- a/solution.py
+++ b/solution.py
@@ -491,7 +491,7 @@
 
     all_heads(q, k, v, do, dot, kept, low, put_query)
     x = sent[: q.shape[0], :]
-    dx_bf = jnp.transpose(nn(w_kv[...], low[...])).astype(BF)
+    dx_bf = jnp.transpose(nn(w_kv[...], low[...]).astype(BF))
     dx_out[...] = dx_bf
     dw = nn(low[...], x)
     dw_out[...] = dw + dw_in[...] if carry else dw
@@ -563,16 +563,16 @@
     outs, pack_one, pack = refs[6:-2], refs[-2], refs[-1]
     place_pieces(ring, mine, other, pack_one, pack)
     width = pack.shape[1]
-    dwo_out[...] = jnp.transpose(pack_one[:width, :].astype(F32))
+    dwo_out[...] = jnp.transpose(pack_one[:width, :]).astype(F32)
     dw1_out[:, :width] = pack_one[width : 2 * width, :].astype(F32)
     dw1_out[:, width:] = pack_one[2 * width : 3 * width, :].astype(F32)
     for at in range(0, dw2_out.shape[0], width):
         dw2_out[at : at + width, :] = jnp.transpose(
-            pack_one[3 * width + at : 4 * width + at, :].astype(F32)
-        )
+            pack_one[3 * width + at : 4 * width + at, :]
+        ).astype(F32)
     dwq_out[...] = pack[:width, :].astype(F32)
-    dwk_out[...] = jnp.transpose(pack[width : 2 * width, :].astype(F32))
-    dwv_out[...] = jnp.transpose(pack[2 * width : 3 * width, :].astype(F32))
+    dwk_out[...] = jnp.transpose(pack[width : 2 * width, :]).astype(F32)
+    dwv_out[...] = jnp.transpose(pack[2 * width : 3 * width, :]).astype(F32)
     vec = pack[3 * width : 3 * width + 16, :].astype(F32)
     vec += pack[3 * width + 16 : 3 * width + 32, :].astype(F32)
     for out, row in zip(outs, (0, 1, 2, (3, 4), 5, 6, 7, 12, 13, 14)):

time: 75.7 us -> 75.6 us (level)
  no operation moved by 1% of the time
where the time goes in v5:
time: 75.6 us; the launch traced here: 75.5 us
  Pallas kernels  35.3 us (47%)
  starting transfers between devices  24.8 us (33%)
  waiting for transfers between devices  11.8 us (16%)
  other arithmetic  1.21 us (2%)
  between operations  1.18 us (2%)
  local copies, waits for them, and re-layouts  1.11 us (1%)
    pallas_call x11, Pallas kernels, call(): pl.pallas_call(kernel, in_specs=[smem if a.ndim == 1 else vmem for a in i...  32.8 us
    ppermute x20, starting transfers between devices, swap(): lax.ppermute(block, axes, [(i, i ^ step) for i in range(lax.axis_size(axe...  20 us
    ppermute x20, waiting for transfers between devices, swap(): lax.ppermute(block, axes, [(i, i ^ step) for i in range(lax.axis_size(axe...  11.4 us
    ppermute x4, starting transfers between devices, send(): return lax.ppermute(block, 'seq', route)  4.79 us
    pallas_call x2, Pallas kernels, body(): pl.pallas_call(functools.partial(select_kernel, cell, carry), in_specs=[p...  2.48 us
  transfers between devices with their start and end apart: 24, of which 12 were waited for; matrix products, arithmetic and copies ran while one was open for 2% of the time, Pallas kernels for 39%

profile of v5, /device:TPU:0, one launch (start us, length us, event | category | flops | bytes accessed | tf_op | source)
XLA Modules:
  0.0 75.5 jit_solution(7788372189585951187)
XLA Ops:
  0.7 1.3 %shard_map.339 = (f32[512,256]{1,0:T(8,128)S(1)}, bf16[512,256]{1,0:T(8,128)(2,1)S(1)}) custom-call(f32[2,512,256]{2,1,0:T(8,128)} %tokens.3, s32[2,512]{1,0:T(2,128)} %masks.2, f32[1,256]{1,0:T(1,128)} %bitcast.47), custom_call_target="tpu_custom_call" | custom-call | tf_op jit(solution)/shard_map/pallas_call | solution.py:693
  2.0 3.0 %collective-permute-start.1 = (bf16[512,256]{1,0:T(8,128)(2,1)S(1)}, bf16[512,256]{1,0:T(8,128)(2,1)S(1)}, u32[]{:S(2)}, u32[]{:S(2)}) collective-permute-start(bf16[512,256]{1,0:T(8,128)(2,1)S(1)} %get-tuple-element.155.refs_0_.sent), channel_id=1, source_target_pairs={{0,1},{1,0},{2,3},{3,2},{4,5},{5,4},{6,7},{7,6},{8,9},{9,8},{10,11... | collective-permute-start | bytes 786440 | tf_op jit(solution)/shard_map/ppermute | solution.py:625
  5.0 1.2 %shard_map.340 = (f32[512,256]{1,0:T(8,128)S(1)}, bf16[512,256]{1,0:T(8,128)(2,1)S(1)}, bf16[528,256]{1,0:T(8,128)(2,1)S(1)}) custom-call(f32[2,512,256]{2,1,0:T(8,128)} %tokens.3, s32[2,512]{1,0:T(2,128)} %masks.2, f32[1,256]{1,0:T(1,128)} %bitcast.48), custom_call_target="tpu_custom_call" | custom-call | tf_op jit(solution)/shard_map/pallas_call | solution.py:693
  6.3 4.7 %shard_map.341 = (bf16[512,512]{1,0:T(8,128)(2,1)S(1)}, bf16[512,512]{1,0:T(8,128)(2,1)S(1)}, bf16[512,512]{1,0:T(8,128)(2,1)S(1)}, bf16[2048,512]{1,0:T(8,128)(...) custom-call(s32[2]{0:T(128)S(1)} %copy-done.15, ...), custom_call_target="tpu_custom_call" | custom-call | flops 2147483648 | bytes 13895688 | tf_op jit(solution)/shard_map/pallas_call | solution.py:610
  11.1 0.1 collective-permute-start
  11.2 0.1 slice_bitcast_fusion
  11.3 0.7 copy-done
  12.1 0.2 copy-done.1
  12.3 6.5 %shard_map.342 = (bf16[512,512]{1,0:T(8,128)(2,1)S(1)}, bf16[512,512]{1,0:T(8,128)(2,1)S(1)}, f32[512,512]{1,0:T(8,128)S(1)}, f32[512,512]{1,0:T(8,128)S(1)}, f3...) custom-call(s32[2]{0:T(128)S(1)} %copy-done.15, ...), custom_call_target="tpu_custom_call" | custom-call | flops 3758096384 | bytes 16016392 | tf_op jit(solution)/shard_map/pallas_call | solution.py:610
  18.9 0.3 collective-permute-done.carrier.x
  19.1 2.7 %shard_map.343 = (f32[512,512]{1,0:T(8,128)S(1)}, bf16[512,256]{1,0:T(8,128)(2,1)S(1)}, f32[512,256]{1,0:T(8,128)S(1)}, f32[256,128]{1,0:T(8,128)S(1)}, f32[8,512]{1,0:T(8,128)S(1)}) custom-call(bf16[512,256]{1,0:T(8,128)(2,1)S(1)} %get-tuple-element.168.sent, bf16[528,256]{1,0:T(8,128)(2,1)S(1)} %collective-permute-done.carrier.x, ...), custom_call_target="tpu_custom_call" | custom-call | flops 2684354560 | bytes 8019968 | tf_op jit(solution)/shard_map/pallas_call | solution.py:610
  21.8 0.8 %collective-permute-start.2 = (bf16[512,256]{1,0:T(8,128)(2,1)S(1)}, bf16[512,256]{1,0:T(8,128)(2,1)S(1)}, u32[]{:S(2)}, u32[]{:S(2)}) collective-permute-start(bf16[512,256]{1,0:T(8,128)(2,1)S(1)} %get-tuple-element.187), channel_id=1, source_target_pairs={{0,1},{1,0},{2,3},{3,2},{4,5},{5,4},{6,7},{7,6},{8,9},{9,8},{10,11... | collective-permute-start | bytes 786440 | tf_op jit(solution)/shard_map/ppermute | solution.py:625
  22.6 6.5 %shard_map.344 = (bf16[512,512]{1,0:T(8,128)(2,1)S(1)}, bf16[512,512]{1,0:T(8,128)(2,1)S(1)}, f32[512,512]{1,0:T(8,128)S(1)}, f32[512,512]{1,0:T(8,128)S(1)}, f3...) custom-call(s32[2]{0:T(128)S(1)} %copy-done.15, ...), custom_call_target="tpu_custom_call" | custom-call | flops 3758096384 | bytes 15385608 | tf_op jit(solution)/shard_map/pallas_call | solution.py:610
  29.2 0.1 collective-permute-done.2.refs_2_
  29.3 2.5 %shard_map.345 = (f32[512,512]{1,0:T(8,128)S(1)}, bf16[512,256]{1,0:T(8,128)(2,1)S(1)}, f32[512,256]{1,0:T(8,128)S(1)}, f32[256,128]{1,0:T(8,128)S(1)}, f32[8,512]{1,0:T(8,128)S(1)}) custom-call(bf16[512,256]{1,0:T(8,128)(2,1)S(1)} %get-tuple-element.186.sent, bf16[528,256]{1,0:T(8,128)(2,1)S(1)} %collective-permute-done.carrier.x, ...), custom_call_target="tpu_custom_call" | custom-call | flops 2684354560 | bytes 8691712 | tf_op jit(solution)/shard_map/pallas_call | solution.py:610
  31.8 0.1 shard_map.346
  31.9 1.2 %collective-permute-start.4 = (bf16[160,256]{1,0:T(8,128)(2,1)S(1)}, bf16[160,256]{1,0:T(8,128)(2,1)S(1)}, u32[]{:S(2)}, u32[]{:S(2)}) collective-permute-start(bf16[160,256]{1,0:T(8,128)(2,1)S(1)} %get-tuple-element.222), channel_id=1, source_target_pairs={{0,1},{1,0},{4,5},{5,4},{2,3},{3,2},{6,7},{7,6},{8,9},{9,8},{12,13... | collective-permute-start | bytes 245768 | tf_op jit(solution)/shard_map/ppermute | solution.py:633
  33.1 1.5 %collective-permute-start.5 = (bf16[160,256]{1,0:T(8,128)(2,1)S(1)}, bf16[160,256]{1,0:T(8,128)(2,1)S(1)}, u32[]{:S(2)}, u32[]{:S(2)}) collective-permute-start(bf16[160,256]{1,0:T(8,128)(2,1)S(1)} %get-tuple-element.223), channel_id=1, source_target_pairs={{0,4},{1,5},{4,0},{5,1},{2,6},{3,7},{6,2},{7,3},{8,12},{9,13},{12,... | collective-permute-start | bytes 245768 | tf_op jit(solution)/shard_map/ppermute | solution.py:633
  34.6 0.9 %collective-permute-start.6 = (bf16[160,256]{1,0:T(8,128)(2,1)S(1)}, bf16[160,256]{1,0:T(8,128)(2,1)S(1)}, u32[]{:S(2)}, u32[]{:S(2)}) collective-permute-start(bf16[160,256]{1,0:T(8,128)(2,1)S(1)} %get-tuple-element.224), channel_id=1, source_target_pairs={{0,5},{1,4},{4,1},{5,0},{2,7},{3,6},{6,3},{7,2},{8,13},{9,12},{12,... | collective-permute-start | bytes 245768 | tf_op jit(solution)/shard_map/ppermute | solution.py:633
  35.5 3.0 %shard_map.347 = (f32[512,256]{1,0:T(8,128)S(1)}, f32[512,256]{1,0:T(8,128)S(1)}, f32[256,128]{1,0:T(8,128)S(1)}, f32[8,512]{1,0:T(8,128)S(1)}, f32[256,512]{1,0:T(8,128)S(1)}) custom-call(bf16[512,256]{1,0:T(8,128)(2,1)S(1)} %get-tuple-element.155.refs_0_.sent, bf16[528,256]{1,0:T(8,128)(2,1)S(1)} %get-tuple-element.159.carrier.sent, ...), custom_call_target="tpu_custom_call" | custom-call | flops 1 | bytes 1 | tf_op jit(solution)/shard_map/pallas_call | solution.py:610
  38.5 1.4 %collective-permute-done.6 = bf16[160,256]{1,0:T(8,128)(2,1)S(1)} collective-permute-done((bf16[160,256]{1,0:T(8,128)(2,1)S(1)}, bf16[160,256]{1,0:T(8,128)(2,1)S(1)}, u32[]{:S(2)}, u32[]{:S(2)}) %collective-permute-start.6) | collective-permute-done | bytes 81952 | tf_op jit(solution)/shard_map/ppermute | solution.py:633
  40.0 1.6 %collective-permute-start.7 = (bf16[160,256]{1,0:T(8,128)(2,1)S(1)}, bf16[160,256]{1,0:T(8,128)(2,1)S(1)}, u32[]{:S(2)}, u32[]{:S(2)}) collective-permute-start(bf16[160,256]{1,0:T(8,128)(2,1)S(1)} %add_convert_fusion.2), channel_id=1, source_target_pairs={{0,8},{8,0},{16,24},{24,16},{1,9},{9,1},{17,25},{25,17},{2,10},{10... | collective-permute-start | bytes 245768 | tf_op jit(solution)/shard_map/ppermute | solution.py:633
  41.7 3.8 %shard_map.348 = (f32[512,256]{1,0:T(8,128)S(1)}, bf16[448,256]{1,0:T(8,128)(2,1)S(1)}, bf16[448,256]{1,0:T(8,128)(2,1)S(1)}) custom-call(bf16[528,256]{1,0:T(8,128)(2,1)S(1)} %get-tuple-element.159.carrier.sent, bf16[528,256]{1,0:T(8,128)(2,1)S(1)} %get-tuple-element.159.carrier.sent, bf16[512,512]{1,0:T(8,128)(2,1)S(1)} %get-tuple-element.188.q, ...), custom_call_target="tpu_custom_call" | custom-call | flops 1 | bytes 1 | tf_op jit(solution)/shard_map/pallas_call | solution.py:610
  45.4 0.1 collective-permute-start.8
  45.6 2.7 %collective-permute-start.12 = (bf16[160,256]{1,0:T(8,128)(2,1)S(1)}, bf16[160,256]{1,0:T(8,128)(2,1)S(1)}, u32[]{:S(2)}, u32[]{:S(2)}) collective-permute-start(bf16[160,256]{1,0:T(8,128)(2,1)S(1)} %add_convert_fusion.1), channel_id=1, source_target_pairs={{0,16},{8,24},{16,0},{24,8},{1,17},{9,25},{17,1},{25,9},{2,18},{10... | collective-permute-start | bytes 245768 | tf_op jit(solution)/shard_map/ppermute | solution.py:633
  48.3 1.0 %collective-permute-start.9 = (bf16[112,256]{1,0:T(8,128)(2,1)S(1)}, bf16[112,256]{1,0:T(8,128)(2,1)S(1)}, u32[]{:S(2)}, u32[]{:S(2)}) collective-permute-start(bf16[112,256]{1,0:T(8,128)(2,1)S(1)} %get-tuple-element.244), channel_id=1, source_target_pairs={{0,1},{1,0},{4,5},{5,4},{2,3},{3,2},{6,7},{7,6},{8,9},{9,8},{12,13... | collective-permute-start | bytes 172040 | tf_op jit(solution)/shard_map/ppermute | solution.py:633
  49.3 1.5 %collective-permute-start.10 = (bf16[112,256]{1,0:T(8,128)(2,1)S(1)}, bf16[112,256]{1,0:T(8,128)(2,1)S(1)}, u32[]{:S(2)}, u32[]{:S(2)}) collective-permute-start(bf16[112,256]{1,0:T(8,128)(2,1)S(1)} %get-tuple-element.245), channel_id=1, source_target_pairs={{0,4},{1,5},{4,0},{5,1},{2,6},{3,7},{6,2},{7,3},{8,12},{9,13},{12,... | collective-permute-start | bytes 172040 | tf_op jit(solution)/shard_map/ppermute | solution.py:633
  50.8 1.0 %collective-permute-start.11 = (bf16[112,256]{1,0:T(8,128)(2,1)S(1)}, bf16[112,256]{1,0:T(8,128)(2,1)S(1)}, u32[]{:S(2)}, u32[]{:S(2)}) collective-permute-start(bf16[112,256]{1,0:T(8,128)(2,1)S(1)} %get-tuple-element.246), channel_id=1, source_target_pairs={{0,5},{1,4},{4,1},{5,0},{2,7},{3,6},{6,3},{7,2},{8,13},{9,12},{12,... | collective-permute-start | bytes 172040 | tf_op jit(solution)/shard_map/ppermute | solution.py:633
  51.8 1.3 %collective-permute-done.12 = bf16[160,256]{1,0:T(8,128)(2,1)S(1)} collective-permute-done((bf16[160,256]{1,0:T(8,128)(2,1)S(1)}, bf16[160,256]{1,0:T(8,128)(2,1)S(1)}, u32[]{:S(2)}, u32[]{:S(2)}) %collective-permute-start.12) | collective-permute-done | bytes 81952 | tf_op jit(solution)/shard_map/ppermute | solution.py:633
  53.1 0.6 collective-permute-done.10
  53.7 2.1 %collective-permute-done.11 = bf16[112,256]{1,0:T(8,128)(2,1)S(1)} collective-permute-done((bf16[112,256]{1,0:T(8,128)(2,1)S(1)}, bf16[112,256]{1,0:T(8,128)(2,1)S(1)}, u32[]{:S(2)}, u32[]{:S(2)}) %collective-permute-start.11) | collective-permute-done | bytes 57376 | tf_op jit(solution)/shard_map/ppermute | solution.py:633
  55.9 0.9 %collective-permute-start.16 = (bf16[512,256]{1,0:T(8,128)(2,1)S(1)}, bf16[512,256]{1,0:T(8,128)(2,1)S(1)}, u32[]{:S(2)}, u32[]{:S(2)}) collective-permute-start(bf16[512,256]{1,0:T(8,128)(2,1)S(1)} %get-tuple-element.255), channel_id=1, source_target_pairs={{0,1},{1,0},{2,3},{3,2},{4,5},{5,4},{6,7},{7,6},{8,9},{9,8},{10,11... | collective-permute-start | bytes 786440 | tf_op jit(solution)/shard_map/ppermute | solution.py:625
  56.8 1.4 %collective-permute-start.15 = (bf16[112,256]{1,0:T(8,128)(2,1)S(1)}, bf16[112,256]{1,0:T(8,128)(2,1)S(1)}, u32[]{:S(2)}, u32[]{:S(2)}) collective-permute-start(bf16[112,256]{1,0:T(8,128)(2,1)S(1)} %add_convert_fusion.4), channel_id=1, source_target_pairs={{0,24},{8,16},{16,8},{24,0},{1,25},{9,17},{17,9},{25,1},{2,26},{10... | collective-permute-start | bytes 172040 | tf_op jit(solution)/shard_map/ppermute | solution.py:633
  58.2 0.6 collective-permute-start.14
  58.8 2.4 %collective-permute-start.13 = (bf16[112,256]{1,0:T(8,128)(2,1)S(1)}, bf16[112,256]{1,0:T(8,128)(2,1)S(1)}, u32[]{:S(2)}, u32[]{:S(2)}) collective-permute-start(bf16[112,256]{1,0:T(8,128)(2,1)S(1)} %add_convert_fusion.4), channel_id=1, source_target_pairs={{0,8},{8,0},{16,24},{24,16},{1,9},{9,1},{17,25},{25,17},{2,10},{10... | collective-permute-start | bytes 172040 | tf_op jit(solution)/shard_map/ppermute | solution.py:633
  61.2 1.6 %collective-permute-done.15 = bf16[112,256]{1,0:T(8,128)(2,1)S(1)} collective-permute-done((bf16[112,256]{1,0:T(8,128)(2,1)S(1)}, bf16[112,256]{1,0:T(8,128)(2,1)S(1)}, u32[]{:S(2)}, u32[]{:S(2)}) %collective-permute-start.15) | collective-permute-done | bytes 57376 | tf_op jit(solution)/shard_map/ppermute | solution.py:633
  62.8 1.2 %collective-permute-done.14 = bf16[112,256]{1,0:T(8,128)(2,1)S(1)} collective-permute-done((bf16[112,256]{1,0:T(8,128)(2,1)S(1)}, bf16[112,256]{1,0:T(8,128)(2,1)S(1)}, u32[]{:S(2)}, u32[]{:S(2)}) %collective-permute-start.14) | collective-permute-done | bytes 57376 | tf_op jit(solution)/shard_map/ppermute | solution.py:633
  64.0 1.3 %collective-permute-start.17 = (bf16[272,256]{1,0:T(8,128)(2,1)S(1)}, bf16[272,256]{1,0:T(8,128)(2,1)S(1)}, u32[]{:S(2)}, u32[]{:S(2)}) collective-permute-start(bf16[272,256]{1,0:T(8,128)(2,1)S(1)} %pad_maximum_fusion.1.refs_0_), channel_id=1, source_target_pairs={{0,1},{1,0},{4,5},{5,4},{2,3},{3,2},{6,7},{7,6},{8,9},{9,8},{12,13... | collective-permute-start | bytes 417800 | tf_op jit(solution)/shard_map/ppermute | solution.py:633
  65.3 1.1 %collective-permute-start.19 = (bf16[272,256]{1,0:T(8,128)(2,1)S(1)}, bf16[272,256]{1,0:T(8,128)(2,1)S(1)}, u32[]{:S(2)}, u32[]{:S(2)}) collective-permute-start(bf16[272,256]{1,0:T(8,128)(2,1)S(1)} %pad_maximum_fusion.1.refs_0_), channel_id=1, source_target_pairs={{0,5},{1,4},{4,1},{5,0},{2,7},{3,6},{6,3},{7,2},{8,13},{9,12},{12,... | collective-permute-start | bytes 417800 | tf_op jit(solution)/shard_map/ppermute | solution.py:633
  66.4 1.2 %collective-permute-start.18 = (bf16[272,256]{1,0:T(8,128)(2,1)S(1)}, bf16[272,256]{1,0:T(8,128)(2,1)S(1)}, u32[]{:S(2)}, u32[]{:S(2)}) collective-permute-start(bf16[272,256]{1,0:T(8,128)(2,1)S(1)} %pad_maximum_fusion.1.refs_0_), channel_id=1, source_target_pairs={{0,4},{1,5},{4,0},{5,1},{2,6},{3,7},{6,2},{7,3},{8,12},{9,13},{12,... | collective-permute-start | bytes 417800 | tf_op jit(solution)/shard_map/ppermute | solution.py:633
  67.6 1.0 %pad_maximum_fusion = f32[2,512,256]{2,1,0:T(8,128)} fusion(f32[1,512,256]{2,1,0:T(8,128)S(1)} %bitcast.28, f32[1,512,256]{2,1,0:T(8,128)S(1)} %bitcast.27), kind=kLoop, calls=%fused_computation | loop fusion | flops 262144 | bytes 2097152 | tf_op jit(solution)/shard_map/stack | solution.py:911
  68.6 1.4 %shard_map.350 = f32[2,512,256]{2,1,0:T(8,128)} custom-call(bf16[528,256]{1,0:T(8,128)(2,1)S(1)} %get-tuple-element.159.carrier.sent, f32[512,256]{1,0:T(8,128)S(1)} %get-tuple-element.259.refs_0_, f32[512,256]{1,0:T(8,128)S(1)} %get-tuple-element.260.refs_1_, bf16[512,256]{1,0:T(8,128)(2,1)S(1)} %collective-permute-done.2.refs_2_, ...), custom_call_target="tpu_custom_call" | custom-call | bytes 2891776 | tf_op jit(solution)/shard_map/pallas_call | solution.py:610
  70.0 1.3 %collective-permute-done.19.refs_3_ = bf16[272,256]{1,0:T(8,128)(2,1)S(1)} collective-permute-done((bf16[272,256]{1,0:T(8,128)(2,1)S(1)}, bf16[272,256]{1,0:T(8,128)(2,1)S(1)}, u32[]{:S(2)}, u32[]{:S(2)}) %collective-permute-start.19) | collective-permute-done | bytes 139296 | tf_op jit(solution)/shard_map/ppermute | solution.py:633
  71.3 0.8 %collective-permute-done.18.refs_2_ = bf16[272,256]{1,0:T(8,128)(2,1)S(1)} collective-permute-done((bf16[272,256]{1,0:T(8,128)(2,1)S(1)}, bf16[272,256]{1,0:T(8,128)(2,1)S(1)}, u32[]{:S(2)}, u32[]{:S(2)}) %collective-permute-start.18) | collective-permute-done | bytes 139296 | tf_op jit(solution)/shard_map/ppermute | solution.py:633
  72.1 0.5 collective-permute-start.21
  72.6 0.8 %collective-permute-done.22.refs_6_ = bf16[272,256]{1,0:T(8,128)(2,1)S(1)} collective-permute-done((bf16[272,256]{1,0:T(8,128)(2,1)S(1)}, bf16[272,256]{1,0:T(8,128)(2,1)S(1)}, u32[]{:S(2)}, u32[]{:S(2)}) %collective-permute-start.22) | collective-permute-done | bytes 139296 | tf_op jit(solution)/shard_map/ppermute | solution.py:633
  73.5 0.2 collective-permute-done.21.refs_5_
  73.7 1.6 %shard_map.351 = (f32[256,256]{1,0:T(8,128)}, f32[256,512]{1,0:T(8,128)}, f32[512,256]{1,0:T(8,128)}, f32[256,256]{1,0:T(8,128)}, f32[256,256]{1,0:T(8,128)}, /*...) custom-call(bf16[272,256]{1,0:T(8,128)(2,1)S(1)} %pad_maximum_fusion, ...), custom_call_target="tpu_custom_call" | custom-call | bytes 3222540 | tf_op jit(solution)/shard_map/pallas_call | solution.py:610
  (55 shorter events, 0.5 us)
Async XLA Ops:
  0.7 5.6 %copy-start.15 = (s32[2]{0:T(128)S(1)}, s32[2]{0:T(128)}, u32[]{:S(2)}) copy-start(s32[2]{0:T(128)} %lengths.5) | copy-start | bytes 28
  0.7 5.6 %copy-start.8 = (f32[256]{0:T(256)S(1)}, f32[256]{0:T(256)}, u32[]{:S(2)}) copy-start(f32[256]{0:T(256)} %param.29) | copy-start | bytes 3076
  0.7 5.6 %copy-start.4 = (f32[256,256]{1,0:T(8,128)S(1)}, f32[256,256]{1,0:T(8,128)}, u32[]{:S(2)}) copy-start(f32[256,256]{1,0:T(8,128)} %refs_4_.1) | copy-start | bytes 786436
  0.7 5.6 %copy-start.3 = (f32[256,256]{1,0:T(8,128)S(1)}, f32[256,256]{1,0:T(8,128)}, u32[]{:S(2)}) copy-start(f32[256,256]{1,0:T(8,128)} %refs_3_.1) | copy-start | bytes 786436
  0.7 5.6 %copy-start.7 = (f32[256]{0:T(256)S(1)}, f32[256]{0:T(256)}, u32[]{:S(2)}) copy-start(f32[256]{0:T(256)} %param.26) | copy-start | bytes 3076
  0.7 5.6 %copy-start.2 = (f32[256,256]{1,0:T(8,128)S(1)}, f32[256,256]{1,0:T(8,128)}, u32[]{:S(2)}) copy-start(f32[256,256]{1,0:T(8,128)} %refs_2_.1) | copy-start | bytes 786436
  2.0 9.3 %collective-permute-start.1 = (bf16[512,256]{1,0:T(8,128)(2,1)S(1)}, bf16[512,256]{1,0:T(8,128)(2,1)S(1)}, u32[]{:S(2)}, u32[]{:S(2)}) collective-permute-start(bf16[512,256]{1,0:T(8,128)(2,1)S(1)} %get-tuple-element.155.refs_0_.sent), channel_id=1, source_target_pairs={{0,1},{1,0},{2,3},{3,2},{4,5},{5,4},{6,7},{7,6},{8,9},{9,8},{10,11... | collective-permute-start | bytes 786440 | tf_op jit(solution)/shard_map/ppermute | solution.py:625
  6.3 4.9 %copy-start.16 = (f32[2,512,256]{2,1,0:T(8,128)S(1)}, f32[2,512,256]{2,1,0:T(8,128)}, u32[]{:S(2)}) copy-start(f32[2,512,256]{2,1,0:T(8,128)} %param.23) | copy-start | bytes 3145732
  11.0 1.0 %copy-start = (f32[256,512]{1,0:T(8,128)S(1)}, f32[256,512]{1,0:T(8,128)}, u32[]{:S(2)}) copy-start(f32[256,512]{1,0:T(8,128)} %w1_in.1) | copy-start | bytes 1572868
  11.0 1.2 %copy-start.1 = (f32[512,256]{1,0:T(8,128)S(1)}, f32[512,256]{1,0:T(8,128)}, u32[]{:S(2)}) copy-start(f32[512,256]{1,0:T(8,128)} %w2_in.1) | copy-start | bytes 1572868
  11.0 1.2 %copy-start.5 = (f32[256,256]{1,0:T(8,128)S(1)}, f32[256,256]{1,0:T(8,128)}, u32[]{:S(2)}) copy-start(f32[256,256]{1,0:T(8,128)} %wo_in.1) | copy-start | bytes 786436
  11.1 1.2 %copy-start.6 = (f32[512]{0:T(512)S(1)}, f32[512]{0:T(512)}, u32[]{:S(2)}) copy-start(f32[512]{0:T(512)} %param.35) | copy-start | bytes 6148
  11.1 1.2 %copy-start.9 = (f32[256]{0:T(256)S(1)}, f32[256]{0:T(256)}, u32[]{:S(2)}) copy-start(f32[256]{0:T(256)} %param.31) | copy-start | bytes 3076
  11.1 1.2 %copy-start.10 = (f32[256]{0:T(256)S(1)}, f32[256]{0:T(256)}, u32[]{:S(2)}) copy-start(f32[256]{0:T(256)} %param.32) | copy-start | bytes 3076
  11.1 1.2 %copy-start.11 = (f32[256]{0:T(256)S(1)}, f32[256]{0:T(256)}, u32[]{:S(2)}) copy-start(f32[256]{0:T(256)} %param.33) | copy-start | bytes 3076
  11.1 1.2 %copy-start.12 = (f32[256]{0:T(256)S(1)}, f32[256]{0:T(256)}, u32[]{:S(2)}) copy-start(f32[256]{0:T(256)} %param.37) | copy-start | bytes 3076
  11.1 1.2 %copy-start.13 = (f32[256]{0:T(256)S(1)}, f32[256]{0:T(256)}, u32[]{:S(2)}) copy-start(f32[256]{0:T(256)} %param.38) | copy-start | bytes 3076
  11.1 1.2 %copy-start.14 = (f32[256]{0:T(256)S(1)}, f32[256]{0:T(256)}, u32[]{:S(2)}) copy-start(f32[256]{0:T(256)} %param.39) | copy-start | bytes 3076
  11.1 8.0 %collective-permute-start = (bf16[528,256]{1,0:T(8,128)(2,1)S(1)}, bf16[528,256]{1,0:T(8,128)(2,1)S(1)}, u32[]{:S(2)}, u32[]{:S(2)}) collective-permute-start(bf16[528,256]{1,0:T(8,128)(2,1)S(1)} %get-tuple-element.159.carrier.sent), channel_id=1, source_target_pairs={{0,1},{1,0},{2,3},{3,2},{4,5},{5,4},{6,7},{7,6},{8,9},{9,8},{10,11... | collective-permute-start | bytes 811016 | tf_op jit(solution)/shard_map/ppermute | solution.py:625
  21.8 7.5 %collective-permute-start.2 = (bf16[512,256]{1,0:T(8,128)(2,1)S(1)}, bf16[512,256]{1,0:T(8,128)(2,1)S(1)}, u32[]{:S(2)}, u32[]{:S(2)}) collective-permute-start(bf16[512,256]{1,0:T(8,128)(2,1)S(1)} %get-tuple-element.187), channel_id=1, source_target_pairs={{0,1},{1,0},{2,3},{3,2},{4,5},{5,4},{6,7},{7,6},{8,9},{9,8},{10,11... | collective-permute-start | bytes 786440 | tf_op jit(solution)/shard_map/ppermute | solution.py:625
  29.1 2.7 %collective-permute-start.3 = (bf16[640,256]{1,0:T(8,128)(2,1)S(1)}, bf16[640,256]{1,0:T(8,128)(2,1)S(1)}, u32[]{:S(2)}, u32[]{:S(2)}) collective-permute-start(bf16[640,256]{1,0:T(8,128)(2,1)S(1)} %get-tuple-element.202), channel_id=1, source_target_pairs={{0,2},{2,0},{1,3},{3,1},{4,6},{6,4},{5,7},{7,5},{8,10},{10,8},{9,1... | collective-permute-start | bytes 983048 | tf_op jit(solution)/shard_map/ppermute | solution.py:633
  31.9 6.6 %collective-permute-start.4 = (bf16[160,256]{1,0:T(8,128)(2,1)S(1)}, bf16[160,256]{1,0:T(8,128)(2,1)S(1)}, u32[]{:S(2)}, u32[]{:S(2)}) collective-permute-start(bf16[160,256]{1,0:T(8,128)(2,1)S(1)} %get-tuple-element.222), channel_id=1, source_target_pairs={{0,1},{1,0},{4,5},{5,4},{2,3},{3,2},{6,7},{7,6},{8,9},{9,8},{12,13... | collective-permute-start | bytes 245768 | tf_op jit(solution)/shard_map/ppermute | solution.py:633
  33.1 5.4 %collective-permute-start.5 = (bf16[160,256]{1,0:T(8,128)(2,1)S(1)}, bf16[160,256]{1,0:T(8,128)(2,1)S(1)}, u32[]{:S(2)}, u32[]{:S(2)}) collective-permute-start(bf16[160,256]{1,0:T(8,128)(2,1)S(1)} %get-tuple-element.223), channel_id=1, source_target_pairs={{0,4},{1,5},{4,0},{5,1},{2,6},{3,7},{6,2},{7,3},{8,12},{9,13},{12,... | collective-permute-start | bytes 245768 | tf_op jit(solution)/shard_map/ppermute | solution.py:633
  34.6 5.3 %collective-permute-start.6 = (bf16[160,256]{1,0:T(8,128)(2,1)S(1)}, bf16[160,256]{1,0:T(8,128)(2,1)S(1)}, u32[]{:S(2)}, u32[]{:S(2)}) collective-permute-start(bf16[160,256]{1,0:T(8,128)(2,1)S(1)} %get-tuple-element.224), channel_id=1, source_target_pairs={{0,5},{1,4},{4,1},{5,0},{2,7},{3,6},{6,3},{7,2},{8,13},{9,12},{12,... | collective-permute-start | bytes 245768 | tf_op jit(solution)/shard_map/ppermute | solution.py:633
  40.0 5.4 %collective-permute-start.7 = (bf16[160,256]{1,0:T(8,128)(2,1)S(1)}, bf16[160,256]{1,0:T(8,128)(2,1)S(1)}, u32[]{:S(2)}, u32[]{:S(2)}) collective-permute-start(bf16[160,256]{1,0:T(8,128)(2,1)S(1)} %add_convert_fusion.2), channel_id=1, source_target_pairs={{0,8},{8,0},{16,24},{24,16},{1,9},{9,1},{17,25},{25,17},{2,10},{10... | collective-permute-start | bytes 245768 | tf_op jit(solution)/shard_map/ppermute | solution.py:633
  45.4 2.8 %collective-permute-start.8 = (bf16[448,256]{1,0:T(8,128)(2,1)S(1)}, bf16[448,256]{1,0:T(8,128)(2,1)S(1)}, u32[]{:S(2)}, u32[]{:S(2)}) collective-permute-start(bf16[448,256]{1,0:T(8,128)(2,1)S(1)} %get-tuple-element.243), channel_id=1, source_target_pairs={{0,2},{2,0},{1,3},{3,1},{4,6},{6,4},{5,7},{7,5},{8,10},{10,8},{9,1... | collective-permute-start | bytes 688136 | tf_op jit(solution)/shard_map/ppermute | solution.py:633
  45.6 7.6 %collective-permute-start.12 = (bf16[160,256]{1,0:T(8,128)(2,1)S(1)}, bf16[160,256]{1,0:T(8,128)(2,1)S(1)}, u32[]{:S(2)}, u32[]{:S(2)}) collective-permute-start(bf16[160,256]{1,0:T(8,128)(2,1)S(1)} %add_convert_fusion.1), channel_id=1, source_target_pairs={{0,16},{8,24},{16,0},{24,8},{1,17},{9,25},{17,1},{25,9},{2,18},{10... | collective-permute-start | bytes 245768 | tf_op jit(solution)/shard_map/ppermute | solution.py:633
  48.3 4.8 %collective-permute-start.9 = (bf16[112,256]{1,0:T(8,128)(2,1)S(1)}, bf16[112,256]{1,0:T(8,128)(2,1)S(1)}, u32[]{:S(2)}, u32[]{:S(2)}) collective-permute-start(bf16[112,256]{1,0:T(8,128)(2,1)S(1)} %get-tuple-element.244), channel_id=1, source_target_pairs={{0,1},{1,0},{4,5},{5,4},{2,3},{3,2},{6,7},{7,6},{8,9},{9,8},{12,13... | collective-permute-start | bytes 172040 | tf_op jit(solution)/shard_map/ppermute | solution.py:633
  49.3 4.5 %collective-permute-start.10 = (bf16[112,256]{1,0:T(8,128)(2,1)S(1)}, bf16[112,256]{1,0:T(8,128)(2,1)S(1)}, u32[]{:S(2)}, u32[]{:S(2)}) collective-permute-start(bf16[112,256]{1,0:T(8,128)(2,1)S(1)} %get-tuple-element.245), channel_id=1, source_target_pairs={{0,4},{1,5},{4,0},{5,1},{2,6},{3,7},{6,2},{7,3},{8,12},{9,13},{12,... | collective-permute-start | bytes 172040 | tf_op jit(solution)/shard_map/ppermute | solution.py:633
  50.8 5.1 %collective-permute-start.11 = (bf16[112,256]{1,0:T(8,128)(2,1)S(1)}, bf16[112,256]{1,0:T(8,128)(2,1)S(1)}, u32[]{:S(2)}, u32[]{:S(2)}) collective-permute-start(bf16[112,256]{1,0:T(8,128)(2,1)S(1)} %get-tuple-element.246), channel_id=1, source_target_pairs={{0,5},{1,4},{4,1},{5,0},{2,7},{3,6},{6,3},{7,2},{8,13},{9,12},{12,... | collective-permute-start | bytes 172040 | tf_op jit(solution)/shard_map/ppermute | solution.py:633
  55.9 8.1 %collective-permute-start.16 = (bf16[512,256]{1,0:T(8,128)(2,1)S(1)}, bf16[512,256]{1,0:T(8,128)(2,1)S(1)}, u32[]{:S(2)}, u32[]{:S(2)}) collective-permute-start(bf16[512,256]{1,0:T(8,128)(2,1)S(1)} %get-tuple-element.255), channel_id=1, source_target_pairs={{0,1},{1,0},{2,3},{3,2},{4,5},{5,4},{6,7},{7,6},{8,9},{9,8},{10,11... | collective-permute-start | bytes 786440 | tf_op jit(solution)/shard_map/ppermute | solution.py:625
  56.8 6.0 %collective-permute-start.15 = (bf16[112,256]{1,0:T(8,128)(2,1)S(1)}, bf16[112,256]{1,0:T(8,128)(2,1)S(1)}, u32[]{:S(2)}, u32[]{:S(2)}) collective-permute-start(bf16[112,256]{1,0:T(8,128)(2,1)S(1)} %add_convert_fusion.4), channel_id=1, source_target_pairs={{0,24},{8,16},{16,8},{24,0},{1,25},{9,17},{17,9},{25,1},{2,26},{10... | collective-permute-start | bytes 172040 | tf_op jit(solution)/shard_map/ppermute | solution.py:633
  58.2 5.8 %collective-permute-start.14 = (bf16[112,256]{1,0:T(8,128)(2,1)S(1)}, bf16[112,256]{1,0:T(8,128)(2,1)S(1)}, u32[]{:S(2)}, u32[]{:S(2)}) collective-permute-start(bf16[112,256]{1,0:T(8,128)(2,1)S(1)} %add_convert_fusion.4), channel_id=1, source_target_pairs={{0,16},{8,24},{16,0},{24,8},{1,17},{9,25},{17,1},{25,9},{2,18},{10... | collective-permute-start | bytes 172040 | tf_op jit(solution)/shard_map/ppermute | solution.py:633
  58.8 5.2 %collective-permute-start.13 = (bf16[112,256]{1,0:T(8,128)(2,1)S(1)}, bf16[112,256]{1,0:T(8,128)(2,1)S(1)}, u32[]{:S(2)}, u32[]{:S(2)}) collective-permute-start(bf16[112,256]{1,0:T(8,128)(2,1)S(1)} %add_convert_fusion.4), channel_id=1, source_target_pairs={{0,8},{8,0},{16,24},{24,16},{1,9},{9,1},{17,25},{25,17},{2,10},{10... | collective-permute-start | bytes 172040 | tf_op jit(solution)/shard_map/ppermute | solution.py:633
  64.0 6.0 %collective-permute-start.17 = (bf16[272,256]{1,0:T(8,128)(2,1)S(1)}, bf16[272,256]{1,0:T(8,128)(2,1)S(1)}, u32[]{:S(2)}, u32[]{:S(2)}) collective-permute-start(bf16[272,256]{1,0:T(8,128)(2,1)S(1)} %pad_maximum_fusion.1.refs_0_), channel_id=1, source_target_pairs={{0,1},{1,0},{4,5},{5,4},{2,3},{3,2},{6,7},{7,6},{8,9},{9,8},{12,13... | collective-permute-start | bytes 417800 | tf_op jit(solution)/shard_map/ppermute | solution.py:633
  65.3 6.0 %collective-permute-start.19 = (bf16[272,256]{1,0:T(8,128)(2,1)S(1)}, bf16[272,256]{1,0:T(8,128)(2,1)S(1)}, u32[]{:S(2)}, u32[]{:S(2)}) collective-permute-start(bf16[272,256]{1,0:T(8,128)(2,1)S(1)} %pad_maximum_fusion.1.refs_0_), channel_id=1, source_target_pairs={{0,5},{1,4},{4,1},{5,0},{2,7},{3,6},{6,3},{7,2},{8,13},{9,12},{12,... | collective-permute-start | bytes 417800 | tf_op jit(solution)/shard_map/ppermute | solution.py:633
  66.4 5.7 %collective-permute-start.18 = (bf16[272,256]{1,0:T(8,128)(2,1)S(1)}, bf16[272,256]{1,0:T(8,128)(2,1)S(1)}, u32[]{:S(2)}, u32[]{:S(2)}) collective-permute-start(bf16[272,256]{1,0:T(8,128)(2,1)S(1)} %pad_maximum_fusion.1.refs_0_), channel_id=1, source_target_pairs={{0,4},{1,5},{4,0},{5,1},{2,6},{3,7},{6,2},{7,3},{8,12},{9,13},{12,... | collective-permute-start | bytes 417800 | tf_op jit(solution)/shard_map/ppermute | solution.py:633
  68.6 4.0 %collective-permute-start.20 = (bf16[272,256]{1,0:T(8,128)(2,1)S(1)}, bf16[272,256]{1,0:T(8,128)(2,1)S(1)}, u32[]{:S(2)}, u32[]{:S(2)}) collective-permute-start(bf16[272,256]{1,0:T(8,128)(2,1)S(1)} %pad_maximum_fusion.1.refs_0_), channel_id=1, source_target_pairs={{0,2},{2,0},{1,3},{3,1},{4,6},{6,4},{5,7},{7,5},{8,10},{10,8},{9,1... | collective-permute-start | bytes 417800 | tf_op jit(solution)/shard_map/ppermute | solution.py:633
  71.3 1.4 %collective-permute-start.23 = (bf16[272,256]{1,0:T(8,128)(2,1)S(1)}, bf16[272,256]{1,0:T(8,128)(2,1)S(1)}, u32[]{:S(2)}, u32[]{:S(2)}) collective-permute-start(bf16[272,256]{1,0:T(8,128)(2,1)S(1)} %collective-permute-done.19.refs_3_), channel_id=1, source_target_pairs={{0,2},{2,0},{1,3},{3,1},{4,6},{6,4},{5,7},{7,5},{8,10},{10,8},{9,1... | collective-permute-start | bytes 417800 | tf_op jit(solution)/shard_map/ppermute | solution.py:633
  72.1 1.4 %collective-permute-start.22 = (bf16[272,256]{1,0:T(8,128)(2,1)S(1)}, bf16[272,256]{1,0:T(8,128)(2,1)S(1)}, u32[]{:S(2)}, u32[]{:S(2)}) collective-permute-start(bf16[272,256]{1,0:T(8,128)(2,1)S(1)} %collective-permute-done.18.refs_2_), channel_id=1, source_target_pairs={{0,2},{2,0},{1,3},{3,1},{4,6},{6,4},{5,7},{7,5},{8,10},{10,8},{9,1... | collective-permute-start | bytes 417800 | tf_op jit(solution)/shard_map/ppermute | solution.py:633
  72.1 1.6 %collective-permute-start.21 = (bf16[272,256]{1,0:T(8,128)(2,1)S(1)}, bf16[272,256]{1,0:T(8,128)(2,1)S(1)}, u32[]{:S(2)}, u32[]{:S(2)}) collective-permute-start(bf16[272,256]{1,0:T(8,128)(2,1)S(1)} %collective-permute-done.17.refs_1_), channel_id=1, source_target_pairs={{0,2},{2,0},{1,3},{3,1},{4,6},{6,4},{5,7},{7,5},{8,10},{10,8},{9,1... | collective-permute-start | bytes 417800 | tf_op jit(solution)/shard_map/ppermute | solution.py:633
